TPU v7x, 512 devices: a whole 4x8x8 slice. The times are simulated.
512 devices in a mesh: lon: 32 (over z_hi, y), lat: 16 (over x, z_lo, core).
Axes of the slice: x: 4, y: 8, z: 8 (z_hi: 4, z_lo: 2; z = z_hi * 2 + z_lo), core: 2. Of those that a mesh axis runs over, the one named last changes fastest.
Arguments:
- thermal_anomaly: float32 [1, 1536, 4096], P(None, 'lat', 'lon'), may hold values from -6 to 6
- saltiness_anomaly: float32 [1, 1536, 4096], P(None, 'lat', 'lon'), may hold values from -6 to 6
- zonal_current: float32 [1, 1536, 4096], P(None, 'lat', 'lon'), may hold values from -3 to 3
- meridional_current: float32 [1, 1536, 4096], P(None, 'lat', 'lon'), may hold values from -3 to 3
- wet_indicator: int32 [1, 1536, 4096], P(None, 'lat', 'lon'), may hold values from 0 to 1, as said below
- opposite_meridian: int32 [4096], P('lon'), may hold values from 0 to 4095, as said below
Outputs:
- temperature_new: float32 [1, 1536, 4096], P(None, 'lat', 'lon')
- salinity_new: float32 [1, 1536, 4096], P(None, 'lat', 'lon')
- zonal_new: float32 [1, 1536, 4096], P(None, 'lat', 'lon')
- meridional_new: float32 [1, 1536, 4096], P(None, 'lat', 'lon')
Inputs may be any that keep to these rules, and one draw needn't show every extreme that they name: `wet_indicator`: A cell that is land at one level is land at every deeper level. `opposite_meridian`: column i's partner j satisfies j // 128 == (-(i // 128)) modulo 4096 // 128, and every column is the partner of exactly one column.
All inputs are finite; a program needn't handle non-finite values.
Results may differ from a plain program's by a relative error of at most 0.00002.
Values sent between devices are 32-bit elements; how exact they have to be, the bound alone decides.
No kernel may reach another device: no remote copies, remote signals or barrier semaphores. Data moves between devices by JAX's collectives and lax.ppermute only.
A program may use at most 64 MiB of HBM per device.

v0:
```python
import jax
import jax.numpy as jnp
from jax import lax
from jax.sharding import PartitionSpec as P

STEPS = 4


TIME_STEP = 0.1
DIFFUSE = 0.15
VISCOUS = 0.15
EXPAND = 0.2
CONTRACT = 0.8
ROTATION = 0.5


def with_halo(x, sides, width, wrap):
    for axis, dim in sides:
        size, length = (lax.axis_size(axis), x.shape[dim])
        up = [(i, (i + 1) % size) for i in range(size if wrap else size - 1)]
        down = [(j, i) for i, j in up]
        last = lax.slice_in_dim(x, length - width, length, axis=dim)
        first = lax.slice_in_dim(x, 0, width, axis=dim)
        before = lax.ppermute(last, axis, up)
        after = lax.ppermute(first, axis, down)
        x = jnp.concatenate([before, x, after], axis=dim)
    return x


def interior(array, width):
    return array[..., width : array.shape[-2] - width, width : array.shape[-1] - width]


def laplace(field, mask):
    centre = field[..., 1:-1, 1:-1]
    total = mask[..., 1:-1, 2:] * (field[..., 1:-1, 2:] - centre)
    total = total + mask[..., 1:-1, :-2] * (field[..., 1:-1, :-2] - centre)
    total = total + mask[..., 2:, 1:-1] * (field[..., 2:, 1:-1] - centre)
    total = total + mask[..., :-2, 1:-1] * (field[..., :-2, 1:-1] - centre)
    return mask[..., 1:-1, 1:-1] * total


def biharmonic(field, mask):
    return laplace(laplace(field, mask), mask[..., 1:-1, 1:-1])


def advection(tracer, zonal, merid, mask):
    centre = tracer[..., 1:-1, 1:-1]
    zonal_centre = zonal[..., 1:-1, 1:-1]
    merid_centre = merid[..., 1:-1, 1:-1]
    eastern = (
        mask[..., 1:-1, 2:]
        * (zonal_centre + zonal[..., 1:-1, 2:])
        * (centre + tracer[..., 1:-1, 2:])
    )
    western = (
        mask[..., 1:-1, :-2]
        * (zonal_centre + zonal[..., 1:-1, :-2])
        * (centre + tracer[..., 1:-1, :-2])
    )
    northern = (
        mask[..., 2:, 1:-1]
        * (merid_centre + merid[..., 2:, 1:-1])
        * (centre + tracer[..., 2:, 1:-1])
    )
    southern = (
        mask[..., :-2, 1:-1]
        * (merid_centre + merid[..., :-2, 1:-1])
        * (centre + tracer[..., :-2, 1:-1])
    )
    return 0.25 * mask[..., 1:-1, 1:-1] * (eastern - western + northern - southern)


def gradient(press, mask):
    centre = press[..., 1:-1, 1:-1]
    centre_mask = mask[..., 1:-1, 1:-1]
    grad_x = (
        0.5
        * centre_mask
        * (
            mask[..., 1:-1, 2:] * (press[..., 1:-1, 2:] - centre)
            + mask[..., 1:-1, :-2] * (centre - press[..., 1:-1, :-2])
        )
    )
    grad_y = (
        0.5
        * centre_mask
        * (
            mask[..., 2:, 1:-1] * (press[..., 2:, 1:-1] - centre)
            + mask[..., :-2, 1:-1] * (centre - press[..., :-2, 1:-1])
        )
    )
    return (grad_x, grad_y)


def advance(extended, mask_ext, press, coriolis):
    smooth = biharmonic(extended, mask_ext)
    edge_mask = interior(mask_ext, 1)
    transport = advection(
        interior(extended[0:2], 1), interior(extended[2], 1), interior(extended[3], 1), edge_mask
    )
    grad_x, grad_y = gradient(interior(press, 1), edge_mask)
    sea_inner = interior(mask_ext, 2)
    previous = interior(extended, 2)
    tracers = sea_inner * (previous[0:2] - TIME_STEP * (transport + DIFFUSE * smooth[0:2]))
    zonal = sea_inner * (
        previous[2] + TIME_STEP * (coriolis * previous[3] - grad_x - VISCOUS * smooth[2])
    )
    merid = sea_inner * (
        previous[3] + TIME_STEP * (-coriolis * previous[2] - grad_y - VISCOUS * smooth[3])
    )
    return jnp.concatenate([tracers, zonal[None], merid[None]], axis=0)


def body(
    thermal_anomaly,
    saltiness_anomaly,
    zonal_current,
    meridional_current,
    wet_indicator,
    opposite_meridian,
):
    lat_count = lax.axis_size("lat")
    lat_place = lax.axis_index("lat")
    parallels_each_block = thermal_anomaly.shape[1]
    total_rows = parallels_each_block * lat_count

    def extend(fields, parity):
        upper_rows = jnp.flip(fields[:, :, parallels_each_block - 2 :, :], axis=2)
        gathered = lax.all_gather(upper_rows, "lon", axis=3, tiled=True)
        ghost_rows = jnp.take(gathered, opposite_meridian, axis=3)
        ghost_rows = ghost_rows * parity[:, None, None, None]
        extended = with_halo(fields, (("lat", 2),), 2, False)
        north_rows = jnp.where(
            lat_place == lat_count - 1, ghost_rows, extended[:, :, parallels_each_block + 2 :, :]
        )
        extended = jnp.concatenate(
            [extended[:, :, : parallels_each_block + 2, :], north_rows], axis=2
        )
        return with_halo(extended, (("lon", 3),), 2, True)

    sea = wet_indicator.astype(jnp.float32)
    mask_ext = extend(sea[None], jnp.ones((1,), jnp.float32))[0]
    row_place = (
        lat_place * parallels_each_block + jnp.arange(parallels_each_block, dtype=jnp.int32)
    ).astype(jnp.float32)
    coriolis = (ROTATION * (2.0 * (row_place + 0.5) / total_rows - 1.0))[:, None]
    parity = jnp.array([1.0, 1.0, -1.0, -1.0], jnp.float32)
    prognostic_fields = jnp.stack(
        [thermal_anomaly, saltiness_anomaly, zonal_current, meridional_current]
    )
    for step_index in range(STEPS):
        extended = extend(prognostic_fields, parity)
        density = mask_ext * (CONTRACT * extended[1] - EXPAND * extended[0])
        press = jnp.cumsum(density, axis=0) - 0.5 * density
        prognostic_fields = advance(extended, mask_ext, press, coriolis)
    return (prognostic_fields[0], prognostic_fields[1], prognostic_fields[2], prognostic_fields[3])


def solution(mesh):
    placed = (
        P(None, "lat", "lon"),
        P(None, "lat", "lon"),
        P(None, "lat", "lon"),
        P(None, "lat", "lon"),
        P(None, "lat", "lon"),
        P("lon"),
    )
    return jax.shard_map(
        body,
        mesh=mesh,
        in_specs=placed,
        out_specs=(
            P(None, "lat", "lon"),
            P(None, "lat", "lon"),
            P(None, "lat", "lon"),
            P(None, "lat", "lon"),
        ),
        check_vma=False,
    )
```

profile of v0, /device:TPU:1, one launch (start us, length us, event | category | flops | bytes accessed | tf_op | source)
XLA Modules:
  0.0 1100.7 jit_solution(14877849941164180681)
XLA Ops:
  2.2 8.8 collective-permute-start.1
  19.7 3.2 collective-permute-start.4
  25.2 195.9 %all_gather.16 = f32[4,1,2,4096]{2,3,1,0:T(8,128)} all-gather(f32[4,1,2,128]{2,3,1,0:T(8,128)S(1)} %rev.18), channel_id=1, replica_groups=mesh['lon'=32,'lat'=16] {'lon'}, dimensions={3}, use_global_device_ids=true | all-gather | bytes 135168 | tf_op jit(solution)/shard_map/all_gather | solution.py:130
  221.0 81.0 %all_gather.15 = f32[1,1,2,4096]{2,3,1,0:T(8,128)S(1)} all-gather(f32[1,1,2,128]{2,3,1,0:T(8,128)S(1)} %rev.17), channel_id=1, replica_groups=mesh['lon'=32,'lat'=16] {'lon'}, dimensions={3}, use_global_device_ids=true | all-gather | bytes 33792 | tf_op jit(solution)/shard_map/all_gather | solution.py:130
  302.0 26.8 %copy.65 = f32[4,2,4096]{0,1,2:T(2,128)} copy(f32[4,2,4096]{1,2,0:T(8,128)} %bitcast.236) | data formatting | bytes 262144 | tf_op jit(solution)/shard_map/jit(_take)/Arg_0.11 | solution.py:131
  329.4 2.9 gather_fusion.1
  335.7 7.6 collective-permute-start.7
  345.3 7.6 collective-permute-start.3
  357.1 13.6 %collective-permute-start.8 = (f32[4,1,2,128]{2,3,1,0:T(8,128)S(1)}, f32[4,1,2,128]{2,3,1,0:T(8,128)S(1)}, u32[]{:S(2)}, u32[]{:S(2)}) collective-permute-start(f32[4,1,2,128]{2,3,1,0:T(8,128)S(1)} %get-tuple-element.43), channel_id=1, source_target_pairs={{0,1},{1,2},{2,3},{3,4},{4,5},{5,6},{6,7},{7,8},{8,9},{9,10},{10,1... | collective-permute-start | bytes 12296 | tf_op jit(solution)/shard_map/ppermute | solution.py:24
  370.7 9.3 collective-permute-start.9
  380.0 188.6 %all_gather.17 = f32[4,1,2,4096]{2,3,1,0:T(8,128)} all-gather(f32[4,1,2,128]{2,3,1,0:T(8,128)S(1)} %rev.19), channel_id=1, replica_groups=mesh['lon'=32,'lat'=16] {'lon'}, dimensions={3}, use_global_device_ids=true | all-gather | bytes 135168 | tf_op jit(solution)/shard_map/all_gather | solution.py:130
  568.6 26.8 %copy.71 = f32[4,2,4096]{0,1,2:T(2,128)} copy(f32[4,2,4096]{1,2,0:T(8,128)} %bitcast.237) | data formatting | bytes 262144 | tf_op jit(solution)/shard_map/jit(_take)/Arg_0.11 | solution.py:131
  595.3 2.9 gather_fusion.2
  601.5 7.8 collective-permute-start.11
  614.4 5.4 collective-permute-start.13
  619.8 192.1 %all_gather.18 = f32[4,1,2,4096]{2,3,1,0:T(8,128)} all-gather(f32[4,1,2,128]{2,3,1,0:T(8,128)S(1)} %rev.20), channel_id=1, replica_groups=mesh['lon'=32,'lat'=16] {'lon'}, dimensions={3}, use_global_device_ids=true | all-gather | bytes 135168 | tf_op jit(solution)/shard_map/all_gather | solution.py:130
  811.9 26.8 %copy.73 = f32[4,2,4096]{0,1,2:T(2,128)} copy(f32[4,2,4096]{1,2,0:T(8,128)} %bitcast.238) | data formatting | bytes 262144 | tf_op jit(solution)/shard_map/jit(_take)/Arg_0.11 | solution.py:131
  838.6 2.9 gather_fusion.3
  844.7 7.6 collective-permute-start.15
  855.7 3.4 collective-permute-start.16
  859.2 4.3 collective-permute-start.17
  863.5 191.0 %all_gather.19 = f32[4,1,2,4096]{2,3,1,0:T(8,128)} all-gather(f32[4,1,2,128]{2,3,1,0:T(8,128)S(1)} %rev.21), channel_id=1, replica_groups=mesh['lon'=32,'lat'=16] {'lon'}, dimensions={3}, use_global_device_ids=true | all-gather | bytes 135168 | tf_op jit(solution)/shard_map/all_gather | solution.py:130
  1054.5 26.8 %copy.75 = f32[4,2,4096]{0,1,2:T(2,128)} copy(f32[4,2,4096]{1,2,0:T(8,128)} %bitcast.239) | data formatting | bytes 262144 | tf_op jit(solution)/shard_map/jit(_take)/Arg_0.11 | solution.py:131
  1087.4 7.6 collective-permute-start.19
  (114 shorter events, 48.9 us)
Async XLA Ops:
  2.2 331.2 %collective-permute-start.1 = (f32[1,1,2,128]{2,3,1,0:T(8,128)}, f32[1,1,2,128]{2,3,1,0:T(8,128)S(1)}, u32[]{:S(2)}, u32[]{:S(2)}) collective-permute-start(f32[1,1,2,128]{2,3,1,0:T(8,128)} %get-tuple-element.87), channel_id=1, source_target_pairs={{1,0},{2,1},{3,2},{4,3},{5,4},{6,5},{7,6},{8,7},{9,8},{10,9},{11,1... | collective-permute-start | bytes 3080 | tf_op jit(solution)/shard_map/ppermute | solution.py:25
  11.0 332.3 %collective-permute-start = (f32[1,1,2,128]{2,3,1,0:T(8,128)S(1)}, f32[1,1,2,128]{2,3,1,0:T(8,128)S(1)}, u32[]{:S(2)}, u32[]{:S(2)}) collective-permute-start(f32[1,1,2,128]{2,3,1,0:T(8,128)S(1)} %get-tuple-element.86), channel_id=1, source_target_pairs={{0,1},{1,2},{2,3},{3,4},{4,5},{5,6},{6,7},{7,8},{8,9},{9,10},{10,1... | collective-permute-start | bytes 3080 | tf_op jit(solution)/shard_map/ppermute | solution.py:24
  17.3 316.2 %collective-permute-start.5 = (f32[4,1,2,128]{2,3,1,0:T(8,128)}, f32[4,1,2,128]{2,3,1,0:T(8,128)S(1)}, u32[]{:S(2)}, u32[]{:S(2)}) collective-permute-start(f32[4,1,2,128]{2,3,1,0:T(8,128)} %get-tuple-element.46), channel_id=1, source_target_pairs={{1,0},{2,1},{3,2},{4,3},{5,4},{6,5},{7,6},{8,7},{9,8},{10,9},{11,1... | collective-permute-start | bytes 12296 | tf_op jit(solution)/shard_map/ppermute | solution.py:25
  19.7 314.0 %collective-permute-start.4 = (f32[4,1,2,128]{2,3,1,0:T(8,128)S(1)}, f32[4,1,2,128]{2,3,1,0:T(8,128)S(1)}, u32[]{:S(2)}, u32[]{:S(2)}) collective-permute-start(f32[4,1,2,128]{2,3,1,0:T(8,128)S(1)} %get-tuple-element.45), channel_id=1, source_target_pairs={{0,1},{1,2},{2,3},{3,4},{4,5},{5,6},{6,7},{7,8},{8,9},{9,10},{10,1... | collective-permute-start | bytes 12296 | tf_op jit(solution)/shard_map/ppermute | solution.py:24
  302.0 31.5 %copy-start.2 = (f32[4]{0:T(128)S(1)}, f32[4]{0:T(128)}, u32[]{:S(2)}) copy-start(f32[4]{0:T(128)} %constant.67.clone) | copy-start | bytes 52
  333.8 22.2 %copy-start.1 = (f32[96]{0:T(128)S(1)}, f32[96]{0:T(128)}, u32[]{:S(2)}) copy-start(f32[96]{0:T(128)} %get-tuple-element.89) | copy-start | bytes 1156
  333.8 19.1 %collective-permute-start.6 = (f32[4,1,100,2]{2,3,1,0:T(2,128)S(1)}, f32[4,1,100,2]{2,3,1,0:T(2,128)S(1)}, u32[]{:S(2)}, u32[]{:S(2)}) collective-permute-start(f32[4,1,100,2]{2,3,1,0:T(2,128)S(1)} %get-tuple-element.21), channel_id=1, source_target_pairs={{0,16},{16,32},{32,48},{48,64},{64,80},{80,96},{96,112},{112,128},... | collective-permute-start | bytes 9608 | tf_op jit(solution)/shard_map/ppermute | solution.py:24
  335.7 17.2 %collective-permute-start.7 = (f32[4,1,100,2]{2,3,1,0:T(2,128)S(1)}, f32[4,1,100,2]{2,3,1,0:T(2,128)S(1)}, u32[]{:S(2)}, u32[]{:S(2)}) collective-permute-start(f32[4,1,100,2]{2,3,1,0:T(2,128)S(1)} %get-tuple-element.22), channel_id=1, source_target_pairs={{16,0},{32,16},{48,32},{64,48},{80,64},{96,80},{112,96},{128,112},... | collective-permute-start | bytes 9608 | tf_op jit(solution)/shard_map/ppermute | solution.py:25
  343.3 9.6 copy-start
  343.4 9.8 collective-permute-start.2
  345.3 8.3 collective-permute-start.3
  357.1 242.3 %collective-permute-start.8 = (f32[4,1,2,128]{2,3,1,0:T(8,128)S(1)}, f32[4,1,2,128]{2,3,1,0:T(8,128)S(1)}, u32[]{:S(2)}, u32[]{:S(2)}) collective-permute-start(f32[4,1,2,128]{2,3,1,0:T(8,128)S(1)} %get-tuple-element.43), channel_id=1, source_target_pairs={{0,1},{1,2},{2,3},{3,4},{4,5},{5,6},{6,7},{7,8},{8,9},{9,10},{10,1... | collective-permute-start | bytes 12296 | tf_op jit(solution)/shard_map/ppermute | solution.py:24
  370.7 228.6 %collective-permute-start.9 = (f32[4,1,2,128]{2,3,1,0:T(8,128)S(1)}, f32[4,1,2,128]{2,3,1,0:T(8,128)S(1)}, u32[]{:S(2)}, u32[]{:S(2)}) collective-permute-start(f32[4,1,2,128]{2,3,1,0:T(8,128)S(1)} %get-tuple-element.44), channel_id=1, source_target_pairs={{1,0},{2,1},{3,2},{4,3},{5,4},{6,5},{7,6},{8,7},{9,8},{10,9},{11,1... | collective-permute-start | bytes 12296 | tf_op jit(solution)/shard_map/ppermute | solution.py:25
  568.6 30.8 %copy-start.3 = (f32[4]{0:T(128)S(1)}, f32[4]{0:T(128)}, u32[]{:S(2)}) copy-start(f32[4]{0:T(128)} %constant.67.clone) | copy-start | bytes 52
  599.5 9.7 collective-permute-start.10
  601.5 8.3 collective-permute-start.11
  612.5 230.3 %collective-permute-start.12 = (f32[4,1,2,128]{2,3,1,0:T(8,128)S(1)}, f32[4,1,2,128]{2,3,1,0:T(8,128)S(1)}, u32[]{:S(2)}, u32[]{:S(2)}) collective-permute-start(f32[4,1,2,128]{2,3,1,0:T(8,128)S(1)} %get-tuple-element.41), channel_id=1, source_target_pairs={{0,1},{1,2},{2,3},{3,4},{4,5},{5,6},{6,7},{7,8},{8,9},{9,10},{10,1... | collective-permute-start | bytes 12296 | tf_op jit(solution)/shard_map/ppermute | solution.py:24
  614.4 228.2 %collective-permute-start.13 = (f32[4,1,2,128]{2,3,1,0:T(8,128)S(1)}, f32[4,1,2,128]{2,3,1,0:T(8,128)S(1)}, u32[]{:S(2)}, u32[]{:S(2)}) collective-permute-start(f32[4,1,2,128]{2,3,1,0:T(8,128)S(1)} %get-tuple-element.42), channel_id=1, source_target_pairs={{1,0},{2,1},{3,2},{4,3},{5,4},{6,5},{7,6},{8,7},{9,8},{10,9},{11,1... | collective-permute-start | bytes 12296 | tf_op jit(solution)/shard_map/ppermute | solution.py:25
  842.8 9.5 collective-permute-start.14
  844.7 8.3 collective-permute-start.15
  855.7 229.6 %collective-permute-start.16 = (f32[4,1,2,128]{2,3,1,0:T(8,128)S(1)}, f32[4,1,2,128]{2,3,1,0:T(8,128)S(1)}, u32[]{:S(2)}, u32[]{:S(2)}) collective-permute-start(f32[4,1,2,128]{2,3,1,0:T(8,128)S(1)} %get-tuple-element.39), channel_id=1, source_target_pairs={{0,1},{1,2},{2,3},{3,4},{4,5},{5,6},{6,7},{7,8},{8,9},{9,10},{10,1... | collective-permute-start | bytes 12296 | tf_op jit(solution)/shard_map/ppermute | solution.py:24
  859.2 226.1 %collective-permute-start.17 = (f32[4,1,2,128]{2,3,1,0:T(8,128)S(1)}, f32[4,1,2,128]{2,3,1,0:T(8,128)S(1)}, u32[]{:S(2)}, u32[]{:S(2)}) collective-permute-start(f32[4,1,2,128]{2,3,1,0:T(8,128)S(1)} %get-tuple-element.40), channel_id=1, source_target_pairs={{1,0},{2,1},{3,2},{4,3},{5,4},{6,5},{7,6},{8,7},{9,8},{10,9},{11,1... | collective-permute-start | bytes 12296 | tf_op jit(solution)/shard_map/ppermute | solution.py:25
  1085.5 9.5 collective-permute-start.18
  1087.4 8.3 collective-permute-start.19
where the time goes:
time: 1100 us
  blocking collectives  849 us (77%)
  local copies, waits for them, and re-layouts  134 us (12%)
  starting transfers between devices  102 us (9%)
  other arithmetic  12.2 us (1%)
    all_gather x5, blocking collectives, extend(): gathered = lax.all_gather(upper_rows, 'lon', axis=3, tiled=True)  849 us
    another operation x4, local copies, waits for them, and re-layouts, extend(): ghost_rows = jnp.take(gathered, opposite_meridian, axis=3)  107 us
    ppermute x10, starting transfers between devices, with_halo(): after = lax.ppermute(first, axis, down)  68.2 us
    ppermute x10, starting transfers between devices, with_halo(): before = lax.ppermute(last, axis, up)  33.6 us
  transfers between devices with their start and end apart: 20, of which 4 were waited for; matrix products, arithmetic and copies ran while one was open for 12% of the time, Pallas kernels for 0%

commit v1 on v0

v1 whole, which is shorter than its diff:
```python
import functools

import jax
import jax.numpy as jnp
from jax import lax
from jax.experimental import pallas as pl
from jax.experimental.pallas import tpu as pltpu
from jax.sharding import PartitionSpec as P

STEPS = 4
TIME_STEP = 0.1
DIFFUSE = 0.15
EXPAND = 0.2
CONTRACT = 0.8
ROTATION = 0.5

HALO = 2 * STEPS
LANES = 128
FIELDS = 4
REACH = 4
ARC = 2 * REACH + 1
CAP = 48
PARITY = (1.0, 1.0, -1.0, -1.0)


def lane_index(rows=8):
    return lax.broadcasted_iota(jnp.int32, (rows, LANES), 1)


def roll(x, shift):
    shift = shift % LANES
    return x if shift == 0 else pltpu.roll(x, shift, 1)


def rows_kernel(t_ref, s_ref, u_ref, v_ref, m_ref, opp_ref, a_ref, b_ref):
    odd = lax.rem(lax.axis_index("lat"), 2) == 1
    height = t_ref.shape[1]
    for i, ref in enumerate((t_ref, s_ref, u_ref, v_ref, m_ref)):
        south = ref[0, 0:HALO, :].astype(jnp.float32)
        north = ref[0, height - HALO : height, :].astype(jnp.float32)
        a_ref[i * 8 : i * 8 + 8, :] = jnp.where(odd, south, north)
        b_ref[i * 8 : i * 8 + 8, :] = jnp.where(odd, north, south)
    b_ref[40:48, :] = jnp.broadcast_to(opp_ref[...].astype(jnp.float32), (8, LANES))


def halo_tiles(refs, ra_ref, rb_ref, odd, i):
    ra, rb = ra_ref[i * 8 : i * 8 + 8, :], rb_ref[i * 8 : i * 8 + 8, :]
    ref = refs[i]
    own = [
        ref[0, 8 * g : 8 * g + 8, :].astype(jnp.float32) for g in range(ref.shape[1] // 8)
    ]
    return [jnp.where(odd, ra, rb)] + own + [jnp.where(odd, rb, ra)]


def columns_kernel(t_ref, s_ref, u_ref, v_ref, m_ref, sb_ref, ra_ref, rb_ref, e_ref, w_ref):
    odd = lax.rem(lax.axis_index("lat"), 2) == 1
    lane = lane_index()
    refs = (t_ref, s_ref, u_ref, v_ref, m_ref)
    for i in range(5):
        tiles = halo_tiles(refs, ra_ref, rb_ref, odd, i)
        east = jnp.zeros((8, LANES), jnp.float32)
        west = jnp.zeros((8, LANES), jnp.float32)
        for g, tile in enumerate(tiles):
            here = (lane >= 8 * g) & (lane < 8 * g + 8)
            east = jnp.where(here, roll(tile, 8 * g - (LANES - HALO)), east)
            west = jnp.where(here, roll(tile, 8 * g), west)
        e_ref[i * 8 : i * 8 + 8, :] = east
        w_ref[i * 8 : i * 8 + 8, :] = west
    for ref in (e_ref, w_ref):
        ref[40 : 40 + CAP, :] = sb_ref[...]
        ref[40 + CAP : 40 + 2 * CAP, :] = rb_ref[...]


def first_pass(centre, north, south, east, west, sea, count, w_e, w_n, w_s, turn, roll_w):
    laps = [
        sea * (((east[i] + west[i]) + (north[i] + south[i])) - count * centre[i])
        for i in range(FIELDS)
    ]
    t, s, u, v = centre
    flow_e = w_e * (u + east[2])
    flow_n = w_n * (v + north[3])
    flow_s = w_s * (v + south[3])
    partial = []
    for i in (0, 1):
        c = centre[i]
        x = flow_e * (c + east[i])
        y = flow_n * (c + north[i]) - flow_s * (c + south[i])
        partial.append(c - (0.25 * TIME_STEP) * ((x - roll_w(x)) + y))
    ratio = EXPAND / CONTRACT
    slope = 0.25 * TIME_STEP * CONTRACT
    q = s - ratio * t
    q_e = east[1] - ratio * east[0]
    q_n = north[1] - ratio * north[0]
    q_s = south[1] - ratio * south[0]
    d = w_e * (q_e - q)
    partial.append(u + (turn * v - slope * (d + roll_w(d))))
    partial.append(v - (turn * u + slope * (w_n * (q_n - q) + w_s * (q - q_s))))
    return laps, partial


def second_pass(partial, lap, north, south, east, west, sea, count):
    mix = ((east + west) + (north + south)) - count * lap
    return sea * (partial - (TIME_STEP * DIFFUSE) * mix)


def steps_kernel(
    lat_count,
    t_ref,
    s_ref,
    u_ref,
    v_ref,
    m_ref,
    sb_ref,
    ra_ref,
    rb_ref,
    rw_ref,
    re_ref,
    w3_ref,
    e3_ref,
    t_out,
    s_out,
    u_out,
    v_out,
    state,
    laps,
    part,
    stat,
    turn_ref,
    cap,
    cap_lap,
    cap_part,
    cap_stat,
    cap_opp,
):
    lat = lax.axis_index("lat")
    odd = lax.rem(lat, 2) == 1
    top = lat == lat_count - 1
    lane = lane_index()
    height = t_ref.shape[1]
    total_rows = height * lat_count
    tiles_n = height // 8 + 2
    band = 8 * tiles_n
    refs = (t_ref, s_ref, u_ref, v_ref, m_ref)
    tile_rows = [8 + 8 * g for g in range(2 * tiles_n)]

    for i in range(5):
        tiles = halo_tiles(refs, ra_ref, rb_ref, odd, i)
        from_w, from_e = rw_ref[i * 8 : i * 8 + 8, :], re_ref[i * 8 : i * 8 + 8, :]
        for g, tile in enumerate(tiles):
            west = jnp.where(lane < HALO, roll(from_w, -8 * g), roll(tile, HALO))
            east = jnp.where(
                lane >= LANES - HALO, roll(from_e, LANES - HALO - 8 * g), roll(tile, -HALO)
            )
            if i < FIELDS:
                state[i, 8 + 8 * g : 16 + 8 * g, :] = west
                state[i, 8 + band + 8 * g : 16 + band + 8 * g, :] = east
            else:
                stat[0, 8 + 8 * g : 16 + 8 * g, :] = west
                stat[0, 8 + band + 8 * g : 16 + band + 8 * g, :] = east
    nothing = jnp.zeros((8, LANES), jnp.float32)
    for row in (0, 8 + 2 * band):
        for i in range(FIELDS):
            state[i, row : row + 8, :] = nothing
            laps[i, row : row + 8, :] = nothing
        for i in range(4):
            stat[i, row : row + 8, :] = nothing

    def ghosts_to_main(source, target):
        for side_row, low, high, shift in ((8, 3, 4, HALO), (8 + band, 4, 5, -HALO)):
            row = side_row + band - HALO
            a, b = source(low), source(high)
            if shift > 0:
                value = jnp.where(lane[0:2] < HALO, roll(a, shift), roll(b, shift))
            else:
                value = jnp.where(lane[0:2] >= LANES - HALO, roll(b, shift), roll(a, shift))
            target(row, value)

    def fill_ghosts(ref, i, parity):
        for side in (0, 1):
            for k in range(ARC):
                index = cap_opp[side, k]
                rows = ref[1 - side, i, ARC - 1 - k, 0:8, :]
                ghost = jnp.take_along_axis(rows, index, axis=1, mode="promise_in_bounds")
                ref[side, i, k, 8:9, :] = parity * ghost[7:8, :]
                ref[side, i, k, 9:10, :] = parity * ghost[6:7, :]

    def main_ghosts():
        for i in range(FIELDS):

            def put(row, value, i=i):
                state[i, row : row + 2, :] = value

            ghosts_to_main(lambda k, i=i: cap[0, i, k, 8:10, :], put)

    def cap_rolls(rows_of, side):
        blocks = [rows_of(side, k) for k in range(ARC)]
        return blocks, *arc_neighbours(blocks)

    def arc_neighbours(blocks):
        e, w = [roll(x, -1) for x in blocks], [roll(x, 1) for x in blocks]
        east = [
            jnp.where(lane == LANES - 1, e[min(k + 1, ARC - 1)], e[k]) for k in range(ARC)
        ]
        west = [jnp.where(lane == 0, w[max(k - 1, 0)], w[k]) for k in range(ARC)]
        return east, west

    @pl.when(top)
    def _():
        pieces = []
        for n in range(3):
            pieces.append((n - REACH, w3_ref, n * 2 * CAP))
        pieces.append((-1, rw_ref, 40))
        pieces.append((1, re_ref, 40))
        for n in range(3):
            pieces.append((n + 2, e3_ref, n * 2 * CAP))
        blocks = [(o + REACH, ref, base, ref, base + CAP) for o, ref, base in pieces]
        blocks.append((REACH, sb_ref, 0, rb_ref, 0))
        for k, own, own_base, facing, facing_base in blocks:
            for side, place, ref, base in (
                (0, k, own, own_base),
                (1, ARC - 1 - k, facing, facing_base),
            ):
                sea = ref[base + 32 : base + 40, :]
                cap_stat[side, 0, place, 0:8, :] = sea
                cap_stat[side, 0, place, 10:16, :] = nothing[0:6]
                for i in range(FIELDS):
                    cap[side, i, place, 0:8, :] = sea * ref[base + 8 * i : base + 8 * i + 8, :]
                    cap[side, i, place, 10:16, :] = nothing[0:6]
                    cap_lap[side, i, place, 0:8, :] = nothing
                    cap_lap[side, i, place, 8:16, :] = nothing
                opp = ref[base + 40 : base + 48, :].astype(jnp.int32)
                cap_opp[side, place] = lax.rem(opp, LANES)
        fill_ghosts(cap_stat, 0, 1.0)
        for i in range(FIELDS):
            fill_ghosts(cap, i, PARITY[i])
        for side in (0, 1):
            for start in (0, 1):
                seas = [cap_stat[side, 0, k, start : start + 8, :] for k in range(ARC)]
                east, west = arc_neighbours(seas)
                for k in range(ARC):
                    north = cap_stat[side, 0, k, start + 1 : start + 9, :]
                    if start:
                        south = cap_stat[side, 0, k, start - 1 : start + 7, :]
                        cap_stat[side, 1, k, start : start + 8, :] = (
                            (east[k] + west[k]) + (north + south)
                        )
                    cap_stat[side, 2, k, start : start + 8, :] = seas[k] * east[k]
                    cap_stat[side, 3, k, start : start + 8, :] = seas[k] * north

        def put(row, value):
            stat[0, row : row + 2, :] = value

        ghosts_to_main(lambda k: cap_stat[0, 0, k, 8:10, :], put)
        main_ghosts()

    base_row = (lat * height - HALO).astype(jnp.float32)
    sub = lax.broadcasted_iota(jnp.int32, (8, LANES), 0).astype(jnp.float32)

    def turning(row):
        return (TIME_STEP * ROTATION) * (2.0 * (row + 0.5) / total_rows - 1.0)

    for n, r in enumerate(tile_rows):
        sea = stat[0, r : r + 8, :]
        north = stat[0, r + 1 : r + 9, :]
        south = stat[0, r - 1 : r + 7, :]
        east, west = roll(sea, -1), roll(sea, 1)
        stat[1, r : r + 8, :] = (east + west) + (north + south)
        stat[2, r : r + 8, :] = sea * east
        stat[3, r : r + 8, :] = sea * north
        for i in range(FIELDS):
            state[i, r : r + 8, :] = sea * state[i, r : r + 8, :]
        if n < tiles_n:
            turn_ref[r : r + 8, :] = turning(base_row + float(8 * n) + sub)

    def main_first(r):
        centre = [state[i, r : r + 8, :] for i in range(FIELDS)]
        north = [state[i, r + 1 : r + 9, :] for i in range(FIELDS)]
        south = [state[i, r - 1 : r + 7, :] for i in range(FIELDS)]
        east = [roll(x, -1) for x in centre]
        west = [roll(x, 1) for x in centre]
        turn_row = r if r < 8 + band else r - band
        lap, partial = first_pass(
            centre,
            north,
            south,
            east,
            west,
            stat[0, r : r + 8, :],
            stat[1, r : r + 8, :],
            stat[2, r : r + 8, :],
            stat[3, r : r + 8, :],
            stat[3, r - 1 : r + 7, :],
            turn_ref[turn_row : turn_row + 8, :],
            lambda x: roll(x, 1),
        )
        for i in range(FIELDS):
            laps[i, r : r + 8, :] = lap[i]
            part[i, r : r + 8, :] = partial[i]

    def main_second(r):
        sea, count = stat[0, r : r + 8, :], stat[1, r : r + 8, :]
        for i in range(FIELDS):
            lap = laps[i, r : r + 8, :]
            state[i, r : r + 8, :] = second_pass(
                part[i, r : r + 8, :],
                lap,
                laps[i, r + 1 : r + 9, :],
                laps[i, r - 1 : r + 7, :],
                roll(lap, -1),
                roll(lap, 1),
                sea,
                count,
            )

    cap_turn = turning(float(total_rows - HALO + 1) + sub)

    def cap_first():
        for side in (0, 1):
            fields = [
                cap_rolls(lambda sd, k, i=i: cap[sd, i, k, 1:9, :], side) for i in range(FIELDS)
            ]
            for k in range(ARC):
                centre = [fields[i][0][k] for i in range(FIELDS)]
                east = [fields[i][1][k] for i in range(FIELDS)]
                west = [fields[i][2][k] for i in range(FIELDS)]
                north = [cap[side, i, k, 2:10, :] for i in range(FIELDS)]
                south = [cap[side, i, k, 0:8, :] for i in range(FIELDS)]
                before = max(k - 1, 0)
                w_e = cap_stat[side, 2, k, 1:9, :]
                w_e_before = cap_stat[side, 2, before, 1:9, :]

                def roll_w(x, kind=iter(range(3))):
                    which = next(kind)
                    b = [fields[i][0][before] for i in range(FIELDS)]
                    be = [fields[i][1][before] for i in range(FIELDS)]
                    if which < 2:
                        other = w_e_before * (b[2] + be[2]) * (b[which] + be[which])
                    else:
                        ratio = EXPAND / CONTRACT
                        other = w_e_before * ((be[1] - ratio * be[0]) - (b[1] - ratio * b[0]))
                    return roll(jnp.where(lane == LANES - 1, other, x), 1)

                lap, partial = first_pass(
                    centre,
                    north,
                    south,
                    east,
                    west,
                    cap_stat[side, 0, k, 1:9, :],
                    cap_stat[side, 1, k, 1:9, :],
                    w_e,
                    cap_stat[side, 3, k, 1:9, :],
                    cap_stat[side, 3, k, 0:8, :],
                    cap_turn,
                    roll_w,
                )
                for i in range(FIELDS):
                    cap_lap[side, i, k, 1:9, :] = lap[i]
                    cap_part[side, i, k, 0:8, :] = partial[i]

    def cap_second():
        for side in (0, 1):
            for i in range(FIELDS):
                blocks, east, west = cap_rolls(
                    lambda sd, k, i=i: cap_lap[sd, i, k, 1:9, :], side
                )
                for k in range(ARC):
                    cap[side, i, k, 1:9, :] = second_pass(
                        cap_part[side, i, k, 0:8, :],
                        blocks[k],
                        cap_lap[side, i, k, 2:10, :],
                        cap_lap[side, i, k, 0:8, :],
                        east[k],
                        west[k],
                        cap_stat[side, 0, k, 1:9, :],
                        cap_stat[side, 1, k, 1:9, :],
                    )

    def step(n, carry):
        for r in tile_rows:
            main_first(r)
        for r in tile_rows:
            main_second(r)

        @pl.when(top & (n < STEPS - 1))
        def _():
            cap_first()
            cap_second()
            for i in range(FIELDS):
                fill_ghosts(cap, i, PARITY[i])
            main_ghosts()

        return carry

    lax.fori_loop(0, STEPS, step, 0)

    for i, out in enumerate((t_out, s_out, u_out, v_out)):
        for g in range(height // 8):
            r = 8 + HALO + 8 * g
            west, east = state[i, r : r + 8, :], state[i, r + band : r + band + 8, :]
            out[0, 8 * g : 8 * g + 8, :] = jnp.where(
                lane < LANES // 2, roll(west, -HALO), roll(east, HALO)
            )


def body(lon_count, lat_count, t, s, u, v, m, opp):
    fields = (t, s, u, v, m)
    height = t.shape[1]
    whole = pl.BlockSpec(memory_space=pltpu.VMEM)
    f32 = jnp.float32
    limit = pltpu.CompilerParams(vmem_limit_bytes=32 * 1024 * 1024)

    def call(kernel, inputs, shapes, scratch=()):
        return pl.pallas_call(
            kernel,
            out_shape=[jax.ShapeDtypeStruct(shape, f32) for shape in shapes],
            in_specs=[whole] * len(inputs),
            out_specs=[whole] * len(shapes),
            scratch_shapes=list(scratch),
            compiler_params=limit,
        )(*inputs)

    def place(lon, lat):
        return (lon % lon_count) * lat_count + lat

    lons, lats = range(lon_count), range(lat_count)
    last = lat_count - 1
    pairs_a = [(place(i, j), place(i, j ^ 1)) for i in lons for j in lats]
    pairs_b = [(place(i, j), place(i, ((j - 1) ^ 1) + 1)) for i in lons for j in lats[1:last]]
    pairs_b += [(place(i, last), place(-i, last)) for i in lons]

    def shift(x, by, rows):
        pairs = [(place(i, j), place(i + by, j)) for i in lons for j in rows]
        return lax.ppermute(x, ("lon", "lat"), pairs)

    send_a, send_b = call(rows_kernel, (*fields, opp.reshape(1, LANES)), [(CAP, LANES)] * 2)
    from_a = lax.ppermute(send_a, ("lon", "lat"), pairs_a)
    from_b = lax.ppermute(send_b, ("lon", "lat"), pairs_b)
    wide = 40 + 2 * CAP
    send_e, send_w = call(
        columns_kernel, (*fields, send_b, from_a, from_b), [(wide, LANES)] * 2
    )
    from_w = shift(send_e, 1, lats)
    from_e = shift(send_w, -1, lats)
    three = jnp.concatenate([from_w[40:], send_e[40:], from_e[40:]], axis=0)
    far_w = shift(three, 3, [last])
    far_e = shift(three, -3, [last])
    rows = 16 + 2 * (height + 2 * HALO)
    return tuple(
        call(
            functools.partial(steps_kernel, lat_count),
            (*fields, send_b, from_a, from_b, from_w, from_e, far_w, far_e),
            [t.shape] * 4,
            [
                pltpu.VMEM((FIELDS, rows, LANES), f32),
                pltpu.VMEM((FIELDS, rows, LANES), f32),
                pltpu.VMEM((FIELDS, rows, LANES), f32),
                pltpu.VMEM((4, rows, LANES), f32),
                pltpu.VMEM((8 + height + 2 * HALO, LANES), f32),
                pltpu.VMEM((2, FIELDS, ARC, 16, LANES), f32),
                pltpu.VMEM((2, FIELDS, ARC, 16, LANES), f32),
                pltpu.VMEM((2, FIELDS, ARC, 8, LANES), f32),
                pltpu.VMEM((2, 4, ARC, 16, LANES), f32),
                pltpu.VMEM((2, ARC, 8, LANES), jnp.int32),
            ],
        )
    )


def solution(mesh):
    placed = P(None, "lat", "lon")
    return jax.shard_map(
        functools.partial(body, mesh.shape["lon"], mesh.shape["lat"]),
        mesh=mesh,
        in_specs=(placed,) * 5 + (P("lon"),),
        out_specs=(placed,) * 4,
        check_vma=False,
    )
```

time: 1100 us -> 68.9 us (0.06)
  the two profiles are of different devices: /device:TPU:1 before, /device:TPU:87 now
where the time goes in v1:
time: 68.9 us; the launch traced here: 68.3 us
  starting transfers between devices  34.7 us (50%)
  waiting for transfers between devices  14.2 us (21%)
  Pallas kernels  12.6 us (18%)
  local copies, waits for them, and re-layouts  6.07 us (9%)
  between operations  0.74 us (1%)
    ppermute x4, starting transfers between devices, shift(): return lax.ppermute(x, ('lon', 'lat'), pairs)  18.9 us
    ppermute x1, starting transfers between devices, body(): from_b = lax.ppermute(send_b, ('lon', 'lat'), pairs_b)  13.2 us
    ppermute x4, waiting for transfers between devices, shift(): return lax.ppermute(x, ('lon', 'lat'), pairs)  13 us
    pallas_call x3, Pallas kernels, call(): pl.pallas_call(kernel, out_shape=[jax.ShapeDtypeStruct(shape, f32) for sh...  12.6 us
    unnamed x16, local copies, waits for them, and re-layouts  5.26 us
    ppermute x1, starting transfers between devices, body(): from_a = lax.ppermute(send_a, ('lon', 'lat'), pairs_a)  2.58 us
  transfers between devices with their start and end apart: 6, of which 4 were waited for; matrix products, arithmetic and copies ran while one was open for 0% of the time, Pallas kernels for 0%

profile of v1, /device:TPU:87, one launch (start us, length us, event | category | flops | bytes accessed | tf_op | source)
XLA Modules:
  0.0 68.3 jit_solution(9130651905187459114)
XLA Ops:
  0.6 0.0 copy-start.7
  0.6 0.6 copy-done.7
  1.3 0.8 %copy-done = f32[1,96,128]{2,1,0:T(8,128)S(1)} copy-done((f32[1,96,128]{2,1,0:T(8,128)S(1)}, f32[1,96,128]{2,1,0:T(8,128)}, u32[]{:S(2)}) %copy-start) | copy-done | bytes 49176
  2.1 0.8 %copy-done.1 = f32[1,96,128]{2,1,0:T(8,128)S(1)} copy-done((f32[1,96,128]{2,1,0:T(8,128)S(1)}, f32[1,96,128]{2,1,0:T(8,128)}, u32[]{:S(2)}) %copy-start.1) | copy-done | bytes 49176
  2.9 0.8 %copy-done.2 = f32[1,96,128]{2,1,0:T(8,128)S(1)} copy-done((f32[1,96,128]{2,1,0:T(8,128)S(1)}, f32[1,96,128]{2,1,0:T(8,128)}, u32[]{:S(2)}) %copy-start.2) | copy-done | bytes 49176
  3.7 0.8 %copy-done.3 = f32[1,96,128]{2,1,0:T(8,128)S(1)} copy-done((f32[1,96,128]{2,1,0:T(8,128)S(1)}, f32[1,96,128]{2,1,0:T(8,128)}, u32[]{:S(2)}) %copy-start.3) | copy-done | bytes 49176
  4.5 0.8 %copy-done.4 = s32[1,96,128]{2,1,0:T(8,128)S(1)} copy-done((s32[1,96,128]{2,1,0:T(8,128)S(1)}, s32[1,96,128]{2,1,0:T(8,128)}, u32[]{:S(2)}) %copy-start.4) | copy-done | bytes 49176
  5.3 2.6 %collective-permute-start = (f32[48,128]{1,0:T(8,128)S(1)}, f32[48,128]{1,0:T(8,128)S(1)}, u32[]{:S(2)}, u32[]{:S(2)}) collective-permute-start(f32[48,128]{1,0:T(8,128)S(1)} %get-tuple-element.9), channel_id=1, source_target_pairs={{0,1},{1,0},{2,3},{3,2},{4,5},{5,4},{6,7},{7,6},{8,9},{9,8},{10,11... | collective-permute-start | bytes 73736 | tf_op jit(solution)/shard_map/ppermute | solution.py:437
  7.9 13.2 %collective-permute-start.1 = (f32[48,128]{1,0:T(8,128)S(1)}, f32[48,128]{1,0:T(8,128)S(1)}, u32[]{:S(2)}, u32[]{:S(2)}) collective-permute-start(f32[48,128]{1,0:T(8,128)S(1)} %get-tuple-element.8.sb_ref), channel_id=1, source_target_pairs={{1,2},{2,1},{3,4},{4,3},{5,6},{6,5},{7,8},{8,7},{9,10},{10,9},{11,... | collective-permute-start | bytes 73736 | tf_op jit(solution)/shard_map/ppermute | solution.py:438
  21.1 0.0 collective-permute-done.ra_ref
  21.1 1.2 %collective-permute-done.1.rb_ref = f32[48,128]{1,0:T(8,128)S(1)} collective-permute-done((f32[48,128]{1,0:T(8,128)S(1)}, f32[48,128]{1,0:T(8,128)S(1)}, u32[]{:S(2)}, u32[]{:S(2)}) %collective-permute-start.1) | collective-permute-done | bytes 24608 | tf_op jit(solution)/shard_map/ppermute | solution.py:438
  22.3 0.2 shard_map.94
  22.5 1.9 %collective-permute-start.3 = (f32[136,128]{1,0:T(8,128)S(1)}, f32[136,128]{1,0:T(8,128)S(1)}, u32[]{:S(2)}, u32[]{:S(2)}) collective-permute-start(f32[136,128]{1,0:T(8,128)S(1)} %get-tuple-element.11), channel_id=1, source_target_pairs={{0,496},{1,497},{2,498},{3,499},{4,500},{5,501},{6,502},{7,503},{8... | collective-permute-start | bytes 208904 | tf_op jit(solution)/shard_map/ppermute | solution.py:434
  24.5 3.4 %collective-permute-start.2 = (f32[136,128]{1,0:T(8,128)S(1)}, f32[136,128]{1,0:T(8,128)S(1)}, u32[]{:S(2)}, u32[]{:S(2)}) collective-permute-start(f32[136,128]{1,0:T(8,128)S(1)} %get-tuple-element.10), channel_id=1, source_target_pairs={{0,16},{1,17},{2,18},{3,19},{4,20},{5,21},{6,22},{7,23},{8,24},{9,... | collective-permute-start | bytes 208904 | tf_op jit(solution)/shard_map/ppermute | solution.py:434
  27.8 0.0 collective-permute-done.3.re_ref
  27.8 0.0 copy-start.5
  27.9 0.6 copy-done.5
  28.5 1.0 %collective-permute-done.2.rw_ref = f32[136,128]{1,0:T(8,128)S(1)} collective-permute-done((f32[136,128]{1,0:T(8,128)S(1)}, f32[136,128]{1,0:T(8,128)S(1)}, u32[]{:S(2)}, u32[]{:S(2)}) %collective-permute-start.2) | collective-permute-done | bytes 69664 | tf_op jit(solution)/shard_map/ppermute | solution.py:434
  29.5 0.8 %slice-done = f32[96,128]{1,0:T(8,128)S(1)} async-done(((f32[136,128]{1,0:T(8,128)}), f32[96,128]{1,0:T(8,128)S(1)}, s32[]{:S(2)}) %slice-start) | async-done | bytes 49176 | tf_op jit(solution)/shard_map/slice | solution.py:445
  30.3 11.7 %collective-permute-start.5 = (f32[288,128]{1,0:T(8,128)S(1)}, f32[288,128]{1,0:T(8,128)S(1)}, u32[]{:S(2)}, u32[]{:S(2)}) collective-permute-start(f32[288,128]{1,0:T(8,128)S(1)} %pad_maximum_fusion), channel_id=1, source_target_pairs={{15,479},{31,495},{47,511},{63,15},{79,31},{95,47},{111,63},{127,7... | collective-permute-start | bytes 442376 | tf_op jit(solution)/shard_map/ppermute | solution.py:434
  42.0 1.9 %collective-permute-start.4 = (f32[288,128]{1,0:T(8,128)S(1)}, f32[288,128]{1,0:T(8,128)S(1)}, u32[]{:S(2)}, u32[]{:S(2)}) collective-permute-start(f32[288,128]{1,0:T(8,128)S(1)} %pad_maximum_fusion), channel_id=1, source_target_pairs={{15,63},{31,79},{47,95},{63,111},{79,127},{95,143},{111,159},{127,... | collective-permute-start | bytes 442376 | tf_op jit(solution)/shard_map/ppermute | solution.py:434
  44.0 2.3 %collective-permute-done.5.e3_ref = f32[288,128]{1,0:T(8,128)S(1)} collective-permute-done((f32[288,128]{1,0:T(8,128)S(1)}, f32[288,128]{1,0:T(8,128)S(1)}, u32[]{:S(2)}, u32[]{:S(2)}) %collective-permute-start.5) | collective-permute-done | bytes 147488 | tf_op jit(solution)/shard_map/ppermute | solution.py:434
  46.2 9.7 %collective-permute-done.4.w3_ref = f32[288,128]{1,0:T(8,128)S(1)} collective-permute-done((f32[288,128]{1,0:T(8,128)S(1)}, f32[288,128]{1,0:T(8,128)S(1)}, u32[]{:S(2)}, u32[]{:S(2)}) %collective-permute-start.4) | collective-permute-done | bytes 147488 | tf_op jit(solution)/shard_map/ppermute | solution.py:434
  55.9 12.4 %shard_map.95 = (f32[1,96,128]{2,1,0:T(8,128)}, f32[1,96,128]{2,1,0:T(8,128)}, f32[1,96,128]{2,1,0:T(8,128)}, f32[1,96,128]{2,1,0:T(8,128)}) custom-call(f32[1,96,128]{2,1,0:T(8,128)S(1)} %copy-done, f32[1,96,128]{2,1,0:T(8,128)S(1)} %copy-done.1, f32[1,96,128]{2,1,0:T(8,128)S(1)} %copy-done.2, f32[1,96,128]{2,1,0:T(8,128)S(1)} %copy-done.3, ...), custom_call_target="tpu_custom_call" | custom-call | tf_op jit(solution)/shard_map/pallas_call | solution.py:414
  (12 shorter events, 0.0 us)
Async XLA Ops:
  0.6 0.7 copy-start.7
  1.3 0.8 %copy-start = (f32[1,96,128]{2,1,0:T(8,128)S(1)}, f32[1,96,128]{2,1,0:T(8,128)}, u32[]{:S(2)}) copy-start(f32[1,96,128]{2,1,0:T(8,128)} %t_ref.5) | copy-start | bytes 147460
  2.1 0.8 %copy-start.1 = (f32[1,96,128]{2,1,0:T(8,128)S(1)}, f32[1,96,128]{2,1,0:T(8,128)}, u32[]{:S(2)}) copy-start(f32[1,96,128]{2,1,0:T(8,128)} %s_ref.5) | copy-start | bytes 147460
  2.9 0.8 %copy-start.2 = (f32[1,96,128]{2,1,0:T(8,128)S(1)}, f32[1,96,128]{2,1,0:T(8,128)}, u32[]{:S(2)}) copy-start(f32[1,96,128]{2,1,0:T(8,128)} %u_ref.5) | copy-start | bytes 147460
  3.7 0.8 %copy-start.3 = (f32[1,96,128]{2,1,0:T(8,128)S(1)}, f32[1,96,128]{2,1,0:T(8,128)}, u32[]{:S(2)}) copy-start(f32[1,96,128]{2,1,0:T(8,128)} %v_ref.5) | copy-start | bytes 147460
  4.5 0.8 %copy-start.4 = (s32[1,96,128]{2,1,0:T(8,128)S(1)}, s32[1,96,128]{2,1,0:T(8,128)}, u32[]{:S(2)}) copy-start(s32[1,96,128]{2,1,0:T(8,128)} %m_ref.5) | copy-start | bytes 147460
  5.3 15.8 %collective-permute-start = (f32[48,128]{1,0:T(8,128)S(1)}, f32[48,128]{1,0:T(8,128)S(1)}, u32[]{:S(2)}, u32[]{:S(2)}) collective-permute-start(f32[48,128]{1,0:T(8,128)S(1)} %get-tuple-element.9), channel_id=1, source_target_pairs={{0,1},{1,0},{2,3},{3,2},{4,5},{5,4},{6,7},{7,6},{8,9},{9,8},{10,11... | collective-permute-start | bytes 73736 | tf_op jit(solution)/shard_map/ppermute | solution.py:437
  7.9 14.4 %collective-permute-start.1 = (f32[48,128]{1,0:T(8,128)S(1)}, f32[48,128]{1,0:T(8,128)S(1)}, u32[]{:S(2)}, u32[]{:S(2)}) collective-permute-start(f32[48,128]{1,0:T(8,128)S(1)} %get-tuple-element.8.sb_ref), channel_id=1, source_target_pairs={{1,2},{2,1},{3,4},{4,3},{5,6},{6,5},{7,8},{8,7},{9,10},{10,9},{11,... | collective-permute-start | bytes 73736 | tf_op jit(solution)/shard_map/ppermute | solution.py:438
  22.5 5.3 %collective-permute-start.3 = (f32[136,128]{1,0:T(8,128)S(1)}, f32[136,128]{1,0:T(8,128)S(1)}, u32[]{:S(2)}, u32[]{:S(2)}) collective-permute-start(f32[136,128]{1,0:T(8,128)S(1)} %get-tuple-element.11), channel_id=1, source_target_pairs={{0,496},{1,497},{2,498},{3,499},{4,500},{5,501},{6,502},{7,503},{8... | collective-permute-start | bytes 208904 | tf_op jit(solution)/shard_map/ppermute | solution.py:434
  24.5 5.1 %collective-permute-start.2 = (f32[136,128]{1,0:T(8,128)S(1)}, f32[136,128]{1,0:T(8,128)S(1)}, u32[]{:S(2)}, u32[]{:S(2)}) collective-permute-start(f32[136,128]{1,0:T(8,128)S(1)} %get-tuple-element.10), channel_id=1, source_target_pairs={{0,16},{1,17},{2,18},{3,19},{4,20},{5,21},{6,22},{7,23},{8,24},{9,... | collective-permute-start | bytes 208904 | tf_op jit(solution)/shard_map/ppermute | solution.py:434
  27.8 0.6 copy-start.5
  29.5 0.8 %slice-start = ((f32[136,128]{1,0:T(8,128)}), f32[96,128]{1,0:T(8,128)S(1)}, s32[]{:S(2)}) async-start(f32[136,128]{1,0:T(8,128)} %copy-done.5), calls=%async_computation | async-start | bytes 98304 | tf_op jit(solution)/shard_map/slice | solution.py:445
  30.3 25.6 %copy-start.6 = (f32[136,128]{1,0:T(8,128)S(1)}, f32[136,128]{1,0:T(8,128)}, u32[]{:S(2)}) copy-start(f32[136,128]{1,0:T(8,128)} %copy-done.5) | copy-start | bytes 208900
  30.3 15.9 %collective-permute-start.5 = (f32[288,128]{1,0:T(8,128)S(1)}, f32[288,128]{1,0:T(8,128)S(1)}, u32[]{:S(2)}, u32[]{:S(2)}) collective-permute-start(f32[288,128]{1,0:T(8,128)S(1)} %pad_maximum_fusion), channel_id=1, source_target_pairs={{15,479},{31,495},{47,511},{63,15},{79,31},{95,47},{111,63},{127,7... | collective-permute-start | bytes 442376 | tf_op jit(solution)/shard_map/ppermute | solution.py:434
  42.0 13.9 %collective-permute-start.4 = (f32[288,128]{1,0:T(8,128)S(1)}, f32[288,128]{1,0:T(8,128)S(1)}, u32[]{:S(2)}, u32[]{:S(2)}) collective-permute-start(f32[288,128]{1,0:T(8,128)S(1)} %pad_maximum_fusion), channel_id=1, source_target_pairs={{15,63},{31,79},{47,95},{63,111},{79,127},{95,143},{111,159},{127,... | collective-permute-start | bytes 442376 | tf_op jit(solution)/shard_map/ppermute | solution.py:434

commit v2 on v0

v2 whole, which is shorter than its diff:
```python
import functools

import jax
import jax.numpy as jnp
from jax import lax
from jax.experimental import pallas as pl
from jax.experimental.pallas import tpu as pltpu
from jax.sharding import PartitionSpec as P

STEPS = 4
TIME_STEP = 0.1
DIFFUSE = 0.15
EXPAND = 0.2
CONTRACT = 0.8
ROTATION = 0.5

HALO = 2 * STEPS
LANES = 128
FIELDS = 4
REACH = 4
ARC = 2 * REACH + 1
CAP = 48
PARITY = (1.0, 1.0, -1.0, -1.0)
GROUP = 14
FAR_ROWS = (2, 4, 6)
FAR = 128
UPPER = 24


def lane_index(rows=8):
    return lax.broadcasted_iota(jnp.int32, (rows, LANES), 1)


def roll(x, shift):
    shift = shift % LANES
    return x if shift == 0 else pltpu.roll(x, shift, 1)


def is_odd():
    return lax.rem(lax.axis_index("lat"), 2) == 1


def is_top():
    return lax.axis_index("lat") == lax.axis_size("lat") - 1


def edge_rows(refs, start, buffer, ints, sems):
    copies = []
    for i, ref in enumerate(refs):
        target = buffer.at[pl.ds(8 * i, 8), :] if i < FIELDS else ints.at[pl.ds(0, 8), :]
        copies.append(
            pltpu.make_async_copy(ref.at[0, pl.ds(start, HALO), :], target, sems.at[i])
        )
    return copies


def fold_rows_kernel(t_ref, s_ref, u_ref, v_ref, m_ref, opp_ref, b_ref, ints, sems):
    height = t_ref.shape[1]
    start = pl.multiple_of(jnp.where(is_odd(), height - HALO, 0), 8)
    copies = edge_rows((t_ref, s_ref, u_ref, v_ref, m_ref), start, b_ref, ints, sems)
    copies.append(pltpu.make_async_copy(opp_ref, ints.at[pl.ds(8, 1), :], sems.at[5]))
    for copy in copies:
        copy.start()
    for copy in copies:
        copy.wait()
    b_ref[32:40, :] = ints[0:8, :].astype(jnp.float32)
    b_ref[40:48, :] = jnp.broadcast_to(ints[8:9, :].astype(jnp.float32), (8, LANES))


def load_kernel(t_ref, s_ref, u_ref, v_ref, m_ref, b_ref, fields, a_ref, ints, sems):
    height = t_ref.shape[1]
    copies = []
    for i, ref in enumerate((t_ref, s_ref, u_ref, v_ref, m_ref)):
        target = fields.at[i] if i < FIELDS else ints
        copies.append(pltpu.make_async_copy(ref.at[0], target, sems.at[i]))
    for copy in copies:
        copy.start()
    for copy in copies:
        copy.wait()
    fields[FIELDS] = ints[...].astype(jnp.float32)
    odd = is_odd()
    for i in range(5):
        a_ref[i * 8 : i * 8 + 8, :] = jnp.where(
            odd, fields[i, 0:HALO, :], fields[i, height - HALO : height, :]
        )


def halo_tiles(fields, ra_ref, rb_ref, odd, i):
    ra, rb = ra_ref[i * 8 : i * 8 + 8, :], rb_ref[i * 8 : i * 8 + 8, :]
    own = [fields[i, 8 * g : 8 * g + 8, :] for g in range(fields.shape[1] // 8)]
    return [jnp.where(odd, ra, rb)] + own + [jnp.where(odd, rb, ra)]


def columns_kernel(fields, sb_ref, ra_ref, rb_ref, e_ref, w_ref):
    odd = is_odd()
    lane = lane_index()
    for i in range(5):
        tiles = halo_tiles(fields, ra_ref, rb_ref, odd, i)
        east = jnp.zeros((8, LANES), jnp.float32)
        west = jnp.zeros((8, LANES), jnp.float32)
        for g, tile in enumerate(tiles):
            here = (lane >= 8 * g) & (lane < 8 * g + 8)
            east = jnp.where(here, roll(tile, 8 * g - (LANES - HALO)), east)
            west = jnp.where(here, roll(tile, 8 * g), west)
        e_ref[i * 8 : i * 8 + 8, :] = east
        w_ref[i * 8 : i * 8 + 8, :] = west
    for ref in (e_ref, w_ref):
        ref[40 : 40 + CAP, :] = sb_ref[...]
        ref[40 + CAP : 40 + 2 * CAP, :] = rb_ref[...]


def far_places(counts):
    base = 0
    for j, n in enumerate(counts):
        for side in (0, 1):
            yield j, side, n, base
            base += 5 * n + 1


def far_kernel(sb_ref, rb_ref, rw_ref, re_ref, e_ref, w_ref):
    @pl.when(is_top())
    def _():
        sources = (
            ((rw_ref, 40), (rw_ref, 40 + CAP)),
            ((sb_ref, 0), (rb_ref, 0)),
            ((re_ref, 40), (re_ref, 40 + CAP)),
        )
        for out, counts in ((e_ref, FAR_ROWS), (w_ref, FAR_ROWS[::-1])):
            for j, side, n, base in far_places(counts):
                ref, at = sources[j][side]
                for i in range(5):
                    out[base + i * n : base + i * n + n, :] = ref[
                        at + 8 * i + 8 - n : at + 8 * i + 8, :
                    ]
                out[base + 5 * n : base + 5 * n + 1, :] = ref[at + 40 : at + 41, :]
            out[FAR - 2 : FAR, :] = jnp.zeros((2, LANES), jnp.float32)


def first_pass(centre, north, south, east, west, sea, count, w_e, w_n, w_s, turn, roll_w):
    laps = [
        sea * (((east[i] + west[i]) + (north[i] + south[i])) - count * centre[i])
        for i in range(FIELDS)
    ]
    t, s, u, v = centre
    flow_e = w_e * (u + east[2])
    flow_n = w_n * (v + north[3])
    flow_s = w_s * (v + south[3])
    partial = []
    for i in (0, 1):
        c = centre[i]
        x = flow_e * (c + east[i])
        y = flow_n * (c + north[i]) - flow_s * (c + south[i])
        partial.append(c - (0.25 * TIME_STEP) * ((x - roll_w[i](x)) + y))
    ratio = EXPAND / CONTRACT
    slope = 0.25 * TIME_STEP * CONTRACT
    q = s - ratio * t
    q_e = east[1] - ratio * east[0]
    q_n = north[1] - ratio * north[0]
    q_s = south[1] - ratio * south[0]
    d = w_e * (q_e - q)
    partial.append(u + (turn * v - slope * (d + roll_w[2](d))))
    partial.append(v - (turn * u + slope * (w_n * (q_n - q) + w_s * (q - q_s))))
    return laps, partial


def second_pass(partial, lap, north, south, east, west, sea, count):
    mix = ((east + west) + (north + south)) - count * lap
    return sea * (partial - (TIME_STEP * DIFFUSE) * mix)


class Band:
    def __init__(self, state, laps, part, stat):
        self.state, self.laps, self.part, self.stat = state, laps, part, stat
        self.tiles = state.shape[1] // 8 - 2

    def pad(self):
        nothing = jnp.zeros((8, LANES), jnp.float32)
        for row in (0, 8 + 8 * self.tiles):
            for i in range(FIELDS):
                self.state[i, row : row + 8, :] = nothing
                self.laps[i, row : row + 8, :] = nothing
            for i in range(4):
                self.stat[i, row : row + 8, :] = nothing

    def each_tile(self, work, group):
        def trip(n, carry):
            start = pl.multiple_of(8 + 8 * group * n, 8)
            for j in range(group):
                work(start + 8 * j)
            return carry

        lax.fori_loop(0, self.tiles // group, trip, 0)

    def weigh(self, turning):
        def work(r):
            sea = self.stat[0, pl.ds(r, 8), :]
            north = self.stat[0, pl.ds(r + 1, 8), :]
            south = self.stat[0, pl.ds(r - 1, 8), :]
            east, west = roll(sea, -1), roll(sea, 1)
            self.stat[1, pl.ds(r, 8), :] = (east + west) + (north + south)
            self.stat[2, pl.ds(r, 8), :] = sea * east
            self.stat[3, pl.ds(r, 8), :] = sea * north
            self.stat[4, pl.ds(r, 8), :] = turning(r)
            for i in range(FIELDS):
                self.state[i, pl.ds(r, 8), :] = sea * self.state[i, pl.ds(r, 8), :]

        return work

    def first(self, r):
        def rows(ref, i, by=0):
            return ref[i, pl.ds(r + by, 8), :]

        centre = [rows(self.state, i) for i in range(FIELDS)]
        lap, partial = first_pass(
            centre,
            [rows(self.state, i, 1) for i in range(FIELDS)],
            [rows(self.state, i, -1) for i in range(FIELDS)],
            [roll(x, -1) for x in centre],
            [roll(x, 1) for x in centre],
            rows(self.stat, 0),
            rows(self.stat, 1),
            rows(self.stat, 2),
            rows(self.stat, 3),
            rows(self.stat, 3, -1),
            rows(self.stat, 4),
            (lambda x: roll(x, 1),) * 3,
        )
        for i in range(FIELDS):
            self.laps[i, pl.ds(r, 8), :] = lap[i]
            self.part[i, pl.ds(r, 8), :] = partial[i]

    def second(self, r):
        sea, count = self.stat[0, pl.ds(r, 8), :], self.stat[1, pl.ds(r, 8), :]
        for i in range(FIELDS):
            lap = self.laps[i, pl.ds(r, 8), :]
            self.state[i, pl.ds(r, 8), :] = second_pass(
                self.part[i, pl.ds(r, 8), :],
                lap,
                self.laps[i, pl.ds(r + 1, 8), :],
                self.laps[i, pl.ds(r - 1, 8), :],
                roll(lap, -1),
                roll(lap, 1),
                sea,
                count,
            )

    def step(self, group):
        self.each_tile(self.first, group)
        self.each_tile(self.second, group)


def shifted_ghosts(blocks):
    before, here, after = blocks
    lane = lane_index(here.shape[0])
    return (
        jnp.where(lane < HALO, roll(before, HALO), roll(here, HALO)),
        jnp.where(lane >= LANES - HALO, roll(after, -HALO), roll(here, -HALO)),
    )


def turning_of(row, total_rows):
    return (TIME_STEP * ROTATION) * (2.0 * (row + 0.5) / total_rows - 1.0)


def row_in_tile():
    return lax.broadcasted_iota(jnp.int32, (8, LANES), 0).astype(jnp.float32)


def main_kernel(
    fields,
    sb_ref,
    ra_ref,
    rb_ref,
    rw_ref,
    re_ref,
    t_out,
    s_out,
    u_out,
    v_out,
    upper_state,
    upper_stat,
    state,
    laps,
    part,
    stat,
):
    odd, top = is_odd(), is_top()
    lane = lane_index()
    height = fields.shape[1]
    total_rows = height * lax.axis_size("lat")
    tiles_n = height // 8 + 2
    band = 8 * tiles_n
    bands = Band(state, laps, part, stat)

    for i in range(5):
        tiles = halo_tiles(fields, ra_ref, rb_ref, odd, i)
        from_w, from_e = rw_ref[i * 8 : i * 8 + 8, :], re_ref[i * 8 : i * 8 + 8, :]
        ref, at = (state, i) if i < FIELDS else (stat, 0)
        for g, tile in enumerate(tiles):
            ref[at, 8 + 8 * g : 16 + 8 * g, :] = jnp.where(
                lane < HALO, roll(from_w, -8 * g), roll(tile, HALO)
            )
            ref[at, 8 + band + 8 * g : 16 + band + 8 * g, :] = jnp.where(
                lane >= LANES - HALO, roll(from_e, LANES - HALO - 8 * g), roll(tile, -HALO)
            )
    bands.pad()

    @pl.when(top)
    def _():
        pairs = ((rw_ref, 40, rw_ref, 40 + CAP), (sb_ref, 0, rb_ref, 0), (re_ref, 40, re_ref, 40 + CAP))
        for i in range(5):
            ghosts = []
            for own, own_at, facing, facing_at in pairs:
                index = lax.rem(own[own_at + 40 : own_at + 48, :].astype(jnp.int32), LANES)
                rows = facing[facing_at + 8 * i : facing_at + 8 * i + 8, :]
                ghosts.append(
                    (PARITY + (1.0,))[i]
                    * jnp.take_along_axis(rows, index, axis=1, mode="promise_in_bounds")
                )
            ref, at = (state, i) if i < FIELDS else (stat, 0)
            for which, ghost in enumerate(shifted_ghosts(ghosts)):
                row = 8 + band * (which + 1) - HALO
                ref[at, row : row + 1, :] = ghost[7:8, :]
                ref[at, row + 1 : row + 2, :] = ghost[6:7, :]

    base_row = (lax.axis_index("lat") * height - HALO).astype(jnp.float32)
    sub = row_in_tile()
    bands.each_tile(
        bands.weigh(
            lambda r: turning_of(
                base_row + lax.rem(r - 8, band).astype(jnp.float32) + sub, total_rows
            )
        ),
        GROUP,
    )

    def step(n, carry):
        bands.step(GROUP)

        @pl.when(top & (n == 0))
        def _():
            for which in (0, 1):
                row = 8 + band * (which + 1) - UPPER
                for i in range(FIELDS):
                    upper_state[i, which] = state[i, row : row + UPPER, :]
                for i in range(5):
                    upper_stat[i, which] = stat[i, row : row + UPPER, :]

        return carry

    lax.fori_loop(0, STEPS, step, 0)

    for i, out in enumerate((t_out, s_out, u_out, v_out)):
        for g in range(height // 8):
            r = 8 + HALO + 8 * g
            west, east = state[i, r : r + 8, :], state[i, r + band : r + band + 8, :]
            out[0, 8 * g : 8 * g + 8, :] = jnp.where(
                lane < LANES // 2, roll(west, -HALO), roll(east, HALO)
            )


def arc_neighbours(blocks):
    lane = lane_index()
    last = len(blocks) - 1
    e, w = [roll(x, -1) for x in blocks], [roll(x, 1) for x in blocks]
    east = [jnp.where(lane == LANES - 1, e[min(k + 1, last)], e[k]) for k in range(last + 1)]
    west = [jnp.where(lane == 0, w[max(k - 1, 0)], w[k]) for k in range(last + 1)]
    return east, west


def cap_kernel(
    t_in,
    s_in,
    u_in,
    v_in,
    upper_state,
    upper_stat,
    sb_ref,
    rb_ref,
    rw_ref,
    re_ref,
    w3_ref,
    e3_ref,
    t_out,
    s_out,
    u_out,
    v_out,
    state,
    laps,
    part,
    stat,
    cap,
    cap_lap,
    cap_part,
    cap_stat,
    cap_opp,
    rows_out,
    sems,
):
    lane = lane_index()
    height = t_out.shape[1]
    total_rows = height * lax.axis_size("lat")
    bands = Band(state, laps, part, stat)
    nothing = jnp.zeros((8, LANES), jnp.float32)
    cap_turn = turning_of(float(total_rows - HALO + 1) + row_in_tile(), total_rows)

    def fill_ghosts(ref, parities, low, high, sides):
        def one(side, carry):
            ghosts = {}
            for k in range(low, high):
                index = cap_opp[side, k]
                for i, parity in enumerate(parities):
                    rows = ref[1 - side, i, ARC - 1 - k, 0:8, :]
                    ghosts[k, i] = parity * jnp.take_along_axis(
                        rows, index, axis=1, mode="promise_in_bounds"
                    )
            for (k, i), ghost in ghosts.items():
                ref[side, i, k, 8:9, :] = ghost[7:8, :]
                ref[side, i, k, 9:10, :] = ghost[6:7, :]
            return carry

        lax.fori_loop(0, sides, one, 0)

    def put_block(side, place, ref, base, n):
        sea = ref[base + 4 * n : base + 5 * n, :]
        cap_stat[side, 0, place, 8 - n : 8, :] = sea
        cap_stat[side, 0, place, 10:16, :] = nothing[0:6]
        if n < 8:
            cap_stat[side, 0, place, 0 : 8 - n, :] = nothing[n:8]
        for i in range(FIELDS):
            cap[side, i, place, 8 - n : 8, :] = sea * ref[base + n * i : base + n * i + n, :]
            if n < 8:
                cap[side, i, place, 0 : 8 - n, :] = nothing[n:8]
            cap[side, i, place, 10:16, :] = nothing[0:6]
            cap_lap[side, i, place, 0:8, :] = nothing
            cap_lap[side, i, place, 8:16, :] = nothing
        opp = jnp.broadcast_to(ref[base + 5 * n : base + 5 * n + 1, :], (8, LANES))
        cap_opp[side, place] = lax.rem(opp.astype(jnp.int32), LANES)

    def cap_weigh():
        for side in (0, 1):
            for start in (0, 1):
                seas = [cap_stat[side, 0, k, start : start + 8, :] for k in range(ARC)]
                east, west = arc_neighbours(seas)
                for k in range(ARC):
                    north = cap_stat[side, 0, k, start + 1 : start + 9, :]
                    if start:
                        south = cap_stat[side, 0, k, start - 1 : start + 7, :]
                        cap_stat[side, 1, k, 1:9, :] = (east[k] + west[k]) + (north + south)
                    cap_stat[side, 2, k, start : start + 8, :] = seas[k] * east[k]
                    cap_stat[side, 3, k, start : start + 8, :] = seas[k] * north

    def cap_first(side, low, high):
        ratio = EXPAND / CONTRACT
        span = range(low - 1, high + 1)
        fields = []
        for i in range(FIELDS):
            blocks = [cap[side, i, k, 1:9, :] for k in span]
            fields.append((blocks, *arc_neighbours(blocks)))
        for n, k in enumerate(span):
            b, be = [f[0][n - 1] for f in fields], [f[1][n - 1] for f in fields]
            w_e = cap_stat[side, 2, max(k - 1, 0), 1:9, :]
            flow = w_e * (b[2] + be[2])
            faces = [flow * (b[i] + be[i]) for i in (0, 1)]
            faces.append(w_e * ((be[1] - ratio * be[0]) - (b[1] - ratio * b[0])))
            lap, partial = first_pass(
                [f[0][n] for f in fields],
                [cap[side, i, k, 2:10, :] for i in range(FIELDS)],
                [cap[side, i, k, 0:8, :] for i in range(FIELDS)],
                [f[1][n] for f in fields],
                [f[2][n] for f in fields],
                cap_stat[side, 0, k, 1:9, :],
                cap_stat[side, 1, k, 1:9, :],
                cap_stat[side, 2, k, 1:9, :],
                cap_stat[side, 3, k, 1:9, :],
                cap_stat[side, 3, k, 0:8, :],
                cap_turn,
                [
                    lambda x, face=face: roll(jnp.where(lane == LANES - 1, face, x), 1)
                    for face in faces
                ],
            )
            for i in range(FIELDS):
                cap_lap[side, i, k, 1:9, :] = lap[i]
                if low <= k < high:
                    cap_part[side, i, k, 0:8, :] = partial[i]

    def cap_second(side, low, high):
        for i in range(FIELDS):
            blocks = [cap_lap[side, i, k, 1:9, :] for k in range(low - 1, high + 1)]
            east, west = arc_neighbours(blocks)
            for n, k in enumerate(range(low - 1, high + 1)):
                if low <= k < high:
                    cap[side, i, k, 1:9, :] = second_pass(
                        cap_part[side, i, k, 0:8, :],
                        blocks[n],
                        cap_lap[side, i, k, 2:10, :],
                        cap_lap[side, i, k, 0:8, :],
                        east[n],
                        west[n],
                        cap_stat[side, 0, k, 1:9, :],
                        cap_stat[side, 1, k, 1:9, :],
                    )

    @pl.when(is_top())
    def _():
        parts = [(j, side, w3_ref, base, n) for j, side, n, base in far_places(FAR_ROWS)]
        parts += [
            (j + REACH + 2, side, e3_ref, base, n)
            for j, side, n, base in far_places(FAR_ROWS[::-1])
        ]
        for side in (0, 1):
            parts.append((REACH - 1, side, rw_ref, 40 + CAP * side, 8))
            parts.append((REACH, side, (sb_ref, rb_ref)[side], 0, 8))
            parts.append((REACH + 1, side, re_ref, 40 + CAP * side, 8))
        for k, side, ref, base, n in parts:
            put_block(side, ARC - 1 - k if side else k, ref, base, n)
        bands.pad()
        for which in (0, 1):
            row = 8 + UPPER * which
            for i in range(FIELDS):
                state[i, row : row + UPPER, :] = upper_state[i, which]
            for i in range(5):
                stat[i, row : row + UPPER, :] = upper_stat[i, which]
        fill_ghosts(cap_stat, (1.0,), 0, ARC, 2)
        fill_ghosts(cap, PARITY, 0, ARC, 2)
        cap_weigh()
        for n in range(STEPS - 1):
            low, high = n + 1, ARC - 1 - n
            first_side = 1 if n == STEPS - 2 else 0

            def one(side, carry, low=low, high=high):
                cap_first(side, low, high)
                cap_second(side, low, high)
                return carry

            lax.fori_loop(first_side, 2, one, 0)
            fill_ghosts(cap, PARITY, low, high, 2 - first_side)
            for i in range(FIELDS):
                ghosts = [cap[0, i, k, 8:10, :] for k in (REACH - 1, REACH, REACH + 1)]
                for which, ghost in enumerate(shifted_ghosts(ghosts)):
                    row = 8 + UPPER * (which + 1) - HALO
                    state[i, row : row + 2, :] = ghost
            bands.step(bands.tiles)
        copies = []
        for i, out in enumerate((t_out, s_out, u_out, v_out)):
            row = 8 + UPPER - 2 * HALO
            west, east = state[i, row : row + 8, :], state[i, row + UPPER : row + UPPER + 8, :]
            rows_out[i] = jnp.where(lane < LANES // 2, roll(west, -HALO), roll(east, HALO))
            copies.append(
                pltpu.make_async_copy(
                    rows_out.at[i], out.at[0, pl.ds(height - HALO, HALO), :], sems.at[i]
                )
            )
        for copy in copies:
            copy.start()
        for copy in copies:
            copy.wait()


def body(lon_count, lat_count, t, s, u, v, m, opp):
    fields = (t, s, u, v, m)
    height = t.shape[1]
    vmem, anywhere = (
        pl.BlockSpec(memory_space=pltpu.VMEM),
        pl.BlockSpec(memory_space=pltpu.HBM),
    )
    f32, i32 = jnp.float32, jnp.int32

    def call(kernel, inputs, shapes, scratch=(), far=0, room=32 * 1024, flops=0):
        return pl.pallas_call(
            kernel,
            out_shape=[jax.ShapeDtypeStruct(shape, f32) for shape in shapes],
            in_specs=[anywhere] * far + [vmem] * (len(inputs) - far),
            out_specs=[vmem] * len(shapes),
            scratch_shapes=list(scratch),
            compiler_params=pltpu.CompilerParams(vmem_limit_bytes=(64 * 1024 - room) * 1024),
            cost_estimate=pl.CostEstimate(flops=flops, bytes_accessed=flops, transcendentals=0),
        )(*inputs)

    def place(lon, lat):
        return (lon % lon_count) * lat_count + lat

    lons, lats = range(lon_count), range(lat_count)
    last = lat_count - 1
    pairs_a = [(place(i, j), place(i, j ^ 1)) for i in lons for j in lats]
    pairs_b = [(place(i, j), place(i, ((j - 1) ^ 1) + 1)) for i in lons for j in lats[1:last]]
    pairs_b += [(place(i, last), place(-i, last)) for i in lons]

    def shift(x, by, rows):
        pairs = [(place(i, j), place(i + by, j)) for i in lons for j in rows]
        return lax.ppermute(x, ("lon", "lat"), pairs)

    (send_b,) = call(
        fold_rows_kernel,
        (*fields, opp.reshape(1, LANES)),
        [(CAP, LANES)],
        [pltpu.VMEM((16, LANES), i32), pltpu.SemaphoreType.DMA((6,))],
        far=6,
        room=64,
    )
    from_b = lax.ppermute(send_b, ("lon", "lat"), pairs_b)
    stack, send_a = call(
        load_kernel,
        (*fields, send_b),
        [(5, height, LANES), (CAP, LANES)],
        [pltpu.VMEM((height, LANES), i32), pltpu.SemaphoreType.DMA((5,))],
        far=5,
        room=384,
    )
    from_a = lax.ppermute(send_a, ("lon", "lat"), pairs_a)
    wide = 40 + 2 * CAP
    send_e, send_w = call(columns_kernel, (stack, send_b, from_a, from_b), [(wide, LANES)] * 2)
    from_w = shift(send_e, 1, lats)
    from_e = shift(send_w, -1, lats)
    send_far_e, send_far_w = call(
        far_kernel, (send_b, from_b, from_w, from_e), [(FAR, LANES)] * 2
    )
    far_w = shift(send_far_e, 3, [last])
    far_e = shift(send_far_w, -3, [last])

    def band_scratch(rows):
        return [pltpu.VMEM((n, 16 + 2 * rows, LANES), f32) for n in (FIELDS, FIELDS, FIELDS, 5)]

    *outs, upper_state, upper_stat = call(
        main_kernel,
        (stack, send_b, from_a, from_b, from_w, from_e),
        [t.shape] * 4 + [(FIELDS, 2, UPPER, LANES), (5, 2, UPPER, LANES)],
        band_scratch(height + 2 * HALO),
        flops=10**7,
    )
    return tuple(
        pl.pallas_call(
            cap_kernel,
            out_shape=[jax.ShapeDtypeStruct(t.shape, f32)] * 4,
            in_specs=[anywhere] * 4 + [vmem] * 8,
            out_specs=[anywhere] * 4,
            scratch_shapes=band_scratch(UPPER)
            + [
                pltpu.VMEM((2, FIELDS, ARC, 16, LANES), f32),
                pltpu.VMEM((2, FIELDS, ARC, 16, LANES), f32),
                pltpu.VMEM((2, FIELDS, ARC, 8, LANES), f32),
                pltpu.VMEM((2, 4, ARC, 16, LANES), f32),
                pltpu.VMEM((2, ARC, 8, LANES), i32),
                pltpu.VMEM((FIELDS, 8, LANES), f32),
                pltpu.SemaphoreType.DMA((FIELDS,)),
            ],
            input_output_aliases={i: i for i in range(4)},
            compiler_params=pltpu.CompilerParams(vmem_limit_bytes=32 * 1024 * 1024),
        )(*outs, upper_state, upper_stat, send_b, from_b, from_w, from_e, far_w, far_e)
    )


def solution(mesh):
    placed = P(None, "lat", "lon")
    return jax.shard_map(
        functools.partial(body, mesh.shape["lon"], mesh.shape["lat"]),
        mesh=mesh,
        in_specs=(placed,) * 5 + (P("lon"),),
        out_specs=(placed,) * 4,
        check_vma=False,
    )
```

time: 1100 us -> 55.7 us (0.05)
  the two profiles are of different devices: /device:TPU:1 before, /device:TPU:71 now
where the time goes in v2:
time: 55.7 us; the launch traced here: 55.3 us
  starting transfers between devices  38 us (68%)
  Pallas kernels  13.9 us (25%)
  waiting for transfers between devices  1.71 us (3%)
  local copies, waits for them, and re-layouts  0.95 us (2%)
  between operations  0.74 us (1%)
    ppermute x4, starting transfers between devices, shift(): return lax.ppermute(x, ('lon', 'lat'), pairs)  34.8 us
    pallas_call x5, Pallas kernels, call(): pl.pallas_call(kernel, out_shape=[jax.ShapeDtypeStruct(shape, f32) for sh...  9.83 us
    pallas_call x1, Pallas kernels, body(): pl.pallas_call(cap_kernel, out_shape=[jax.ShapeDtypeStruct(t.shape, f32)]...  4.02 us
    ppermute x1, starting transfers between devices, body(): from_a = lax.ppermute(send_a, ('lon', 'lat'), pairs_a)  2.58 us
    ppermute x4, waiting for transfers between devices, shift(): return lax.ppermute(x, ('lon', 'lat'), pairs)  1.35 us
  transfers between devices with their start and end apart: 6, of which 2 were waited for; matrix products, arithmetic and copies ran while one was open for 0% of the time, Pallas kernels for 10%

profile of v2, /device:TPU:71, one launch (start us, length us, event | category | flops | bytes accessed | tf_op | source)
XLA Modules:
  0.0 55.3 jit_solution(9958086838013284600)
XLA Ops:
  0.6 1.4 %shard_map.93.b_ref.sb_ref = f32[48,128]{1,0:T(8,128)} custom-call(f32[1,96,128]{2,1,0:T(8,128)} %t_ref.3, f32[1,96,128]{2,1,0:T(8,128)} %s_ref.3, f32[1,96,128]{2,1,0:T(8,128)} %u_ref.3, f32[1,96,128]{2,1,0:T(8,128)} %v_ref.3, s32[1,96,128]{2,1,0:T(8,128)} %m_ref.3, s32[1,128]{1,0:T(1,128)} %bitcast.1), custom_call_target="tpu_custom_call" | custom-call | tf_op jit(solution)/shard_map/pallas_call | solution.py:571
  2.1 0.0 copy-start.2
  2.1 2.4 %shard_map.94 = (f32[5,96,128]{2,1,0:T(8,128)}, f32[48,128]{1,0:T(8,128)}) custom-call(f32[1,96,128]{2,1,0:T(8,128)} %t_ref.3, f32[1,96,128]{2,1,0:T(8,128)} %s_ref.3, f32[1,96,128]{2,1,0:T(8,128)} %u_ref.3, f32[1,96,128]{2,1,0:T(8,128)} %v_ref.3, s32[1,96,128]{2,1,0:T(8,128)} %m_ref.3, f32[48,128]{1,0:T(8,128)} %shard_map.93.b_ref.sb_ref), custom_call_target="tpu_custom_call" | custom-call | tf_op jit(solution)/shard_map/pallas_call | solution.py:571
  4.5 2.6 %collective-permute-start = (f32[48,128]{1,0:T(8,128)}, f32[48,128]{1,0:T(8,128)S(1)}, u32[]{:S(2)}, u32[]{:S(2)}) collective-permute-start(f32[48,128]{1,0:T(8,128)} %get-tuple-element.17), channel_id=1, source_target_pairs={{0,1},{1,0},{2,3},{3,2},{4,5},{5,4},{6,7},{7,6},{8,9},{9,8},{10,11... | collective-permute-start | bytes 73736 | tf_op jit(solution)/shard_map/ppermute | solution.py:611
  7.1 0.0 copy-done.2
  7.1 0.7 %collective-permute-start.1 = (f32[48,128]{1,0:T(8,128)S(1)}, f32[48,128]{1,0:T(8,128)S(1)}, u32[]{:S(2)}, u32[]{:S(2)}) collective-permute-start(f32[48,128]{1,0:T(8,128)S(1)} %copy-done.2), channel_id=1, source_target_pairs={{1,2},{2,1},{3,4},{4,3},{5,6},{6,5},{7,8},{8,7},{9,10},{10,9},{11,... | collective-permute-start | bytes 73736 | tf_op jit(solution)/shard_map/ppermute | solution.py:602
  7.8 0.4 collective-permute-done.ra_ref
  8.2 0.0 collective-permute-done.1.rb_ref
  8.2 0.0 copy-start
  8.2 0.9 %copy-done = f32[5,96,128]{2,1,0:T(8,128)S(1)} copy-done((f32[5,96,128]{2,1,0:T(8,128)S(1)}, f32[5,96,128]{2,1,0:T(8,128)}, u32[]{:S(2)}) %copy-start) | copy-done | bytes 245784
  9.1 0.0 copy-start.1
  9.1 0.2 shard_map.95
  9.3 15.9 %collective-permute-start.2 = (f32[136,128]{1,0:T(8,128)S(1)}, f32[136,128]{1,0:T(8,128)S(1)}, u32[]{:S(2)}, u32[]{:S(2)}) collective-permute-start(f32[136,128]{1,0:T(8,128)S(1)} %get-tuple-element.18), channel_id=1, source_target_pairs={{0,16},{1,17},{2,18},{3,19},{4,20},{5,21},{6,22},{7,23},{8,24},{9,... | collective-permute-start | bytes 208904 | tf_op jit(solution)/shard_map/ppermute | solution.py:592
  25.3 7.6 %collective-permute-start.3 = (f32[136,128]{1,0:T(8,128)S(1)}, f32[136,128]{1,0:T(8,128)S(1)}, u32[]{:S(2)}, u32[]{:S(2)}) collective-permute-start(f32[136,128]{1,0:T(8,128)S(1)} %get-tuple-element.19), channel_id=1, source_target_pairs={{0,496},{1,497},{2,498},{3,499},{4,500},{5,501},{6,502},{7,503},{8... | collective-permute-start | bytes 208904 | tf_op jit(solution)/shard_map/ppermute | solution.py:592
  32.8 0.0 collective-permute-done.2.rw_ref
  32.9 1.3 %collective-permute-done.3.re_ref = f32[136,128]{1,0:T(8,128)S(1)} collective-permute-done((f32[136,128]{1,0:T(8,128)S(1)}, f32[136,128]{1,0:T(8,128)S(1)}, u32[]{:S(2)}, u32[]{:S(2)}) %collective-permute-start.3) | collective-permute-done | bytes 69664 | tf_op jit(solution)/shard_map/ppermute | solution.py:592
  34.2 1.9 %collective-permute-start.4 = (f32[128,128]{1,0:T(8,128)S(1)}, f32[128,128]{1,0:T(8,128)S(1)}, u32[]{:S(2)}, u32[]{:S(2)}) collective-permute-start(f32[128,128]{1,0:T(8,128)S(1)} %get-tuple-element.26), channel_id=1, source_target_pairs={{15,63},{31,79},{47,95},{63,111},{79,127},{95,143},{111,159},{127,... | collective-permute-start | bytes 196616 | tf_op jit(solution)/shard_map/ppermute | solution.py:592
  36.1 9.4 %collective-permute-start.5 = (f32[128,128]{1,0:T(8,128)S(1)}, f32[128,128]{1,0:T(8,128)S(1)}, u32[]{:S(2)}, u32[]{:S(2)}) collective-permute-start(f32[128,128]{1,0:T(8,128)S(1)} %get-tuple-element.27), channel_id=1, source_target_pairs={{15,479},{31,495},{47,511},{63,15},{79,31},{95,47},{111,63},{127,7... | collective-permute-start | bytes 196616 | tf_op jit(solution)/shard_map/ppermute | solution.py:592
  45.5 0.0 copy-done.1
  45.5 5.7 %shard_map.96 = (f32[1,96,128]{2,1,0:T(8,128)}, f32[1,96,128]{2,1,0:T(8,128)}, f32[1,96,128]{2,1,0:T(8,128)}, f32[1,96,128]{2,1,0:T(8,128)}, f32[4,2,24,128]{3,2...) custom-call(f32[5,96,128]{2,1,0:T(8,128)S(1)} %copy-done.1, f32[48,128]{1,0:T(8,128)S(1)} %copy-done.2, ...), custom_call_target="tpu_custom_call" | custom-call | flops 10000000 | bytes 10000000 | tf_op jit(solution)/shard_map/pallas_call | solution.py:571
  51.3 0.0 collective-permute-done.4.w3_ref
  51.3 0.0 collective-permute-done.5.e3_ref
  51.3 4.0 %shard_map.98 = (f32[1,96,128]{2,1,0:T(8,128)}, f32[1,96,128]{2,1,0:T(8,128)}, f32[1,96,128]{2,1,0:T(8,128)}, f32[1,96,128]{2,1,0:T(8,128)}) custom-call(f32[1,96,128]{2,1,0:T(8,128)} %get-tuple-element.20.t_in, f32[1,96,128]{2,1,0:T(8,128)} %get-tuple-element.21.s_in, ...), custom_call_target="tpu_custom_call", output_to_operand_aliasing={{0}: (0, {}), {1}: (1, {}), {2}: (2, {}), {3}: (3, {})} | custom-call | tf_op jit(solution)/shard_map/pallas_call | solution.py:633
  (1 shorter events, 0.0 us)
Async XLA Ops:
  2.1 5.1 %copy-start.2 = (f32[48,128]{1,0:T(8,128)S(1)}, f32[48,128]{1,0:T(8,128)}, u32[]{:S(2)}) copy-start(f32[48,128]{1,0:T(8,128)} %shard_map.93.b_ref.sb_ref) | copy-start | bytes 73732
  4.5 3.6 %collective-permute-start = (f32[48,128]{1,0:T(8,128)}, f32[48,128]{1,0:T(8,128)S(1)}, u32[]{:S(2)}, u32[]{:S(2)}) collective-permute-start(f32[48,128]{1,0:T(8,128)} %get-tuple-element.17), channel_id=1, source_target_pairs={{0,1},{1,0},{2,3},{3,2},{4,5},{5,4},{6,7},{7,6},{8,9},{9,8},{10,11... | collective-permute-start | bytes 73736 | tf_op jit(solution)/shard_map/ppermute | solution.py:611
  7.1 1.0 %collective-permute-start.1 = (f32[48,128]{1,0:T(8,128)S(1)}, f32[48,128]{1,0:T(8,128)S(1)}, u32[]{:S(2)}, u32[]{:S(2)}) collective-permute-start(f32[48,128]{1,0:T(8,128)S(1)} %copy-done.2), channel_id=1, source_target_pairs={{1,2},{2,1},{3,4},{4,3},{5,6},{6,5},{7,8},{8,7},{9,10},{10,9},{11,... | collective-permute-start | bytes 73736 | tf_op jit(solution)/shard_map/ppermute | solution.py:602
  8.2 0.9 %copy-start = (f32[5,96,128]{2,1,0:T(8,128)S(1)}, f32[5,96,128]{2,1,0:T(8,128)}, u32[]{:S(2)}) copy-start(f32[5,96,128]{2,1,0:T(8,128)} %get-tuple-element.16.fields) | copy-start | bytes 737284
  9.1 36.4 %copy-start.1 = (f32[5,96,128]{2,1,0:T(8,128)S(1)}, f32[5,96,128]{2,1,0:T(8,128)}, u32[]{:S(2)}) copy-start(f32[5,96,128]{2,1,0:T(8,128)} %get-tuple-element.16.fields) | copy-start | bytes 737284
  9.3 23.5 %collective-permute-start.2 = (f32[136,128]{1,0:T(8,128)S(1)}, f32[136,128]{1,0:T(8,128)S(1)}, u32[]{:S(2)}, u32[]{:S(2)}) collective-permute-start(f32[136,128]{1,0:T(8,128)S(1)} %get-tuple-element.18), channel_id=1, source_target_pairs={{0,16},{1,17},{2,18},{3,19},{4,20},{5,21},{6,22},{7,23},{8,24},{9,... | collective-permute-start | bytes 208904 | tf_op jit(solution)/shard_map/ppermute | solution.py:592
  25.3 8.9 %collective-permute-start.3 = (f32[136,128]{1,0:T(8,128)S(1)}, f32[136,128]{1,0:T(8,128)S(1)}, u32[]{:S(2)}, u32[]{:S(2)}) collective-permute-start(f32[136,128]{1,0:T(8,128)S(1)} %get-tuple-element.19), channel_id=1, source_target_pairs={{0,496},{1,497},{2,498},{3,499},{4,500},{5,501},{6,502},{7,503},{8... | collective-permute-start | bytes 208904 | tf_op jit(solution)/shard_map/ppermute | solution.py:592
  34.2 17.1 %collective-permute-start.4 = (f32[128,128]{1,0:T(8,128)S(1)}, f32[128,128]{1,0:T(8,128)S(1)}, u32[]{:S(2)}, u32[]{:S(2)}) collective-permute-start(f32[128,128]{1,0:T(8,128)S(1)} %get-tuple-element.26), channel_id=1, source_target_pairs={{15,63},{31,79},{47,95},{63,111},{79,127},{95,143},{111,159},{127,... | collective-permute-start | bytes 196616 | tf_op jit(solution)/shard_map/ppermute | solution.py:592
  36.1 15.1 %collective-permute-start.5 = (f32[128,128]{1,0:T(8,128)S(1)}, f32[128,128]{1,0:T(8,128)S(1)}, u32[]{:S(2)}, u32[]{:S(2)}) collective-permute-start(f32[128,128]{1,0:T(8,128)S(1)} %get-tuple-element.27), channel_id=1, source_target_pairs={{15,479},{31,495},{47,511},{63,15},{79,31},{95,47},{111,63},{127,7... | collective-permute-start | bytes 196616 | tf_op jit(solution)/shard_map/ppermute | solution.py:592

commit v3 on v2

--- a/solution.py
+++ b/solution.py
@@ -44,31 +44,23 @@
     return lax.axis_index("lat") == lax.axis_size("lat") - 1
 
 
-def edge_rows(refs, start, buffer, ints, sems):
-    copies = []
-    for i, ref in enumerate(refs):
-        target = buffer.at[pl.ds(8 * i, 8), :] if i < FIELDS else ints.at[pl.ds(0, 8), :]
+def fold_rows_kernel(t_ref, s_ref, u_ref, v_ref, m_ref, opp_ref, out, ints, sems):
+    start = t_ref.shape[1] - HALO
+    copies = [pltpu.make_async_copy(opp_ref, ints.at[pl.ds(8, 1), :], sems.at[5])]
+    for i, ref in enumerate((t_ref, s_ref, u_ref, v_ref, m_ref)):
+        target = out.at[pl.ds(8 * i, 8), :] if i < FIELDS else ints.at[pl.ds(0, 8), :]
         copies.append(
             pltpu.make_async_copy(ref.at[0, pl.ds(start, HALO), :], target, sems.at[i])
         )
-    return copies
-
-
-def fold_rows_kernel(t_ref, s_ref, u_ref, v_ref, m_ref, opp_ref, b_ref, ints, sems):
-    height = t_ref.shape[1]
-    start = pl.multiple_of(jnp.where(is_odd(), height - HALO, 0), 8)
-    copies = edge_rows((t_ref, s_ref, u_ref, v_ref, m_ref), start, b_ref, ints, sems)
-    copies.append(pltpu.make_async_copy(opp_ref, ints.at[pl.ds(8, 1), :], sems.at[5]))
     for copy in copies:
         copy.start()
     for copy in copies:
         copy.wait()
-    b_ref[32:40, :] = ints[0:8, :].astype(jnp.float32)
-    b_ref[40:48, :] = jnp.broadcast_to(ints[8:9, :].astype(jnp.float32), (8, LANES))
-
-
-def load_kernel(t_ref, s_ref, u_ref, v_ref, m_ref, b_ref, fields, a_ref, ints, sems):
-    height = t_ref.shape[1]
+    out[32:40, :] = ints[0:8, :].astype(jnp.float32)
+    out[40:48, :] = jnp.broadcast_to(ints[8:9, :].astype(jnp.float32), (8, LANES))
+
+
+def load_kernel(t_ref, s_ref, u_ref, v_ref, m_ref, after, fields, e_ref, w_ref, ints, sems):
     copies = []
     for i, ref in enumerate((t_ref, s_ref, u_ref, v_ref, m_ref)):
         target = fields.at[i] if i < FIELDS else ints
@@ -78,35 +70,48 @@
     for copy in copies:
         copy.wait()
     fields[FIELDS] = ints[...].astype(jnp.float32)
-    odd = is_odd()
-    for i in range(5):
-        a_ref[i * 8 : i * 8 + 8, :] = jnp.where(
-            odd, fields[i, 0:HALO, :], fields[i, height - HALO : height, :]
-        )
-
-
-def halo_tiles(fields, ra_ref, rb_ref, odd, i):
-    ra, rb = ra_ref[i * 8 : i * 8 + 8, :], rb_ref[i * 8 : i * 8 + 8, :]
-    own = [fields[i, 8 * g : 8 * g + 8, :] for g in range(fields.shape[1] // 8)]
-    return [jnp.where(odd, ra, rb)] + own + [jnp.where(odd, rb, ra)]
-
-
-def columns_kernel(fields, sb_ref, ra_ref, rb_ref, e_ref, w_ref):
-    odd = is_odd()
     lane = lane_index()
     for i in range(5):
-        tiles = halo_tiles(fields, ra_ref, rb_ref, odd, i)
         east = jnp.zeros((8, LANES), jnp.float32)
         west = jnp.zeros((8, LANES), jnp.float32)
-        for g, tile in enumerate(tiles):
+        for g in range(fields.shape[1] // 8):
+            tile = fields[i, 8 * g : 8 * g + 8, :]
             here = (lane >= 8 * g) & (lane < 8 * g + 8)
             east = jnp.where(here, roll(tile, 8 * g - (LANES - HALO)), east)
             west = jnp.where(here, roll(tile, 8 * g), west)
         e_ref[i * 8 : i * 8 + 8, :] = east
         w_ref[i * 8 : i * 8 + 8, :] = west
-    for ref in (e_ref, w_ref):
-        ref[40 : 40 + CAP, :] = sb_ref[...]
-        ref[40 + CAP : 40 + 2 * CAP, :] = rb_ref[...]
+
+
+def pair_kernel(e_in, w_in, sb_ref, rb_ref, e_ref, w_ref):
+    for ref, columns in ((e_ref, e_in), (w_ref, w_in)):
+        ref[0:40, :] = columns[...]
+
+        @pl.when(is_top())
+        def _(ref=ref):
+            ref[40 : 40 + CAP, :] = sb_ref[...]
+            ref[40 + CAP : 40 + 2 * CAP, :] = rb_ref[...]
+
+
+def rows_kernel(fields, rw_ref, re_ref, after, a_ref, b_ref):
+    odd = is_odd()
+    lane = lane_index()
+    height = fields.shape[1]
+    north_lanes = height - HALO
+    corners = [jnp.zeros((8, LANES), jnp.float32)] * 2
+    for i in range(5):
+        south, north = fields[i, 0:HALO, :], fields[i, height - HALO : height, :]
+        a_ref[i * 8 : i * 8 + 8, :] = jnp.where(odd, south, north)
+        b_ref[i * 8 : i * 8 + 8, :] = jnp.where(odd, north, south)
+        for ref, at in ((rw_ref, 16 * i), (re_ref, 16 * i + 8)):
+            columns = ref[i * 8 : i * 8 + 8, :]
+            here = (lane >= at) & (lane < at + 8)
+            corners = [
+                jnp.where(here, roll(columns, at - start), corner)
+                for start, corner in zip((0, north_lanes), corners)
+            ]
+    a_ref[40:48, :] = jnp.where(odd, corners[0], corners[1])
+    b_ref[40:48, :] = jnp.where(odd, corners[1], corners[0])
 
 
 def far_places(counts):
@@ -269,6 +274,7 @@
 def main_kernel(
     fields,
     sb_ref,
+    fold_ref,
     ra_ref,
     rb_ref,
     rw_ref,
@@ -292,22 +298,33 @@
     band = 8 * tiles_n
     bands = Band(state, laps, part, stat)
 
+    south_corner = jnp.where(odd, ra_ref[40:48, :], rb_ref[40:48, :])
+    north_corner = jnp.where(odd, rb_ref[40:48, :], ra_ref[40:48, :])
     for i in range(5):
-        tiles = halo_tiles(fields, ra_ref, rb_ref, odd, i)
+        ra, rb = ra_ref[i * 8 : i * 8 + 8, :], rb_ref[i * 8 : i * 8 + 8, :]
         from_w, from_e = rw_ref[i * 8 : i * 8 + 8, :], re_ref[i * 8 : i * 8 + 8, :]
+        tiles = [(jnp.where(odd, ra, rb), south_corner, 16 * i, south_corner, 16 * i + 8)]
+        for g in range(height // 8):
+            tile = fields[i, 8 * g : 8 * g + 8, :]
+            tiles.append((tile, from_w, 8 * g, from_e, 8 * g))
+        tiles.append((jnp.where(odd, rb, ra), north_corner, 16 * i, north_corner, 16 * i + 8))
         ref, at = (state, i) if i < FIELDS else (stat, 0)
-        for g, tile in enumerate(tiles):
+        for g, (tile, west, west_at, east, east_at) in enumerate(tiles):
             ref[at, 8 + 8 * g : 16 + 8 * g, :] = jnp.where(
-                lane < HALO, roll(from_w, -8 * g), roll(tile, HALO)
+                lane < HALO, roll(west, -west_at), roll(tile, HALO)
             )
             ref[at, 8 + band + 8 * g : 16 + band + 8 * g, :] = jnp.where(
-                lane >= LANES - HALO, roll(from_e, LANES - HALO - 8 * g), roll(tile, -HALO)
+                lane >= LANES - HALO, roll(east, LANES - HALO - east_at), roll(tile, -HALO)
             )
     bands.pad()
 
     @pl.when(top)
     def _():
-        pairs = ((rw_ref, 40, rw_ref, 40 + CAP), (sb_ref, 0, rb_ref, 0), (re_ref, 40, re_ref, 40 + CAP))
+        pairs = (
+            (rw_ref, 40, rw_ref, 40 + CAP),
+            (sb_ref, 0, fold_ref, 0),
+            (re_ref, 40, re_ref, 40 + CAP),
+        )
         for i in range(5):
             ghosts = []
             for own, own_at, facing, facing_at in pairs:
@@ -567,14 +584,18 @@
     )
     f32, i32 = jnp.float32, jnp.int32
 
-    def call(kernel, inputs, shapes, scratch=(), far=0, room=32 * 1024, flops=0):
+    def call(kernel, inputs, shapes, scratch=(), far=0, flops=0):
+        inputs = [
+            pltpu.with_memory_space_constraint(x, pltpu.HBM) if i < far else x
+            for i, x in enumerate(inputs)
+        ]
         return pl.pallas_call(
             kernel,
             out_shape=[jax.ShapeDtypeStruct(shape, f32) for shape in shapes],
             in_specs=[anywhere] * far + [vmem] * (len(inputs) - far),
             out_specs=[vmem] * len(shapes),
             scratch_shapes=list(scratch),
-            compiler_params=pltpu.CompilerParams(vmem_limit_bytes=(64 * 1024 - room) * 1024),
+            compiler_params=pltpu.CompilerParams(vmem_limit_bytes=32 * 1024 * 1024),
             cost_estimate=pl.CostEstimate(flops=flops, bytes_accessed=flops, transcendentals=0),
         )(*inputs)
 
@@ -585,46 +606,52 @@
     last = lat_count - 1
     pairs_a = [(place(i, j), place(i, j ^ 1)) for i in lons for j in lats]
     pairs_b = [(place(i, j), place(i, ((j - 1) ^ 1) + 1)) for i in lons for j in lats[1:last]]
-    pairs_b += [(place(i, last), place(-i, last)) for i in lons]
+    pairs_fold = [(place(i, last), place(-i, last)) for i in lons]
 
     def shift(x, by, rows):
         pairs = [(place(i, j), place(i + by, j)) for i in lons for j in rows]
         return lax.ppermute(x, ("lon", "lat"), pairs)
 
-    (send_b,) = call(
+    def along_lat(x, pairs):
+        return lax.ppermute(x, ("lon", "lat"), pairs)
+
+    (top_rows,) = call(
         fold_rows_kernel,
         (*fields, opp.reshape(1, LANES)),
         [(CAP, LANES)],
         [pltpu.VMEM((16, LANES), i32), pltpu.SemaphoreType.DMA((6,))],
         far=6,
-        room=64,
-    )
-    from_b = lax.ppermute(send_b, ("lon", "lat"), pairs_b)
-    stack, send_a = call(
+    )
+    from_fold = along_lat(top_rows, pairs_fold)
+    stack, columns_e, columns_w = call(
         load_kernel,
-        (*fields, send_b),
-        [(5, height, LANES), (CAP, LANES)],
+        (*fields, top_rows),
+        [(5, height, LANES), (40, LANES), (40, LANES)],
         [pltpu.VMEM((height, LANES), i32), pltpu.SemaphoreType.DMA((5,))],
         far=5,
-        room=384,
-    )
-    from_a = lax.ppermute(send_a, ("lon", "lat"), pairs_a)
-    wide = 40 + 2 * CAP
-    send_e, send_w = call(columns_kernel, (stack, send_b, from_a, from_b), [(wide, LANES)] * 2)
+    )
+    send_e, send_w = call(
+        pair_kernel, (columns_e, columns_w, top_rows, from_fold), [(40 + 2 * CAP, LANES)] * 2
+    )
     from_w = shift(send_e, 1, lats)
     from_e = shift(send_w, -1, lats)
     send_far_e, send_far_w = call(
-        far_kernel, (send_b, from_b, from_w, from_e), [(FAR, LANES)] * 2
+        far_kernel, (top_rows, from_fold, from_w, from_e), [(FAR, LANES)] * 2
     )
     far_w = shift(send_far_e, 3, [last])
     far_e = shift(send_far_w, -3, [last])
+    send_a, send_b = call(
+        rows_kernel, (stack, from_w, from_e, send_far_e), [(CAP, LANES)] * 2
+    )
+    from_a = along_lat(send_a, pairs_a)
+    from_b = along_lat(send_b, pairs_b)
 
     def band_scratch(rows):
         return [pltpu.VMEM((n, 16 + 2 * rows, LANES), f32) for n in (FIELDS, FIELDS, FIELDS, 5)]
 
     *outs, upper_state, upper_stat = call(
         main_kernel,
-        (stack, send_b, from_a, from_b, from_w, from_e),
+        (stack, top_rows, from_fold, from_a, from_b, from_w, from_e),
         [t.shape] * 4 + [(FIELDS, 2, UPPER, LANES), (5, 2, UPPER, LANES)],
         band_scratch(height + 2 * HALO),
         flops=10**7,
@@ -647,7 +674,7 @@
             ],
             input_output_aliases={i: i for i in range(4)},
             compiler_params=pltpu.CompilerParams(vmem_limit_bytes=32 * 1024 * 1024),
-        )(*outs, upper_state, upper_stat, send_b, from_b, from_w, from_e, far_w, far_e)
+        )(*outs, upper_state, upper_stat, top_rows, from_fold, from_w, from_e, far_w, far_e)
     )
 
 

time: 55.7 us -> 50.9 us (0.914)
  the two profiles are of different devices: /device:TPU:71 before, /device:TPU:23 now
where the time goes in v3:
time: 50.9 us; the launch traced here: 50.5 us
  starting transfers between devices  36.6 us (72%)
  Pallas kernels  7.66 us (15%)
  waiting for transfers between devices  5.51 us (11%)
  between operations  0.74 us (1%)
    ppermute x3, starting transfers between devices, along_lat(): return lax.ppermute(x, ('lon', 'lat'), pairs)  30 us
    pallas_call x6, Pallas kernels, call(): pl.pallas_call(kernel, out_shape=[jax.ShapeDtypeStruct(shape, f32) for sh...  7.61 us
    ppermute x4, starting transfers between devices, shift(): return lax.ppermute(x, ('lon', 'lat'), pairs)  6.6 us
    ppermute x4, waiting for transfers between devices, shift(): return lax.ppermute(x, ('lon', 'lat'), pairs)  4.02 us
    ppermute x3, waiting for transfers between devices, along_lat(): return lax.ppermute(x, ('lon', 'lat'), pairs)  1.49 us
  transfers between devices with their start and end apart: 7, of which 2 were waited for; matrix products, arithmetic and copies ran while one was open for 0% of the time, Pallas kernels for 13%

profile of v3, /device:TPU:23, one launch (start us, length us, event | category | flops | bytes accessed | tf_op | source)
XLA Modules:
  0.0 50.5 jit_solution(316995122707490447)
XLA Ops:
  0.6 0.8 %shard_map.93.after.sb_ref = f32[48,128]{1,0:T(8,128)S(1)} custom-call(f32[1,96,128]{2,1,0:T(8,128)} %t_ref.3, f32[1,96,128]{2,1,0:T(8,128)} %s_ref.3, f32[1,96,128]{2,1,0:T(8,128)} %u_ref.3, f32[1,96,128]{2,1,0:T(8,128)} %v_ref.3, s32[1,96,128]{2,1,0:T(8,128)} %m_ref.3, s32[1,128]{1,0:T(1,128)} %bitcast.1), custom_call_target="tpu_custom_call" | custom-call | tf_op jit(solution)/shard_map/pallas_call | solution.py:592
  1.5 0.7 %collective-permute-start = (f32[48,128]{1,0:T(8,128)S(1)}, f32[48,128]{1,0:T(8,128)S(1)}, u32[]{:S(2)}, u32[]{:S(2)}) collective-permute-start(f32[48,128]{1,0:T(8,128)S(1)} %shard_map.93.after.sb_ref), channel_id=1, source_target_pairs={{15,15},{31,511},{47,495},{63,479},{79,463},{95,447},{111,431},{12... | collective-permute-start | bytes 73736 | tf_op jit(solution)/shard_map/ppermute | solution.py:616
  2.1 1.1 %shard_map.94 = (f32[5,96,128]{2,1,0:T(8,128)S(1)}, f32[40,128]{1,0:T(8,128)S(1)}, f32[40,128]{1,0:T(8,128)S(1)}) custom-call(f32[1,96,128]{2,1,0:T(8,128)} %t_ref.3, f32[1,96,128]{2,1,0:T(8,128)} %s_ref.3, f32[1,96,128]{2,1,0:T(8,128)} %u_ref.3, f32[1,96,128]{2,1,0:T(8,128)} %v_ref.3, s32[1,96,128]{2,1,0:T(8,128)} %m_ref.3, ...), custom_call_target="tpu_custom_call" | custom-call | tf_op jit(solution)/shard_map/pallas_call | solution.py:592
  3.3 0.0 collective-permute-done.rb_ref.fold_ref
  3.3 3.2 %collective-permute-start.1 = (f32[136,128]{1,0:T(8,128)S(1)}, f32[136,128]{1,0:T(8,128)S(1)}, u32[]{:S(2)}, u32[]{:S(2)}) collective-permute-start(f32[136,128]{1,0:T(8,128)S(1)} %get-tuple-element.22), channel_id=1, source_target_pairs={{0,16},{1,17},{2,18},{3,19},{4,20},{5,21},{6,22},{7,23},{8,24},{9,... | collective-permute-start | bytes 208904 | tf_op jit(solution)/shard_map/ppermute | solution.py:613
  6.5 2.1 %collective-permute-start.2 = (f32[136,128]{1,0:T(8,128)S(1)}, f32[136,128]{1,0:T(8,128)S(1)}, u32[]{:S(2)}, u32[]{:S(2)}) collective-permute-start(f32[136,128]{1,0:T(8,128)S(1)} %get-tuple-element.23), channel_id=1, source_target_pairs={{0,496},{1,497},{2,498},{3,499},{4,500},{5,501},{6,502},{7,503},{8... | collective-permute-start | bytes 208904 | tf_op jit(solution)/shard_map/ppermute | solution.py:613
  8.6 0.0 collective-permute-done.1.rw_ref
  8.6 4.0 %collective-permute-done.2.re_ref = f32[136,128]{1,0:T(8,128)S(1)} collective-permute-done((f32[136,128]{1,0:T(8,128)S(1)}, f32[136,128]{1,0:T(8,128)S(1)}, u32[]{:S(2)}, u32[]{:S(2)}) %collective-permute-start.2) | collective-permute-done | bytes 69664 | tf_op jit(solution)/shard_map/ppermute | solution.py:613
  12.6 0.7 %collective-permute-start.6 = (f32[128,128]{1,0:T(8,128)S(1)}, f32[128,128]{1,0:T(8,128)S(1)}, u32[]{:S(2)}, u32[]{:S(2)}) collective-permute-start(f32[128,128]{1,0:T(8,128)S(1)} %get-tuple-element.33), channel_id=1, source_target_pairs={{15,479},{31,495},{47,511},{63,15},{79,31},{95,47},{111,63},{127,7... | collective-permute-start | bytes 196616 | tf_op jit(solution)/shard_map/ppermute | solution.py:613
  13.3 0.7 %collective-permute-start.5 = (f32[128,128]{1,0:T(8,128)S(1)}, f32[128,128]{1,0:T(8,128)S(1)}, u32[]{:S(2)}, u32[]{:S(2)}) collective-permute-start(f32[128,128]{1,0:T(8,128)S(1)} %get-tuple-element.24.after), channel_id=1, source_target_pairs={{15,63},{31,79},{47,95},{63,111},{79,127},{95,143},{111,159},{127,... | collective-permute-start | bytes 196616 | tf_op jit(solution)/shard_map/ppermute | solution.py:613
  14.0 0.1 shard_map.97
  14.1 3.7 %collective-permute-start.3 = (f32[48,128]{1,0:T(8,128)S(1)}, f32[48,128]{1,0:T(8,128)S(1)}, u32[]{:S(2)}, u32[]{:S(2)}) collective-permute-start(f32[48,128]{1,0:T(8,128)S(1)} %get-tuple-element.25), channel_id=1, source_target_pairs={{0,1},{1,0},{2,3},{3,2},{4,5},{5,4},{6,7},{7,6},{8,9},{9,8},{10,11... | collective-permute-start | bytes 73736 | tf_op jit(solution)/shard_map/ppermute | solution.py:616
  17.8 25.6 %collective-permute-start.4 = (f32[48,128]{1,0:T(8,128)S(1)}, f32[48,128]{1,0:T(8,128)S(1)}, u32[]{:S(2)}, u32[]{:S(2)}) collective-permute-start(f32[48,128]{1,0:T(8,128)S(1)} %get-tuple-element.26), channel_id=1, source_target_pairs={{1,2},{2,1},{3,4},{4,3},{5,6},{6,5},{7,8},{8,7},{9,10},{10,9},{11,... | collective-permute-start | bytes 73736 | tf_op jit(solution)/shard_map/ppermute | solution.py:616
  43.4 0.0 collective-permute-done.3.ra_ref
  43.5 1.5 %collective-permute-done.4.rb_ref = f32[48,128]{1,0:T(8,128)S(1)} collective-permute-done((f32[48,128]{1,0:T(8,128)S(1)}, f32[48,128]{1,0:T(8,128)S(1)}, u32[]{:S(2)}, u32[]{:S(2)}) %collective-permute-start.4) | collective-permute-done | bytes 24608 | tf_op jit(solution)/shard_map/ppermute | solution.py:616
  44.9 5.5 %shard_map.98 = (f32[1,96,128]{2,1,0:T(8,128)}, f32[1,96,128]{2,1,0:T(8,128)}, f32[1,96,128]{2,1,0:T(8,128)}, f32[1,96,128]{2,1,0:T(8,128)}, f32[4,2,24,128]{3,2...) custom-call(f32[5,96,128]{2,1,0:T(8,128)S(1)} %get-tuple-element.19.fields, f32[48,128]{1,0:T(8,128)S(1)} %shard_map.93.after.sb_ref, ...), custom_call_target="tpu_custom_call" | custom-call | flops 10000000 | bytes 10000000 | tf_op jit(solution)/shard_map/pallas_call | solution.py:592
  50.5 0.0 collective-permute-done.6.e3_ref
  50.5 0.0 collective-permute-done.5.w3_ref
  (3 shorter events, 0.1 us)
Async XLA Ops:
  1.5 1.8 %collective-permute-start = (f32[48,128]{1,0:T(8,128)S(1)}, f32[48,128]{1,0:T(8,128)S(1)}, u32[]{:S(2)}, u32[]{:S(2)}) collective-permute-start(f32[48,128]{1,0:T(8,128)S(1)} %shard_map.93.after.sb_ref), channel_id=1, source_target_pairs={{15,15},{31,511},{47,495},{63,479},{79,463},{95,447},{111,431},{12... | collective-permute-start | bytes 73736 | tf_op jit(solution)/shard_map/ppermute | solution.py:616
  3.3 5.3 %collective-permute-start.1 = (f32[136,128]{1,0:T(8,128)S(1)}, f32[136,128]{1,0:T(8,128)S(1)}, u32[]{:S(2)}, u32[]{:S(2)}) collective-permute-start(f32[136,128]{1,0:T(8,128)S(1)} %get-tuple-element.22), channel_id=1, source_target_pairs={{0,16},{1,17},{2,18},{3,19},{4,20},{5,21},{6,22},{7,23},{8,24},{9,... | collective-permute-start | bytes 208904 | tf_op jit(solution)/shard_map/ppermute | solution.py:613
  6.5 6.1 %collective-permute-start.2 = (f32[136,128]{1,0:T(8,128)S(1)}, f32[136,128]{1,0:T(8,128)S(1)}, u32[]{:S(2)}, u32[]{:S(2)}) collective-permute-start(f32[136,128]{1,0:T(8,128)S(1)} %get-tuple-element.23), channel_id=1, source_target_pairs={{0,496},{1,497},{2,498},{3,499},{4,500},{5,501},{6,502},{7,503},{8... | collective-permute-start | bytes 208904 | tf_op jit(solution)/shard_map/ppermute | solution.py:613
  12.6 37.9 %collective-permute-start.6 = (f32[128,128]{1,0:T(8,128)S(1)}, f32[128,128]{1,0:T(8,128)S(1)}, u32[]{:S(2)}, u32[]{:S(2)}) collective-permute-start(f32[128,128]{1,0:T(8,128)S(1)} %get-tuple-element.33), channel_id=1, source_target_pairs={{15,479},{31,495},{47,511},{63,15},{79,31},{95,47},{111,63},{127,7... | collective-permute-start | bytes 196616 | tf_op jit(solution)/shard_map/ppermute | solution.py:613
  13.3 37.2 %collective-permute-start.5 = (f32[128,128]{1,0:T(8,128)S(1)}, f32[128,128]{1,0:T(8,128)S(1)}, u32[]{:S(2)}, u32[]{:S(2)}) collective-permute-start(f32[128,128]{1,0:T(8,128)S(1)} %get-tuple-element.24.after), channel_id=1, source_target_pairs={{15,63},{31,79},{47,95},{63,111},{79,127},{95,143},{111,159},{127,... | collective-permute-start | bytes 196616 | tf_op jit(solution)/shard_map/ppermute | solution.py:613
  14.1 29.4 %collective-permute-start.3 = (f32[48,128]{1,0:T(8,128)S(1)}, f32[48,128]{1,0:T(8,128)S(1)}, u32[]{:S(2)}, u32[]{:S(2)}) collective-permute-start(f32[48,128]{1,0:T(8,128)S(1)} %get-tuple-element.25), channel_id=1, source_target_pairs={{0,1},{1,0},{2,3},{3,2},{4,5},{5,4},{6,7},{7,6},{8,9},{9,8},{10,11... | collective-permute-start | bytes 73736 | tf_op jit(solution)/shard_map/ppermute | solution.py:616
  17.8 27.1 %collective-permute-start.4 = (f32[48,128]{1,0:T(8,128)S(1)}, f32[48,128]{1,0:T(8,128)S(1)}, u32[]{:S(2)}, u32[]{:S(2)}) collective-permute-start(f32[48,128]{1,0:T(8,128)S(1)} %get-tuple-element.26), channel_id=1, source_target_pairs={{1,2},{2,1},{3,4},{4,3},{5,6},{6,5},{7,8},{8,7},{9,10},{10,9},{11,... | collective-permute-start | bytes 73736 | tf_op jit(solution)/shard_map/ppermute | solution.py:616

commit v4 on v2

--- a/solution.py
+++ b/solution.py
@@ -44,31 +44,43 @@
     return lax.axis_index("lat") == lax.axis_size("lat") - 1
 
 
-def edge_rows(refs, start, buffer, ints, sems):
-    copies = []
-    for i, ref in enumerate(refs):
-        target = buffer.at[pl.ds(8 * i, 8), :] if i < FIELDS else ints.at[pl.ds(0, 8), :]
+def is_odd_lon():
+    return lax.rem(lax.axis_index("lon"), 2) == 1
+
+
+class Either:
+    def __init__(self, flag, yes, no):
+        self.flag, self.yes, self.no = flag, yes, no
+
+    def __getitem__(self, index):
+        return jnp.where(self.flag, self.yes[index], self.no[index])
+
+
+def first_rows_kernel(t_ref, s_ref, u_ref, v_ref, m_ref, opp_ref, out, ints, sems):
+    start = pl.multiple_of(jnp.where(is_odd(), t_ref.shape[1] - HALO, 0), 8)
+    copies = [pltpu.make_async_copy(opp_ref, ints.at[pl.ds(8, 1), :], sems.at[5])]
+    for i, ref in enumerate((t_ref, s_ref, u_ref, v_ref, m_ref)):
+        target = out.at[pl.ds(8 * i, 8), :] if i < FIELDS else ints.at[pl.ds(0, 8), :]
         copies.append(
             pltpu.make_async_copy(ref.at[0, pl.ds(start, HALO), :], target, sems.at[i])
         )
-    return copies
-
-
-def fold_rows_kernel(t_ref, s_ref, u_ref, v_ref, m_ref, opp_ref, b_ref, ints, sems):
-    height = t_ref.shape[1]
-    start = pl.multiple_of(jnp.where(is_odd(), height - HALO, 0), 8)
-    copies = edge_rows((t_ref, s_ref, u_ref, v_ref, m_ref), start, b_ref, ints, sems)
-    copies.append(pltpu.make_async_copy(opp_ref, ints.at[pl.ds(8, 1), :], sems.at[5]))
     for copy in copies:
         copy.start()
     for copy in copies:
         copy.wait()
-    b_ref[32:40, :] = ints[0:8, :].astype(jnp.float32)
-    b_ref[40:48, :] = jnp.broadcast_to(ints[8:9, :].astype(jnp.float32), (8, LANES))
-
-
-def load_kernel(t_ref, s_ref, u_ref, v_ref, m_ref, b_ref, fields, a_ref, ints, sems):
-    height = t_ref.shape[1]
+    out[32:40, :] = ints[0:8, :].astype(jnp.float32)
+    out[40:48, :] = jnp.broadcast_to(ints[8:9, :].astype(jnp.float32), (8, LANES))
+
+
+def add_columns(e, w, tile, g):
+    lane = lane_index()
+    here = (lane >= 8 * g) & (lane < 8 * g + 8)
+    e = jnp.where(here, roll(tile, 8 * g - (LANES - HALO)), e)
+    return e, jnp.where(here, roll(tile, 8 * g), w)
+
+
+def load_kernel(t_ref, s_ref, u_ref, v_ref, m_ref, after, fields, a_ref, e_ref, w_ref, ints, sems):
+    height = fields.shape[1]
     copies = []
     for i, ref in enumerate((t_ref, s_ref, u_ref, v_ref, m_ref)):
         target = fields.at[i] if i < FIELDS else ints
@@ -80,33 +92,29 @@
     fields[FIELDS] = ints[...].astype(jnp.float32)
     odd = is_odd()
     for i in range(5):
-        a_ref[i * 8 : i * 8 + 8, :] = jnp.where(
-            odd, fields[i, 0:HALO, :], fields[i, height - HALO : height, :]
-        )
-
-
-def halo_tiles(fields, ra_ref, rb_ref, odd, i):
-    ra, rb = ra_ref[i * 8 : i * 8 + 8, :], rb_ref[i * 8 : i * 8 + 8, :]
-    own = [fields[i, 8 * g : 8 * g + 8, :] for g in range(fields.shape[1] // 8)]
-    return [jnp.where(odd, ra, rb)] + own + [jnp.where(odd, rb, ra)]
-
-
-def columns_kernel(fields, sb_ref, ra_ref, rb_ref, e_ref, w_ref):
+        south, north = fields[i, 0:HALO, :], fields[i, height - HALO : height, :]
+        a_ref[i * 8 : i * 8 + 8, :] = jnp.where(odd, south, north)
+        e = w = jnp.zeros((8, LANES), jnp.float32)
+        for g in range(height // 8):
+            e, w = add_columns(e, w, fields[i, 8 * g : 8 * g + 8, :], g + 1)
+        e_ref[i * 8 : i * 8 + 8, :] = e
+        w_ref[i * 8 : i * 8 + 8, :] = w
+
+
+def pair_kernel(height, e_in, w_in, sb_ref, ra_ref, rb_ref, e_ref, w_ref):
     odd = is_odd()
-    lane = lane_index()
     for i in range(5):
-        tiles = halo_tiles(fields, ra_ref, rb_ref, odd, i)
-        east = jnp.zeros((8, LANES), jnp.float32)
-        west = jnp.zeros((8, LANES), jnp.float32)
-        for g, tile in enumerate(tiles):
-            here = (lane >= 8 * g) & (lane < 8 * g + 8)
-            east = jnp.where(here, roll(tile, 8 * g - (LANES - HALO)), east)
-            west = jnp.where(here, roll(tile, 8 * g), west)
-        e_ref[i * 8 : i * 8 + 8, :] = east
-        w_ref[i * 8 : i * 8 + 8, :] = west
-    for ref in (e_ref, w_ref):
-        ref[40 : 40 + CAP, :] = sb_ref[...]
-        ref[40 + CAP : 40 + 2 * CAP, :] = rb_ref[...]
+        at = slice(i * 8, i * 8 + 8)
+        ra, rb = ra_ref[at, :], rb_ref[at, :]
+        e, w = add_columns(e_in[at, :], w_in[at, :], jnp.where(odd, ra, rb), 0)
+        e, w = add_columns(e, w, jnp.where(odd, rb, ra), height // 8 + 1)
+        e_ref[at, :], w_ref[at, :] = e, w
+
+    @pl.when(is_top())
+    def _():
+        for ref in (e_ref, w_ref):
+            ref[40 : 40 + CAP, :] = sb_ref[...]
+            ref[40 + CAP : 40 + 2 * CAP, :] = rb_ref[...]
 
 
 def far_places(counts):
@@ -117,15 +125,17 @@
             base += 5 * n + 1
 
 
-def far_kernel(sb_ref, rb_ref, rw_ref, re_ref, e_ref, w_ref):
+def far_kernel(sb_ref, rb_ref, rw_ref, re_ref, first, second):
     @pl.when(is_top())
     def _():
+        far_flag = jnp.logical_not(is_odd_lon())
         sources = (
             ((rw_ref, 40), (rw_ref, 40 + CAP)),
             ((sb_ref, 0), (rb_ref, 0)),
             ((re_ref, 40), (re_ref, 40 + CAP)),
         )
-        for out, counts in ((e_ref, FAR_ROWS), (w_ref, FAR_ROWS[::-1])):
+
+        def fill(out, counts):
             for j, side, n, base in far_places(counts):
                 ref, at = sources[j][side]
                 for i in range(5):
@@ -134,6 +144,16 @@
                     ]
                 out[base + 5 * n : base + 5 * n + 1, :] = ref[at + 40 : at + 41, :]
             out[FAR - 2 : FAR, :] = jnp.zeros((2, LANES), jnp.float32)
+
+        @pl.when(far_flag)
+        def _():
+            fill(first, FAR_ROWS)
+            fill(second, FAR_ROWS[::-1])
+
+        @pl.when(jnp.logical_not(far_flag))
+        def _():
+            fill(first, FAR_ROWS[::-1])
+            fill(second, FAR_ROWS)
 
 
 def first_pass(centre, north, south, east, west, sea, count, w_e, w_n, w_s, turn, roll_w):
@@ -293,8 +313,11 @@
     bands = Band(state, laps, part, stat)
 
     for i in range(5):
-        tiles = halo_tiles(fields, ra_ref, rb_ref, odd, i)
-        from_w, from_e = rw_ref[i * 8 : i * 8 + 8, :], re_ref[i * 8 : i * 8 + 8, :]
+        at = slice(i * 8, i * 8 + 8)
+        ra, rb, from_w, from_e = ra_ref[at, :], rb_ref[at, :], rw_ref[at, :], re_ref[at, :]
+        tiles = [jnp.where(odd, ra, rb)]
+        tiles += [fields[i, 8 * g : 8 * g + 8, :] for g in range(height // 8)]
+        tiles += [jnp.where(odd, rb, ra)]
         ref, at = (state, i) if i < FIELDS else (stat, 0)
         for g, tile in enumerate(tiles):
             ref[at, 8 + 8 * g : 16 + 8 * g, :] = jnp.where(
@@ -307,7 +330,11 @@
 
     @pl.when(top)
     def _():
-        pairs = ((rw_ref, 40, rw_ref, 40 + CAP), (sb_ref, 0, rb_ref, 0), (re_ref, 40, re_ref, 40 + CAP))
+        pairs = (
+            (rw_ref, 40, rw_ref, 40 + CAP),
+            (sb_ref, 0, rb_ref, 0),
+            (re_ref, 40, re_ref, 40 + CAP),
+        )
         for i in range(5):
             ghosts = []
             for own, own_at, facing, facing_at in pairs:
@@ -379,8 +406,8 @@
     rb_ref,
     rw_ref,
     re_ref,
-    w3_ref,
-    e3_ref,
+    first_far,
+    second_far,
     t_out,
     s_out,
     u_out,
@@ -397,6 +424,9 @@
     rows_out,
     sems,
 ):
+    far_flag = jnp.logical_not(is_odd_lon())
+    w3_ref = Either(far_flag, second_far, first_far)
+    e3_ref = Either(far_flag, first_far, second_far)
     lane = lane_index()
     height = t_out.shape[1]
     total_rows = height * lax.axis_size("lat")
@@ -567,14 +597,18 @@
     )
     f32, i32 = jnp.float32, jnp.int32
 
-    def call(kernel, inputs, shapes, scratch=(), far=0, room=32 * 1024, flops=0):
+    def call(kernel, inputs, shapes, scratch=(), far=0, flops=0):
+        inputs = [
+            pltpu.with_memory_space_constraint(x, pltpu.HBM) if i < far else x
+            for i, x in enumerate(inputs)
+        ]
         return pl.pallas_call(
             kernel,
             out_shape=[jax.ShapeDtypeStruct(shape, f32) for shape in shapes],
             in_specs=[anywhere] * far + [vmem] * (len(inputs) - far),
             out_specs=[vmem] * len(shapes),
             scratch_shapes=list(scratch),
-            compiler_params=pltpu.CompilerParams(vmem_limit_bytes=(64 * 1024 - room) * 1024),
+            compiler_params=pltpu.CompilerParams(vmem_limit_bytes=32 * 1024 * 1024),
             cost_estimate=pl.CostEstimate(flops=flops, bytes_accessed=flops, transcendentals=0),
         )(*inputs)
 
@@ -587,37 +621,47 @@
     pairs_b = [(place(i, j), place(i, ((j - 1) ^ 1) + 1)) for i in lons for j in lats[1:last]]
     pairs_b += [(place(i, last), place(-i, last)) for i in lons]
 
-    def shift(x, by, rows):
-        pairs = [(place(i, j), place(i + by, j)) for i in lons for j in rows]
+    def swap(x, by, rest, rows):
+        pairs = []
+        for i in lons:
+            other = i + by if i % 2 == rest else i - by
+            pairs += [(place(i, j), place(other, j)) for j in rows]
+        return exchange(x, pairs)
+
+    def shift(x, by):
+        return exchange(x, [(place(i, j), place(i + by, j)) for i in lons for j in lats])
+
+    def exchange(x, pairs):
         return lax.ppermute(x, ("lon", "lat"), pairs)
 
     (send_b,) = call(
-        fold_rows_kernel,
+        first_rows_kernel,
         (*fields, opp.reshape(1, LANES)),
         [(CAP, LANES)],
         [pltpu.VMEM((16, LANES), i32), pltpu.SemaphoreType.DMA((6,))],
         far=6,
-        room=64,
-    )
-    from_b = lax.ppermute(send_b, ("lon", "lat"), pairs_b)
-    stack, send_a = call(
+    )
+    from_b = exchange(send_b, pairs_b)
+    stack, send_a, columns_e, columns_w = call(
         load_kernel,
         (*fields, send_b),
-        [(5, height, LANES), (CAP, LANES)],
+        [(5, height, LANES), (40, LANES), (40, LANES), (40, LANES)],
         [pltpu.VMEM((height, LANES), i32), pltpu.SemaphoreType.DMA((5,))],
         far=5,
-        room=384,
-    )
-    from_a = lax.ppermute(send_a, ("lon", "lat"), pairs_a)
-    wide = 40 + 2 * CAP
-    send_e, send_w = call(columns_kernel, (stack, send_b, from_a, from_b), [(wide, LANES)] * 2)
-    from_w = shift(send_e, 1, lats)
-    from_e = shift(send_w, -1, lats)
-    send_far_e, send_far_w = call(
+    )
+    from_a = exchange(send_a, pairs_a)
+    send_e, send_w = call(
+        functools.partial(pair_kernel, height),
+        (columns_e, columns_w, send_b, from_a, from_b),
+        [(40 + 2 * CAP, LANES)] * 2,
+    )
+    from_w = shift(send_e, 1)
+    from_e = shift(send_w, -1)
+    far_send_1, far_send_2 = call(
         far_kernel, (send_b, from_b, from_w, from_e), [(FAR, LANES)] * 2
     )
-    far_w = shift(send_far_e, 3, [last])
-    far_e = shift(send_far_w, -3, [last])
+    far_1 = swap(far_send_1, 3, 0, [last])
+    far_2 = swap(far_send_2, 3, 1, [last])
 
     def band_scratch(rows):
         return [pltpu.VMEM((n, 16 + 2 * rows, LANES), f32) for n in (FIELDS, FIELDS, FIELDS, 5)]
@@ -647,7 +691,7 @@
             ],
             input_output_aliases={i: i for i in range(4)},
             compiler_params=pltpu.CompilerParams(vmem_limit_bytes=32 * 1024 * 1024),
-        )(*outs, upper_state, upper_stat, send_b, from_b, from_w, from_e, far_w, far_e)
+        )(*outs, upper_state, upper_stat, send_b, from_b, from_w, from_e, far_1, far_2)
     )
 
 

time: 55.7 us -> 47.2 us (0.85)
  starting transfers between devices: 38 us -> 31.7 us
  Pallas kernels: 13.9 us -> 11.8 us
  local copies, waits for them, and re-layouts: 0.95 us -> 0 us
  waiting for transfers between devices: 1.71 us -> 2.58 us
    ppermute x6, starting transfers between devices: 38 us -> 31.7 us  [exchange(): return lax.ppermute(x, ('lon', 'lat'), pairs)]
    pallas_call x5, Pallas kernels: 9.83 us -> 7.8 us  [call(): pl.pallas_call(kernel, out_shape=[jax.ShapeDtypeStruct(shape, f32) for sh...]
    unnamed x6 -> x0, local copies, waits for them, and re-layouts: 0.95 us -> none
    ppermute x6, waiting for transfers between devices: 1.71 us -> 2.58 us  [exchange(): return lax.ppermute(x, ('lon', 'lat'), pairs)]
  transfers between devices with their start and end apart: 6 -> 6, of which waited for: 2 -> 2; matrix products, arithmetic and copies ran while one was open for 0% -> 0% of each run, Pallas kernels for 10% -> 15%
where the time goes in v4:
time: 47.2 us; the launch traced here: 46.8 us
  starting transfers between devices  31.7 us (67%)
  Pallas kernels  11.8 us (25%)
  waiting for transfers between devices  2.58 us (5%)
  between operations  0.71 us (2%)
    ppermute x6, starting transfers between devices, exchange(): return lax.ppermute(x, ('lon', 'lat'), pairs)  31.7 us
    pallas_call x5, Pallas kernels, call(): pl.pallas_call(kernel, out_shape=[jax.ShapeDtypeStruct(shape, f32) for sh...  7.8 us
    pallas_call x1, Pallas kernels, body(): pl.pallas_call(cap_kernel, out_shape=[jax.ShapeDtypeStruct(t.shape, f32)]...  4.03 us
    ppermute x6, waiting for transfers between devices, exchange(): return lax.ppermute(x, ('lon', 'lat'), pairs)  2.58 us
  transfers between devices with their start and end apart: 6, of which 2 were waited for; matrix products, arithmetic and copies ran while one was open for 0% of the time, Pallas kernels for 15%

profile of v4, /device:TPU:71, one launch (start us, length us, event | category | flops | bytes accessed | tf_op | source)
XLA Modules:
  0.0 46.8 jit_solution(5238716182884884959)
XLA Ops:
  0.6 0.8 %shard_map.93.after.sb_ref = f32[48,128]{1,0:T(8,128)S(1)} custom-call(f32[1,96,128]{2,1,0:T(8,128)} %t_ref.3, f32[1,96,128]{2,1,0:T(8,128)} %s_ref.3, f32[1,96,128]{2,1,0:T(8,128)} %u_ref.3, f32[1,96,128]{2,1,0:T(8,128)} %v_ref.3, s32[1,96,128]{2,1,0:T(8,128)} %m_ref.3, s32[1,128]{1,0:T(1,128)} %bitcast.1), custom_call_target="tpu_custom_call" | custom-call | tf_op jit(solution)/shard_map/pallas_call | solution.py:605
  1.5 0.7 %collective-permute-start.1 = (f32[48,128]{1,0:T(8,128)S(1)}, f32[48,128]{1,0:T(8,128)S(1)}, u32[]{:S(2)}, u32[]{:S(2)}) collective-permute-start(f32[48,128]{1,0:T(8,128)S(1)} %shard_map.93.after.sb_ref), channel_id=1, source_target_pairs={{1,2},{2,1},{3,4},{4,3},{5,6},{6,5},{7,8},{8,7},{9,10},{10,9},{11,... | collective-permute-start | bytes 73736 | tf_op jit(solution)/shard_map/ppermute | solution.py:635
  2.1 1.1 %shard_map.94 = (f32[5,96,128]{2,1,0:T(8,128)S(1)}, f32[40,128]{1,0:T(8,128)S(1)}, f32[40,128]{1,0:T(8,128)S(1)}, f32[40,128]{1,0:T(8,128)S(1)}) custom-call(f32[1,96,128]{2,1,0:T(8,128)} %t_ref.3, f32[1,96,128]{2,1,0:T(8,128)} %s_ref.3, f32[1,96,128]{2,1,0:T(8,128)} %u_ref.3, f32[1,96,128]{2,1,0:T(8,128)} %v_ref.3, s32[1,96,128]{2,1,0:T(8,128)} %m_ref.3, ...), custom_call_target="tpu_custom_call" | custom-call | tf_op jit(solution)/shard_map/pallas_call | solution.py:605
  3.3 3.8 %collective-permute-start = (f32[40,128]{1,0:T(8,128)S(1)}, f32[40,128]{1,0:T(8,128)S(1)}, u32[]{:S(2)}, u32[]{:S(2)}) collective-permute-start(f32[40,128]{1,0:T(8,128)S(1)} %get-tuple-element.19), channel_id=1, source_target_pairs={{0,1},{1,0},{2,3},{3,2},{4,5},{5,4},{6,7},{7,6},{8,9},{9,8},{10,11... | collective-permute-start | bytes 61448 | tf_op jit(solution)/shard_map/ppermute | solution.py:635
  7.1 0.8 %collective-permute-done.ra_ref = f32[40,128]{1,0:T(8,128)S(1)} collective-permute-done((f32[40,128]{1,0:T(8,128)S(1)}, f32[40,128]{1,0:T(8,128)S(1)}, u32[]{:S(2)}, u32[]{:S(2)}) %collective-permute-start) | collective-permute-done | bytes 20512 | tf_op jit(solution)/shard_map/ppermute | solution.py:635
  8.0 0.0 collective-permute-done.1.rb_ref
  8.0 0.1 shard_map.95
  8.0 13.5 %collective-permute-start.2 = (f32[136,128]{1,0:T(8,128)S(1)}, f32[136,128]{1,0:T(8,128)S(1)}, u32[]{:S(2)}, u32[]{:S(2)}) collective-permute-start(f32[136,128]{1,0:T(8,128)S(1)} %get-tuple-element.22), channel_id=1, source_target_pairs={{0,16},{1,17},{2,18},{3,19},{4,20},{5,21},{6,22},{7,23},{8,24},{9,... | collective-permute-start | bytes 208904 | tf_op jit(solution)/shard_map/ppermute | solution.py:635
  21.6 4.3 %collective-permute-start.3 = (f32[136,128]{1,0:T(8,128)S(1)}, f32[136,128]{1,0:T(8,128)S(1)}, u32[]{:S(2)}, u32[]{:S(2)}) collective-permute-start(f32[136,128]{1,0:T(8,128)S(1)} %get-tuple-element.23), channel_id=1, source_target_pairs={{0,496},{1,497},{2,498},{3,499},{4,500},{5,501},{6,502},{7,503},{8... | collective-permute-start | bytes 208904 | tf_op jit(solution)/shard_map/ppermute | solution.py:635
  25.8 0.0 collective-permute-done.2.rw_ref
  25.9 1.7 %collective-permute-done.3.re_ref = f32[136,128]{1,0:T(8,128)S(1)} collective-permute-done((f32[136,128]{1,0:T(8,128)S(1)}, f32[136,128]{1,0:T(8,128)S(1)}, u32[]{:S(2)}, u32[]{:S(2)}) %collective-permute-start.3) | collective-permute-done | bytes 69664 | tf_op jit(solution)/shard_map/ppermute | solution.py:635
  27.6 3.9 %collective-permute-start.4 = (f32[128,128]{1,0:T(8,128)S(1)}, f32[128,128]{1,0:T(8,128)S(1)}, u32[]{:S(2)}, u32[]{:S(2)}) collective-permute-start(f32[128,128]{1,0:T(8,128)S(1)} %get-tuple-element.30), channel_id=1, source_target_pairs={{15,63},{31,495},{47,95},{63,15},{79,127},{95,47},{111,159},{127,7... | collective-permute-start | bytes 196616 | tf_op jit(solution)/shard_map/ppermute | solution.py:635
  31.5 5.5 %collective-permute-start.5 = (f32[128,128]{1,0:T(8,128)S(1)}, f32[128,128]{1,0:T(8,128)S(1)}, u32[]{:S(2)}, u32[]{:S(2)}) collective-permute-start(f32[128,128]{1,0:T(8,128)S(1)} %get-tuple-element.31), channel_id=1, source_target_pairs={{15,479},{31,79},{47,511},{63,111},{79,31},{95,143},{111,63},{127,... | collective-permute-start | bytes 196616 | tf_op jit(solution)/shard_map/ppermute | solution.py:635
  37.1 5.7 %shard_map.96 = (f32[1,96,128]{2,1,0:T(8,128)}, f32[1,96,128]{2,1,0:T(8,128)}, f32[1,96,128]{2,1,0:T(8,128)}, f32[1,96,128]{2,1,0:T(8,128)}, f32[4,2,24,128]{3,2...) custom-call(f32[5,96,128]{2,1,0:T(8,128)S(1)} %get-tuple-element.18.fields, f32[48,128]{1,0:T(8,128)S(1)} %shard_map.93.after.sb_ref, ...), custom_call_target="tpu_custom_call" | custom-call | flops 10000000 | bytes 10000000 | tf_op jit(solution)/shard_map/pallas_call | solution.py:605
  42.8 0.0 collective-permute-done.4.first_far
  42.8 0.0 collective-permute-done.5.second_far
  42.8 4.0 %shard_map.98 = (f32[1,96,128]{2,1,0:T(8,128)}, f32[1,96,128]{2,1,0:T(8,128)}, f32[1,96,128]{2,1,0:T(8,128)}, f32[1,96,128]{2,1,0:T(8,128)}) custom-call(f32[1,96,128]{2,1,0:T(8,128)} %get-tuple-element.24.t_in, f32[1,96,128]{2,1,0:T(8,128)} %get-tuple-element.25.s_in, ...), custom_call_target="tpu_custom_call", output_to_operand_aliasing={{0}: (0, {}), {1}: (1, {}), {2}: (2, {}), {3}: (3, {})} | custom-call | tf_op jit(solution)/shard_map/pallas_call | solution.py:677
  (1 shorter events, 0.0 us)
Async XLA Ops:
  1.5 6.5 %collective-permute-start.1 = (f32[48,128]{1,0:T(8,128)S(1)}, f32[48,128]{1,0:T(8,128)S(1)}, u32[]{:S(2)}, u32[]{:S(2)}) collective-permute-start(f32[48,128]{1,0:T(8,128)S(1)} %shard_map.93.after.sb_ref), channel_id=1, source_target_pairs={{1,2},{2,1},{3,4},{4,3},{5,6},{6,5},{7,8},{8,7},{9,10},{10,9},{11,... | collective-permute-start | bytes 73736 | tf_op jit(solution)/shard_map/ppermute | solution.py:635
  3.3 4.7 %collective-permute-start = (f32[40,128]{1,0:T(8,128)S(1)}, f32[40,128]{1,0:T(8,128)S(1)}, u32[]{:S(2)}, u32[]{:S(2)}) collective-permute-start(f32[40,128]{1,0:T(8,128)S(1)} %get-tuple-element.19), channel_id=1, source_target_pairs={{0,1},{1,0},{2,3},{3,2},{4,5},{5,4},{6,7},{7,6},{8,9},{9,8},{10,11... | collective-permute-start | bytes 61448 | tf_op jit(solution)/shard_map/ppermute | solution.py:635
  8.0 17.8 %collective-permute-start.2 = (f32[136,128]{1,0:T(8,128)S(1)}, f32[136,128]{1,0:T(8,128)S(1)}, u32[]{:S(2)}, u32[]{:S(2)}) collective-permute-start(f32[136,128]{1,0:T(8,128)S(1)} %get-tuple-element.22), channel_id=1, source_target_pairs={{0,16},{1,17},{2,18},{3,19},{4,20},{5,21},{6,22},{7,23},{8,24},{9,... | collective-permute-start | bytes 208904 | tf_op jit(solution)/shard_map/ppermute | solution.py:635
  21.6 6.0 %collective-permute-start.3 = (f32[136,128]{1,0:T(8,128)S(1)}, f32[136,128]{1,0:T(8,128)S(1)}, u32[]{:S(2)}, u32[]{:S(2)}) collective-permute-start(f32[136,128]{1,0:T(8,128)S(1)} %get-tuple-element.23), channel_id=1, source_target_pairs={{0,496},{1,497},{2,498},{3,499},{4,500},{5,501},{6,502},{7,503},{8... | collective-permute-start | bytes 208904 | tf_op jit(solution)/shard_map/ppermute | solution.py:635
  27.6 15.2 %collective-permute-start.4 = (f32[128,128]{1,0:T(8,128)S(1)}, f32[128,128]{1,0:T(8,128)S(1)}, u32[]{:S(2)}, u32[]{:S(2)}) collective-permute-start(f32[128,128]{1,0:T(8,128)S(1)} %get-tuple-element.30), channel_id=1, source_target_pairs={{15,63},{31,495},{47,95},{63,15},{79,127},{95,47},{111,159},{127,7... | collective-permute-start | bytes 196616 | tf_op jit(solution)/shard_map/ppermute | solution.py:635
  31.5 11.3 %collective-permute-start.5 = (f32[128,128]{1,0:T(8,128)S(1)}, f32[128,128]{1,0:T(8,128)S(1)}, u32[]{:S(2)}, u32[]{:S(2)}) collective-permute-start(f32[128,128]{1,0:T(8,128)S(1)} %get-tuple-element.31), channel_id=1, source_target_pairs={{15,479},{31,79},{47,511},{63,111},{79,31},{95,143},{111,63},{127,... | collective-permute-start | bytes 196616 | tf_op jit(solution)/shard_map/ppermute | solution.py:635

commit v5 on v4

v5 whole, which is shorter than its diff:
```python
import functools

import jax
import jax.numpy as jnp
from jax import lax
from jax.experimental import pallas as pl
from jax.experimental.pallas import tpu as pltpu
from jax.sharding import PartitionSpec as P

STEPS = 4
TIME_STEP = 0.1
DIFFUSE = 0.15
EXPAND = 0.2
CONTRACT = 0.8
ROTATION = 0.5

HALO = 2 * STEPS
LANES = 128
FIELDS = 4
REACH = 4
ARC = 2 * REACH + 1
CAP = 48
PARITY = (1.0, 1.0, -1.0, -1.0)
STATS = 6
STRIP = 8
STRIP_STEP = 6
FAR_ROWS = (2, 4, 6)
FAR = 128
UPPER = 24


def lane_index(rows=8):
    return lax.broadcasted_iota(jnp.int32, (rows, LANES), 1)


def roll(x, shift):
    shift = shift % LANES
    return x if shift == 0 else pltpu.roll(x, shift, 1)


def is_odd():
    return lax.rem(lax.axis_index("lat"), 2) == 1


def is_top():
    return lax.axis_index("lat") == lax.axis_size("lat") - 1


def is_early():
    return lax.axis_index("lon") < lax.axis_size("lon") // 4


def is_odd_lon():
    return lax.rem(lax.axis_index("lon"), 2) == 1


class Either:
    def __init__(self, flag, yes, no):
        self.flag, self.yes, self.no = flag, yes, no

    def __getitem__(self, index):
        return jnp.where(self.flag, self.yes[index], self.no[index])


def near_refs(first, second):
    odd_lon = is_odd_lon()
    return Either(odd_lon, second, first), Either(odd_lon, first, second)


def first_rows_kernel(t_ref, s_ref, u_ref, v_ref, m_ref, opp_ref, after, out, ints, sems):
    start = pl.multiple_of(jnp.where(is_odd(), t_ref.shape[1] - HALO, 0), 8)
    copies = [pltpu.make_async_copy(opp_ref, ints.at[pl.ds(8, 1), :], sems.at[5])]
    for i, ref in enumerate((t_ref, s_ref, u_ref, v_ref, m_ref)):
        target = out.at[pl.ds(8 * i, 8), :] if i < FIELDS else ints.at[pl.ds(0, 8), :]
        copies.append(
            pltpu.make_async_copy(ref.at[0, pl.ds(start, HALO), :], target, sems.at[i])
        )
    for copy in copies:
        copy.start()
    for copy in copies:
        copy.wait()
    out[32:40, :] = ints[0:8, :].astype(jnp.float32)
    out[40:48, :] = jnp.broadcast_to(ints[8:9, :].astype(jnp.float32), (8, LANES))


def add_columns(e, w, tile, g):
    lane = lane_index()
    slots = ([g] if g < STRIP else []) + ([g - STRIP_STEP + STRIP] if g >= STRIP_STEP else [])
    for slot in slots:
        here = (lane >= 8 * slot) & (lane < 8 * slot + 8)
        e = jnp.where(here, roll(tile, 8 * slot - (LANES - HALO)), e)
        w = jnp.where(here, roll(tile, 8 * slot), w)
    return e, w


def pair_kernel(height, e_in, w_in, sb_ref, ra_ref, rb_ref, first, second):
    odd, odd_lon = is_odd(), is_odd_lon()
    for i in range(5):
        at = slice(i * 8, i * 8 + 8)
        ra, rb = ra_ref[at, :], rb_ref[at, :]
        e, w = add_columns(e_in[at, :], w_in[at, :], jnp.where(odd, ra, rb), 0)
        e, w = add_columns(e, w, jnp.where(odd, rb, ra), height // 8 + 1)
        first[at, :] = jnp.where(odd_lon, e, w)
        second[at, :] = jnp.where(odd_lon, w, e)

    @pl.when(is_top())
    def _():
        for ref in (first, second):
            ref[40 : 40 + CAP, :] = sb_ref[...]
            ref[40 + CAP : 40 + 2 * CAP, :] = rb_ref[...]


def far_places(counts):
    base = 0
    for j, n in enumerate(counts):
        for side in (0, 1):
            yield j, side, n, base
            base += 5 * n + 1


def far_kernel(sb_ref, rb_ref, first_in, second_in, first, second):
    @pl.when(is_top())
    def _():
        far_flag = jnp.logical_not(is_odd_lon())
        rw_ref, re_ref = near_refs(first_in, second_in)
        sources = (
            ((rw_ref, 40), (rw_ref, 40 + CAP)),
            ((sb_ref, 0), (rb_ref, 0)),
            ((re_ref, 40), (re_ref, 40 + CAP)),
        )

        def fill(out, counts):
            for j, side, n, base in far_places(counts):
                ref, at = sources[j][side]
                for i in range(5):
                    out[base + i * n : base + i * n + n, :] = ref[
                        at + 8 * i + 8 - n : at + 8 * i + 8, :
                    ]
                out[base + 5 * n : base + 5 * n + 1, :] = ref[at + 40 : at + 41, :]
            out[FAR - 2 : FAR, :] = jnp.zeros((2, LANES), jnp.float32)

        @pl.when(far_flag)
        def _():
            fill(first, FAR_ROWS)
            fill(second, FAR_ROWS[::-1])

        @pl.when(jnp.logical_not(far_flag))
        def _():
            fill(first, FAR_ROWS[::-1])
            fill(second, FAR_ROWS)


def first_pass(centre, north, south, east, west, stat, w_s):
    sea, count, w_e, w_n, turn = stat
    laps = [
        sea * (((east[i] + west[i]) + (north[i] + south[i])) - count * centre[i])
        for i in range(FIELDS)
    ]
    t, s, u, v = centre
    flow_e = (0.25 * TIME_STEP) * w_e * (u + east[2])
    flow_n = (0.25 * TIME_STEP) * w_n * (v + north[3])
    flow_s = (0.25 * TIME_STEP) * w_s * (v + south[3])
    partial, flux = [], []
    for i in (0, 1):
        c = centre[i]
        flux.append(flow_e * (c + east[i]))
        partial.append(c - (flow_n * (c + north[i]) - flow_s * (c + south[i])))
    ratio = EXPAND / CONTRACT
    slope = 0.25 * TIME_STEP * CONTRACT
    q = s - ratio * t
    q_e = east[1] - ratio * east[0]
    q_n = north[1] - ratio * north[0]
    q_s = south[1] - ratio * south[0]
    flux.append(slope * w_e * (q_e - q))
    partial.append(u + turn * v)
    partial.append(v - (turn * u + slope * (w_n * (q_n - q) + w_s * (q - q_s))))
    return laps, partial, flux


def face_terms(i, lap, east, w_e, flux):
    mix = (TIME_STEP * DIFFUSE) * w_e * (east - lap)
    if i < 2:
        return flux + mix, flux + mix
    if i == 2:
        return flux + mix, mix - flux
    return mix, mix


def second_pass(partial, loss, gain, lap, north, south, sea, count_ns):
    mix = (TIME_STEP * DIFFUSE) * ((north + south) - count_ns * lap)
    return sea * (partial - ((loss - gain) + mix))


class Band:
    def __init__(self, state, laps, part, flux, stat):
        self.state, self.laps, self.part, self.flux, self.stat = state, laps, part, flux, stat
        self.rows = range(8, state.shape[1] - 8, 8)

    def pad(self):
        nothing = jnp.zeros((8, LANES), jnp.float32)
        for row in (0, self.rows[-1] + 8):
            for i in range(FIELDS):
                self.state[i, row : row + 8, :] = nothing
                self.laps[i, row : row + 8, :] = nothing
            for i in range(STATS):
                self.stat[i, row : row + 8, :] = nothing

    def weigh(self, turning):
        for r in self.rows:
            at = slice(r, r + 8)
            sea = self.stat[0, at, :]
            north, south = self.stat[0, r + 1 : r + 9, :], self.stat[0, r - 1 : r + 7, :]
            east, west = roll(sea, -1), roll(sea, 1)
            self.stat[1, at, :] = (east + west) + (north + south)
            self.stat[2, at, :] = sea * east
            self.stat[3, at, :] = sea * north
            self.stat[4, at, :] = turning(r)
            self.stat[5, at, :] = north + south
            for i in range(FIELDS):
                self.state[i, at, :] = sea * self.state[i, at, :]

    def step(self):
        for r in self.rows:
            at, up, down = slice(r, r + 8), slice(r + 1, r + 9), slice(r - 1, r + 7)
            centre = [self.state[i, at, :] for i in range(FIELDS)]
            lap, partial, flux = first_pass(
                centre,
                [self.state[i, up, :] for i in range(FIELDS)],
                [self.state[i, down, :] for i in range(FIELDS)],
                [roll(x, -1) for x in centre],
                [roll(x, 1) for x in centre],
                [self.stat[i, at, :] for i in range(5)],
                self.stat[3, down, :],
            )
            for i in range(FIELDS):
                self.laps[i, at, :] = lap[i]
                self.part[i, at, :] = partial[i]
                if i < 3:
                    self.flux[i, at, :] = flux[i]
        for r in self.rows:
            at, up, down = slice(r, r + 8), slice(r + 1, r + 9), slice(r - 1, r + 7)
            sea, w_e, count_ns = (self.stat[i, at, :] for i in (0, 2, 5))
            for i in range(FIELDS):
                lap = self.laps[i, at, :]
                flux = self.flux[i, at, :] if i < 3 else None
                loss, gain = face_terms(i, lap, roll(lap, -1), w_e, flux)
                self.state[i, at, :] = second_pass(
                    self.part[i, at, :],
                    loss,
                    roll(gain, 1),
                    lap,
                    self.laps[i, up, :],
                    self.laps[i, down, :],
                    sea,
                    count_ns,
                )


def strip_own(low, high):
    lane = lane_index()
    second = lane >= 64
    west = jnp.where(second, roll(high, 72), roll(low, 8))
    east = jnp.where(second, roll(high, 112), roll(low, 48))
    return jnp.where(lax.rem(lane, 64) < 32, west, east)


def prepare(refs, fields, a_ref, e_ref, w_ref, inner, strip, ints, state, laps, part, flux, stat, sems):
    height = fields.shape[1]
    total_rows = height * lax.axis_size("lat")
    copies = []
    for i, ref in enumerate(refs):
        target = fields.at[i] if i < FIELDS else ints
        copies.append(pltpu.make_async_copy(ref.at[0], target, sems.at[i]))
    for copy in copies:
        copy.start()
    for copy in copies:
        copy.wait()
    fields[FIELDS] = ints[...].astype(jnp.float32)
    odd = is_odd()
    bands = Band(state, laps, part, flux, stat)
    bands.pad()
    for i in range(5):
        tiles = [fields[i, 8 * g : 8 * g + 8, :] for g in range(height // 8)]
        a_ref[i * 8 : i * 8 + 8, :] = jnp.where(odd, tiles[0], tiles[-1])
        e = w = jnp.zeros((8, LANES), jnp.float32)
        ref, at = (state, i) if i < FIELDS else (stat, 0)
        for g, tile in enumerate(tiles):
            e, w = add_columns(e, w, tile, g + 1)
            ref[at, 8 + 8 * g : 16 + 8 * g, :] = tile
        e_ref[i * 8 : i * 8 + 8, :] = e
        w_ref[i * 8 : i * 8 + 8, :] = w
        for n in range(STRIP):
            low, high = tiles[max(n - 1, 0)], tiles[min(n + STRIP_STEP - 1, len(tiles) - 1)]
            strip[i, 8 * n : 8 * n + 8, :] = strip_own(low, high)
    base_row = (lax.axis_index("lat") * height).astype(jnp.float32)
    sub = row_in_tile()
    bands.weigh(lambda r: turning_of(base_row + float(r - 8) + sub, total_rows))

    def step(n, carry):
        bands.step()
        return carry

    lax.fori_loop(0, STEPS, step, 0)
    for i in range(FIELDS):
        for g in range(height // 8):
            inner[i, 8 * g : 8 * g + 8, :] = state[i, 8 + 8 * g : 16 + 8 * g, :]


def early_kernel(*refs):
    @pl.when(is_early())
    def _():
        prepare(refs[:5], *refs[5:])


def late_kernel(*refs):
    early = is_early()

    @pl.when(early)
    def _():
        for source, target in zip(refs[6:12], refs[12:18]):
            target[...] = source[...]

    @pl.when(jnp.logical_not(early))
    def _():
        prepare(refs[:5], *refs[12:])


def strip_ghosts(blocks, old):
    before, here, after = blocks
    lane = lane_index(here.shape[0])
    new = jnp.where(lane < 96, roll(here, 72), roll(here, 112))
    new = jnp.where(lane < 72, roll(before, 64 - (LANES - HALO)), new)
    new = jnp.where(lane >= 112, roll(after, 112), new)
    return jnp.where(lane < 64, old, new)


def join_columns(centre, strip, second):
    lane = lane_index()
    start = 64 if second else 0
    west, east = roll(strip, -start - HALO), roll(strip, LANES - HALO - start - 40)
    return jnp.where(lane < HALO, west, jnp.where(lane >= LANES - HALO, east, centre))


def turning_of(row, total_rows):
    return (TIME_STEP * ROTATION) * (2.0 * (row + 0.5) / total_rows - 1.0)


def row_in_tile():
    return lax.broadcasted_iota(jnp.int32, (8, LANES), 0).astype(jnp.float32)


def frame_kernel(
    fields,
    strip,
    inner,
    sb_ref,
    ra_ref,
    rb_ref,
    first_in,
    second_in,
    t_out,
    s_out,
    u_out,
    v_out,
    upper_state,
    upper_stat,
    state,
    laps,
    part,
    flux,
    stat,
):
    rw_ref, re_ref = near_refs(first_in, second_in)
    odd, top = is_odd(), is_top()
    lane = lane_index()
    height = fields.shape[1]
    total_rows = height * lax.axis_size("lat")
    north_row, strip_row = 8 + UPPER, 8 + 2 * UPPER
    bands = Band(state, laps, part, flux, stat)
    bands.pad()
    side = lax.rem(lane, 64)

    for i in range(5):
        at = slice(i * 8, i * 8 + 8)
        ra, rb, from_w, from_e = ra_ref[at, :], rb_ref[at, :], rw_ref[at, :], re_ref[at, :]
        south, north = jnp.where(odd, ra, rb), jnp.where(odd, rb, ra)
        ref, at = (state, i) if i < FIELDS else (stat, 0)
        ref[at, 8:16, :] = south
        ref[at, 16 : 8 + UPPER, :] = fields[i, 0 : UPPER - 8, :]
        ref[at, north_row : north_row + UPPER - 8, :] = fields[i, height - UPPER + 8 : height, :]
        ref[at, north_row + UPPER - 8 : strip_row, :] = north
        for n in range(STRIP):
            own = strip[i, 8 * n : 8 * n + 8, :]
            if n == 0:
                own = jnp.where(lane < 64, strip_own(south, south), own)
            if n == STRIP - 1:
                own = jnp.where(lane >= 64, strip_own(north, north), own)
            own = jnp.where(side < HALO, roll(from_w, -8 * n), own)
            own = jnp.where(side >= 48, roll(from_e, 48 - 8 * n), own)
            ref[at, strip_row + 8 * n : strip_row + 8 * n + 8, :] = own

    @pl.when(top)
    def _():
        pairs = (
            (rw_ref, 40, rw_ref, 40 + CAP),
            (sb_ref, 0, rb_ref, 0),
            (re_ref, 40, re_ref, 40 + CAP),
        )
        for i in range(5):
            ghosts = []
            for own, own_at, facing, facing_at in pairs:
                index = lax.rem(own[own_at + 40 : own_at + 48, :].astype(jnp.int32), LANES)
                rows = facing[facing_at + 8 * i : facing_at + 8 * i + 8, :]
                ghosts.append(
                    (PARITY + (1.0,))[i]
                    * jnp.take_along_axis(rows, index, axis=1, mode="promise_in_bounds")
                )
            ref, at = (state, i) if i < FIELDS else (stat, 0)
            row = north_row + UPPER - HALO
            ref[at, row : row + 1, :] = ghosts[1][7:8, :]
            ref[at, row + 1 : row + 2, :] = ghosts[1][6:7, :]
            for n in (0, 1):
                row = strip_row + 8 * STRIP - HALO + n
                ref[at, row : row + 1, :] = strip_ghosts(
                    [ghost[7 - n : 8 - n, :] for ghost in ghosts], ref[at, row : row + 1, :]
                )

    base_row = (lax.axis_index("lat") * height - HALO).astype(jnp.float32)
    sub = row_in_tile()
    second = jnp.where(lane >= 64, 8.0 * STRIP_STEP, 0.0)

    def turning(r):
        if r < north_row:
            row = base_row + float(r - 8) + sub
        elif r < strip_row:
            row = base_row + float(height + 2 * HALO - UPPER + r - north_row) + sub
        else:
            row = base_row + float(r - strip_row) + sub + second
        return turning_of(row, total_rows)

    bands.weigh(turning)

    def step(n, carry):
        bands.step()

        @pl.when(top & (n == 0))
        def _():
            for which, row in enumerate((north_row, strip_row + 8 * STRIP - UPPER)):
                for i in range(FIELDS):
                    upper_state[i, which] = state[i, row : row + UPPER, :]
                for i in range(STATS):
                    upper_stat[i, which] = stat[i, row : row + UPPER, :]

        return carry

    lax.fori_loop(0, STEPS, step, 0)

    tiles_n = height // 8
    for i, out in enumerate((t_out, s_out, u_out, v_out)):
        for g in range(tiles_n):
            if g == 0:
                centre = state[i, 16:24, :]
            elif g == tiles_n - 1:
                centre = state[i, north_row + 8 : north_row + 16, :]
            else:
                centre = inner[i, 8 * g : 8 * g + 8, :]
            late = g + 1 > STRIP_STEP
            row = strip_row + 8 * (g + 1 - (STRIP_STEP if late else 0))
            out[0, 8 * g : 8 * g + 8, :] = join_columns(centre, state[i, row : row + 8, :], late)


def arc_east(blocks):
    lane, last = lane_index(), len(blocks) - 1
    e = [roll(x, -1) for x in blocks]
    return [jnp.where(lane == LANES - 1, e[min(k + 1, last)], e[k]) for k in range(last + 1)]


def arc_west(blocks):
    lane = lane_index()
    w = [roll(x, 1) for x in blocks]
    return [jnp.where(lane == 0, w[max(k - 1, 0)], w[k]) for k in range(len(blocks))]


def cap_kernel(
    t_in,
    s_in,
    u_in,
    v_in,
    upper_state,
    upper_stat,
    sb_ref,
    rb_ref,
    first_in,
    second_in,
    first_far,
    second_far,
    t_out,
    s_out,
    u_out,
    v_out,
    state,
    laps,
    part,
    flux,
    stat,
    cap,
    cap_lap,
    cap_part,
    cap_flux,
    cap_stat,
    cap_opp,
    rows_out,
    sems,
):
    rw_ref, re_ref = near_refs(first_in, second_in)
    far_flag = jnp.logical_not(is_odd_lon())
    w3_ref = Either(far_flag, second_far, first_far)
    e3_ref = Either(far_flag, first_far, second_far)
    lane = lane_index()
    height = t_out.shape[1]
    total_rows = height * lax.axis_size("lat")
    bands = Band(state, laps, part, flux, stat)
    nothing = jnp.zeros((8, LANES), jnp.float32)
    cap_turn = turning_of(float(total_rows - HALO + 1) + row_in_tile(), total_rows)

    def fill_ghosts(ref, parities, low, high, sides):
        for side in range(sides):
            ghosts = {}
            for k in range(low, high):
                index = cap_opp[side, k]
                for i, parity in enumerate(parities):
                    rows = ref[1 - side, i, ARC - 1 - k, 0:8, :]
                    ghosts[k, i] = parity * jnp.take_along_axis(
                        rows, index, axis=1, mode="promise_in_bounds"
                    )
            for (k, i), ghost in ghosts.items():
                ref[side, i, k, 8:9, :] = ghost[7:8, :]
                ref[side, i, k, 9:10, :] = ghost[6:7, :]

    def put_block(side, place, ref, base, n):
        sea = ref[base + 4 * n : base + 5 * n, :]
        cap_stat[side, 0, place, 8 - n : 8, :] = sea
        cap_stat[side, 0, place, 10:16, :] = nothing[0:6]
        if n < 8:
            cap_stat[side, 0, place, 0 : 8 - n, :] = nothing[n:8]
        for i in range(FIELDS):
            cap[side, i, place, 8 - n : 8, :] = sea * ref[base + n * i : base + n * i + n, :]
            if n < 8:
                cap[side, i, place, 0 : 8 - n, :] = nothing[n:8]
            cap[side, i, place, 10:16, :] = nothing[0:6]
            cap_lap[side, i, place, 0:8, :] = nothing
            cap_lap[side, i, place, 8:16, :] = nothing
        opp = jnp.broadcast_to(ref[base + 5 * n : base + 5 * n + 1, :], (8, LANES))
        cap_opp[side, place] = lax.rem(opp.astype(jnp.int32), LANES)

    def cap_weigh():
        for side in (0, 1):
            for start in (0, 1):
                seas = [cap_stat[side, 0, k, start : start + 8, :] for k in range(ARC)]
                east, west = arc_east(seas), arc_west(seas)
                for k in range(ARC):
                    north = cap_stat[side, 0, k, start + 1 : start + 9, :]
                    if start:
                        south = cap_stat[side, 0, k, start - 1 : start + 7, :]
                        cap_stat[side, 1, k, 1:9, :] = (east[k] + west[k]) + (north + south)
                        cap_stat[side, 4, k, 1:9, :] = north + south
                    cap_stat[side, 2, k, start : start + 8, :] = seas[k] * east[k]
                    cap_stat[side, 3, k, start : start + 8, :] = seas[k] * north

    def cap_first(side, low, high):
        span = range(low - 1, high + 1)
        fields = [[cap[side, i, k, 1:9, :] for k in span] for i in range(FIELDS)]
        east, west = [arc_east(f) for f in fields], [arc_west(f) for f in fields]
        for n, k in enumerate(span):
            lap, partial, fluxes = first_pass(
                [f[n] for f in fields],
                [cap[side, i, k, 2:10, :] for i in range(FIELDS)],
                [cap[side, i, k, 0:8, :] for i in range(FIELDS)],
                [f[n] for f in east],
                [f[n] for f in west],
                [cap_stat[side, i, k, 1:9, :] for i in range(4)] + [cap_turn],
                cap_stat[side, 3, k, 0:8, :],
            )
            for i in range(FIELDS):
                cap_lap[side, i, k, 1:9, :] = lap[i]
                if i < 3:
                    cap_flux[side, i, k, 0:8, :] = fluxes[i]
                if low <= k < high:
                    cap_part[side, i, k, 0:8, :] = partial[i]

    def cap_second(side, low, high):
        span = range(low - 1, high + 1)
        for i in range(FIELDS):
            blocks = [cap_lap[side, i, k, 1:9, :] for k in span]
            terms = [
                face_terms(
                    i,
                    blocks[n],
                    east,
                    cap_stat[side, 2, span[n], 1:9, :],
                    cap_flux[side, i, span[n], 0:8, :] if i < 3 else None,
                )
                for n, east in enumerate(arc_east(blocks))
            ]
            gains = arc_west([gain for _, gain in terms])
            for n, k in enumerate(span):
                if low <= k < high:
                    cap[side, i, k, 1:9, :] = second_pass(
                        cap_part[side, i, k, 0:8, :],
                        terms[n][0],
                        gains[n],
                        blocks[n],
                        cap_lap[side, i, k, 2:10, :],
                        cap_lap[side, i, k, 0:8, :],
                        cap_stat[side, 0, k, 1:9, :],
                        cap_stat[side, 4, k, 1:9, :],
                    )

    @pl.when(is_top())
    def _():
        parts = [(j, side, w3_ref, base, n) for j, side, n, base in far_places(FAR_ROWS)]
        parts += [
            (j + REACH + 2, side, e3_ref, base, n)
            for j, side, n, base in far_places(FAR_ROWS[::-1])
        ]
        for side in (0, 1):
            parts.append((REACH - 1, side, rw_ref, 40 + CAP * side, 8))
            parts.append((REACH, side, (sb_ref, rb_ref)[side], 0, 8))
            parts.append((REACH + 1, side, re_ref, 40 + CAP * side, 8))
        for k, side, ref, base, n in parts:
            put_block(side, ARC - 1 - k if side else k, ref, base, n)
        bands.pad()
        for which in (0, 1):
            row = 8 + UPPER * which
            for i in range(FIELDS):
                state[i, row : row + UPPER, :] = upper_state[i, which]
            for i in range(STATS):
                stat[i, row : row + UPPER, :] = upper_stat[i, which]
        fill_ghosts(cap_stat, (1.0,), 0, ARC, 2)
        fill_ghosts(cap, PARITY, 0, ARC, 2)
        cap_weigh()
        for n in range(STEPS - 1):
            low, high = n + 1, ARC - 1 - n
            first_side = 1 if n == STEPS - 2 else 0

            def one(side, carry, low=low, high=high):
                cap_first(side, low, high)
                cap_second(side, low, high)
                return carry

            lax.fori_loop(first_side, 2, one, 0)
            fill_ghosts(cap, PARITY, low, high, 2 - first_side)
            for i in range(FIELDS):
                ghosts = [cap[0, i, k, 8:10, :] for k in (REACH - 1, REACH, REACH + 1)]
                row = 8 + UPPER - HALO
                state[i, row : row + 2, :] = ghosts[1]
                row += UPPER
                state[i, row : row + 2, :] = strip_ghosts(ghosts, state[i, row : row + 2, :])
            bands.step()
        copies = []
        for i, out in enumerate((t_out, s_out, u_out, v_out)):
            row = 8 + UPPER - 2 * HALO
            rows_out[i] = join_columns(
                state[i, row : row + 8, :], state[i, row + UPPER : row + UPPER + 8, :], True
            )
            copies.append(
                pltpu.make_async_copy(
                    rows_out.at[i], out.at[0, pl.ds(height - HALO, HALO), :], sems.at[i]
                )
            )
        for copy in copies:
            copy.start()
        for copy in copies:
            copy.wait()


def body(lon_count, lat_count, t, s, u, v, m, opp):
    fields = (t, s, u, v, m)
    height = t.shape[1]
    vmem, anywhere = (
        pl.BlockSpec(memory_space=pltpu.VMEM),
        pl.BlockSpec(memory_space=pltpu.HBM),
    )
    f32, i32 = jnp.float32, jnp.int32

    def call(kernel, inputs, shapes, scratch=(), far=0, flops=0):
        inputs = [
            pltpu.with_memory_space_constraint(x, pltpu.HBM) if i < far else x
            for i, x in enumerate(inputs)
        ]
        return pl.pallas_call(
            kernel,
            out_shape=[jax.ShapeDtypeStruct(shape, f32) for shape in shapes],
            in_specs=[anywhere] * far + [vmem] * (len(inputs) - far),
            out_specs=[vmem] * len(shapes),
            scratch_shapes=list(scratch),
            compiler_params=pltpu.CompilerParams(vmem_limit_bytes=32 * 1024 * 1024),
            cost_estimate=pl.CostEstimate(flops=flops, bytes_accessed=flops, transcendentals=0),
        )(*inputs)

    def place(lon, lat):
        return (lon % lon_count) * lat_count + lat

    lons, lats = range(lon_count), range(lat_count)
    last = lat_count - 1
    pairs_a = [(place(i, j), place(i, j ^ 1)) for i in lons for j in lats]
    pairs_b = [(place(i, j), place(i, ((j - 1) ^ 1) + 1)) for i in lons for j in lats[1:last]]
    pairs_b += [(place(i, last), place(-i, last)) for i in lons]

    def swap(x, by, rest, rows):
        pairs = []
        for i in lons:
            other = i + by if i % 2 == rest else i - by
            pairs += [(place(i, j), place(other, j)) for j in rows]
        return exchange(x, pairs)

    def exchange(x, pairs):
        return lax.ppermute(x, ("lon", "lat"), pairs)

    def band_scratch(rows):
        return [
            pltpu.VMEM((n, 16 + rows, LANES), f32) for n in (FIELDS, FIELDS, FIELDS, 3, STATS)
        ]

    prepared = [(5, height, LANES), (40, LANES), (40, LANES), (40, LANES)]
    prepared += [(FIELDS, height, LANES), (5, 8 * STRIP, LANES)]
    scratch = [pltpu.VMEM((height, LANES), i32), *band_scratch(height), pltpu.SemaphoreType.DMA((5,))]
    own = call(early_kernel, fields, prepared, scratch, far=5, flops=10**7)
    (send_b,) = call(
        first_rows_kernel,
        (*fields, opp.reshape(1, LANES), own[1]),
        [(CAP, LANES)],
        [pltpu.VMEM((16, LANES), i32), pltpu.SemaphoreType.DMA((6,))],
        far=6,
    )
    from_b = exchange(send_b, pairs_b)
    stack, send_a, columns_e, columns_w, inner, strip = call(
        late_kernel, (*fields, send_b, *own), prepared, scratch, far=5, flops=10**7
    )
    from_a = exchange(send_a, pairs_a)
    send_1, send_2 = call(
        functools.partial(pair_kernel, height),
        (columns_e, columns_w, send_b, from_a, from_b),
        [(40 + 2 * CAP, LANES)] * 2,
    )
    near_1 = swap(send_1, 1, 1, lats)
    near_2 = swap(send_2, 1, 0, lats)
    far_send_1, far_send_2 = call(
        far_kernel, (send_b, from_b, near_1, near_2), [(FAR, LANES)] * 2
    )
    far_1 = swap(far_send_1, 3, 0, [last])
    far_2 = swap(far_send_2, 3, 1, [last])

    *outs, upper_state, upper_stat = call(
        frame_kernel,
        (stack, strip, inner, send_b, from_a, from_b, near_1, near_2),
        [t.shape] * 4 + [(FIELDS, 2, UPPER, LANES), (STATS, 2, UPPER, LANES)],
        band_scratch(2 * UPPER + 8 * STRIP),
        flops=10**7,
    )
    return tuple(
        pl.pallas_call(
            cap_kernel,
            out_shape=[jax.ShapeDtypeStruct(t.shape, f32)] * 4,
            in_specs=[anywhere] * 4 + [vmem] * 8,
            out_specs=[anywhere] * 4,
            scratch_shapes=band_scratch(2 * UPPER)
            + [
                pltpu.VMEM((2, FIELDS, ARC, 16, LANES), f32),
                pltpu.VMEM((2, FIELDS, ARC, 16, LANES), f32),
                pltpu.VMEM((2, FIELDS, ARC, 8, LANES), f32),
                pltpu.VMEM((2, 3, ARC, 8, LANES), f32),
                pltpu.VMEM((2, 5, ARC, 16, LANES), f32),
                pltpu.VMEM((2, ARC, 8, LANES), i32),
                pltpu.VMEM((FIELDS, 8, LANES), f32),
                pltpu.SemaphoreType.DMA((FIELDS,)),
            ],
            input_output_aliases={i: i for i in range(4)},
            compiler_params=pltpu.CompilerParams(vmem_limit_bytes=32 * 1024 * 1024),
        )(*outs, upper_state, upper_stat, send_b, from_b, near_1, near_2, far_1, far_2)
    )


def solution(mesh):
    placed = P(None, "lat", "lon")
    return jax.shard_map(
        functools.partial(body, mesh.shape["lon"], mesh.shape["lat"]),
        mesh=mesh,
        in_specs=(placed,) * 5 + (P("lon"),),
        out_specs=(placed,) * 4,
        check_vma=False,
    )
```

time: 47.2 us -> 46.4 us (0.983)
  waiting for transfers between devices: 2.58 us -> 5.67 us
  starting transfers between devices: 31.7 us -> 29 us
  Pallas kernels: 11.8 us -> 10.7 us
    ppermute x6, waiting for transfers between devices: 2.58 us -> 5.67 us  [exchange(): return lax.ppermute(x, ('lon', 'lat'), pairs)]
    ppermute x6, starting transfers between devices: 31.7 us -> 29 us  [exchange(): return lax.ppermute(x, ('lon', 'lat'), pairs)]
    pallas_call x5 -> x6, Pallas kernels: 7.8 us -> 7.08 us  [call(): pl.pallas_call(kernel, out_shape=[jax.ShapeDtypeStruct(shape, f32) for sh...]
  transfers between devices with their start and end apart: 6 -> 6, of which waited for: 2 -> 4; matrix products, arithmetic and copies ran while one was open for 0% -> 0% of each run, Pallas kernels for 15% -> 7%
where the time goes in v5:
time: 46.4 us; the launch traced here: 46.1 us
  starting transfers between devices  29 us (62%)
  Pallas kernels  10.7 us (23%)
  waiting for transfers between devices  5.67 us (12%)
  between operations  0.72 us (2%)
    ppermute x6, starting transfers between devices, exchange(): return lax.ppermute(x, ('lon', 'lat'), pairs)  29 us
    pallas_call x6, Pallas kernels, call(): pl.pallas_call(kernel, out_shape=[jax.ShapeDtypeStruct(shape, f32) for sh...  7.08 us
    ppermute x6, waiting for transfers between devices, exchange(): return lax.ppermute(x, ('lon', 'lat'), pairs)  5.67 us
    pallas_call x1, Pallas kernels, body(): pl.pallas_call(cap_kernel, out_shape=[jax.ShapeDtypeStruct(t.shape, f32)]...  3.63 us
  transfers between devices with their start and end apart: 6, of which 4 were waited for; matrix products, arithmetic and copies ran while one was open for 0% of the time, Pallas kernels for 7%

profile of v5, /device:TPU:71, one launch (start us, length us, event | category | flops | bytes accessed | tf_op | source)
XLA Modules:
  0.0 46.1 jit_solution(4408497763074155435)
XLA Ops:
  0.6 2.9 %shard_map.93 = (f32[5,96,128]{2,1,0:T(8,128)S(1)}, f32[40,128]{1,0:T(8,128)S(1)}, f32[40,128]{1,0:T(8,128)S(1)}, f32[40,128]{1,0:T(8,128)S(1)}, f32[4,96,128]{2,1,0:T(8,128)S(1)}, /*index=5*/f32[5,64,128]{2,1,0:T(8,128)S(1)}) custom-call(f32[1,96,128]{2,1,0:T(8,128)} %refs_0_.3, f32[1,96,128]{2,1,0:T(8,128)} %refs_1_.3, f32[1,96,128]{2,1,0:T(8,128)} %refs_2_.3, ...), custom_call_target="tpu_custom_call" | custom-call | flops 10000000 | bytes 10000000 | tf_op jit(solution)/shard_map/pallas_call | solution.py:691
  3.6 0.8 %shard_map.94.refs_5_.sb_ref = f32[48,128]{1,0:T(8,128)S(1)} custom-call(f32[1,96,128]{2,1,0:T(8,128)} %refs_0_.3, f32[1,96,128]{2,1,0:T(8,128)} %refs_1_.3, f32[1,96,128]{2,1,0:T(8,128)} %refs_2_.3, f32[1,96,128]{2,1,0:T(8,128)} %refs_3_.3, s32[1,96,128]{2,1,0:T(8,128)} %refs_4_.3, s32[1,128]{1,0:T(1,128)} %bitcast.1, ...), custom_call_target="tpu_custom_call" | custom-call | tf_op jit(solution)/shard_map/pallas_call | solution.py:691
  4.4 0.7 %collective-permute-start.1 = (f32[48,128]{1,0:T(8,128)S(1)}, f32[48,128]{1,0:T(8,128)S(1)}, u32[]{:S(2)}, u32[]{:S(2)}) collective-permute-start(f32[48,128]{1,0:T(8,128)S(1)} %shard_map.94.refs_5_.sb_ref), channel_id=1, source_target_pairs={{1,2},{2,1},{3,4},{4,3},{5,6},{6,5},{7,8},{8,7},{9,10},{10,9},{11,... | collective-permute-start | bytes 73736 | tf_op jit(solution)/shard_map/ppermute | solution.py:718
  5.1 0.1 shard_map.95
  5.2 3.8 %collective-permute-start = (f32[40,128]{1,0:T(8,128)S(1)}, f32[40,128]{1,0:T(8,128)S(1)}, u32[]{:S(2)}, u32[]{:S(2)}) collective-permute-start(f32[40,128]{1,0:T(8,128)S(1)} %get-tuple-element.35), channel_id=1, source_target_pairs={{0,1},{1,0},{2,3},{3,2},{4,5},{5,4},{6,7},{7,6},{8,9},{9,8},{10,11... | collective-permute-start | bytes 61448 | tf_op jit(solution)/shard_map/ppermute | solution.py:718
  9.0 0.8 %collective-permute-done.ra_ref = f32[40,128]{1,0:T(8,128)S(1)} collective-permute-done((f32[40,128]{1,0:T(8,128)S(1)}, f32[40,128]{1,0:T(8,128)S(1)}, u32[]{:S(2)}, u32[]{:S(2)}) %collective-permute-start) | collective-permute-done | bytes 20512 | tf_op jit(solution)/shard_map/ppermute | solution.py:718
  9.9 0.0 collective-permute-done.1.rb_ref
  9.9 0.1 shard_map.96
  9.9 14.0 %collective-permute-start.2 = (f32[136,128]{1,0:T(8,128)S(1)}, f32[136,128]{1,0:T(8,128)S(1)}, u32[]{:S(2)}, u32[]{:S(2)}) collective-permute-start(f32[136,128]{1,0:T(8,128)S(1)} %get-tuple-element.38), channel_id=1, source_target_pairs={{0,496},{1,497},{2,498},{3,499},{4,500},{5,501},{6,502},{7,503},{8... | collective-permute-start | bytes 208904 | tf_op jit(solution)/shard_map/ppermute | solution.py:718
  24.0 1.9 %collective-permute-start.3 = (f32[136,128]{1,0:T(8,128)S(1)}, f32[136,128]{1,0:T(8,128)S(1)}, u32[]{:S(2)}, u32[]{:S(2)}) collective-permute-start(f32[136,128]{1,0:T(8,128)S(1)} %get-tuple-element.39), channel_id=1, source_target_pairs={{0,16},{1,17},{2,18},{3,19},{4,20},{5,21},{6,22},{7,23},{8,24},{9,... | collective-permute-start | bytes 208904 | tf_op jit(solution)/shard_map/ppermute | solution.py:718
  25.9 0.3 collective-permute-done.2.first_in
  26.2 3.3 %collective-permute-done.3.second_in = f32[136,128]{1,0:T(8,128)S(1)} collective-permute-done((f32[136,128]{1,0:T(8,128)S(1)}, f32[136,128]{1,0:T(8,128)S(1)}, u32[]{:S(2)}, u32[]{:S(2)}) %collective-permute-start.3) | collective-permute-done | bytes 69664 | tf_op jit(solution)/shard_map/ppermute | solution.py:718
  29.5 1.9 %collective-permute-start.4 = (f32[128,128]{1,0:T(8,128)S(1)}, f32[128,128]{1,0:T(8,128)S(1)}, u32[]{:S(2)}, u32[]{:S(2)}) collective-permute-start(f32[128,128]{1,0:T(8,128)S(1)} %get-tuple-element.46), channel_id=1, source_target_pairs={{15,63},{31,495},{47,95},{63,15},{79,127},{95,47},{111,159},{127,7... | collective-permute-start | bytes 196616 | tf_op jit(solution)/shard_map/ppermute | solution.py:718
  31.4 6.6 %collective-permute-start.5 = (f32[128,128]{1,0:T(8,128)S(1)}, f32[128,128]{1,0:T(8,128)S(1)}, u32[]{:S(2)}, u32[]{:S(2)}) collective-permute-start(f32[128,128]{1,0:T(8,128)S(1)} %get-tuple-element.47), channel_id=1, source_target_pairs={{15,479},{31,79},{47,511},{63,111},{79,31},{95,143},{111,63},{127,... | collective-permute-start | bytes 196616 | tf_op jit(solution)/shard_map/ppermute | solution.py:718
  38.0 3.1 %shard_map.97 = (f32[1,96,128]{2,1,0:T(8,128)}, f32[1,96,128]{2,1,0:T(8,128)}, f32[1,96,128]{2,1,0:T(8,128)}, f32[1,96,128]{2,1,0:T(8,128)}, f32[4,2,24,128]{3,2...) custom-call(f32[5,96,128]{2,1,0:T(8,128)S(1)} %get-tuple-element.32.fields, f32[5,64,128]{2,1,0:T(8,128)S(1)} %get-tuple-element.33.strip, ...), custom_call_target="tpu_custom_call" | custom-call | flops 10000000 | bytes 10000000 | tf_op jit(solution)/shard_map/pallas_call | solution.py:691
  41.2 0.0 collective-permute-done.4.first_far
  41.2 1.3 %collective-permute-done.5.second_far = f32[128,128]{1,0:T(8,128)S(1)} collective-permute-done((f32[128,128]{1,0:T(8,128)S(1)}, f32[128,128]{1,0:T(8,128)S(1)}, u32[]{:S(2)}, u32[]{:S(2)}) %collective-permute-start.5) | collective-permute-done | bytes 65568 | tf_op jit(solution)/shard_map/ppermute | solution.py:718
  42.5 3.6 %shard_map.99 = (f32[1,96,128]{2,1,0:T(8,128)}, f32[1,96,128]{2,1,0:T(8,128)}, f32[1,96,128]{2,1,0:T(8,128)}, f32[1,96,128]{2,1,0:T(8,128)}) custom-call(f32[1,96,128]{2,1,0:T(8,128)} %get-tuple-element.40.t_in, f32[1,96,128]{2,1,0:T(8,128)} %get-tuple-element.41.s_in, ...), custom_call_target="tpu_custom_call", output_to_operand_aliasing={{0}: (0, {}), {1}: (1, {}), {2}: (2, {}), {3}: (3, {})} | custom-call | tf_op jit(solution)/shard_map/pallas_call | solution.py:762
  (1 shorter events, 0.0 us)
Async XLA Ops:
  4.4 5.5 %collective-permute-start.1 = (f32[48,128]{1,0:T(8,128)S(1)}, f32[48,128]{1,0:T(8,128)S(1)}, u32[]{:S(2)}, u32[]{:S(2)}) collective-permute-start(f32[48,128]{1,0:T(8,128)S(1)} %shard_map.94.refs_5_.sb_ref), channel_id=1, source_target_pairs={{1,2},{2,1},{3,4},{4,3},{5,6},{6,5},{7,8},{8,7},{9,10},{10,9},{11,... | collective-permute-start | bytes 73736 | tf_op jit(solution)/shard_map/ppermute | solution.py:718
  5.2 4.7 %collective-permute-start = (f32[40,128]{1,0:T(8,128)S(1)}, f32[40,128]{1,0:T(8,128)S(1)}, u32[]{:S(2)}, u32[]{:S(2)}) collective-permute-start(f32[40,128]{1,0:T(8,128)S(1)} %get-tuple-element.35), channel_id=1, source_target_pairs={{0,1},{1,0},{2,3},{3,2},{4,5},{5,4},{6,7},{7,6},{8,9},{9,8},{10,11... | collective-permute-start | bytes 61448 | tf_op jit(solution)/shard_map/ppermute | solution.py:718
  9.9 16.2 %collective-permute-start.2 = (f32[136,128]{1,0:T(8,128)S(1)}, f32[136,128]{1,0:T(8,128)S(1)}, u32[]{:S(2)}, u32[]{:S(2)}) collective-permute-start(f32[136,128]{1,0:T(8,128)S(1)} %get-tuple-element.38), channel_id=1, source_target_pairs={{0,496},{1,497},{2,498},{3,499},{4,500},{5,501},{6,502},{7,503},{8... | collective-permute-start | bytes 208904 | tf_op jit(solution)/shard_map/ppermute | solution.py:718
  24.0 5.5 %collective-permute-start.3 = (f32[136,128]{1,0:T(8,128)S(1)}, f32[136,128]{1,0:T(8,128)S(1)}, u32[]{:S(2)}, u32[]{:S(2)}) collective-permute-start(f32[136,128]{1,0:T(8,128)S(1)} %get-tuple-element.39), channel_id=1, source_target_pairs={{0,16},{1,17},{2,18},{3,19},{4,20},{5,21},{6,22},{7,23},{8,24},{9,... | collective-permute-start | bytes 208904 | tf_op jit(solution)/shard_map/ppermute | solution.py:718
  29.5 11.7 %collective-permute-start.4 = (f32[128,128]{1,0:T(8,128)S(1)}, f32[128,128]{1,0:T(8,128)S(1)}, u32[]{:S(2)}, u32[]{:S(2)}) collective-permute-start(f32[128,128]{1,0:T(8,128)S(1)} %get-tuple-element.46), channel_id=1, source_target_pairs={{15,63},{31,495},{47,95},{63,15},{79,127},{95,47},{111,159},{127,7... | collective-permute-start | bytes 196616 | tf_op jit(solution)/shard_map/ppermute | solution.py:718
  31.4 11.0 %collective-permute-start.5 = (f32[128,128]{1,0:T(8,128)S(1)}, f32[128,128]{1,0:T(8,128)S(1)}, u32[]{:S(2)}, u32[]{:S(2)}) collective-permute-start(f32[128,128]{1,0:T(8,128)S(1)} %get-tuple-element.47), channel_id=1, source_target_pairs={{15,479},{31,79},{47,511},{63,111},{79,31},{95,143},{111,63},{127,... | collective-permute-start | bytes 196616 | tf_op jit(solution)/shard_map/ppermute | solution.py:718

commit v6 on v5

--- a/solution.py
+++ b/solution.py
@@ -219,7 +219,8 @@
             for i in range(FIELDS):
                 self.state[i, at, :] = sea * self.state[i, at, :]
 
-    def step(self):
+    def step(self, kept=None):
+        kept = self.rows if kept is None else kept
         for r in self.rows:
             at, up, down = slice(r, r + 8), slice(r + 1, r + 9), slice(r - 1, r + 7)
             centre = [self.state[i, at, :] for i in range(FIELDS)]
@@ -234,10 +235,11 @@
             )
             for i in range(FIELDS):
                 self.laps[i, at, :] = lap[i]
-                self.part[i, at, :] = partial[i]
-                if i < 3:
-                    self.flux[i, at, :] = flux[i]
-        for r in self.rows:
+                if r in kept:
+                    self.part[i, at, :] = partial[i]
+                    if i < 3:
+                        self.flux[i, at, :] = flux[i]
+        for r in kept:
             at, up, down = slice(r, r + 8), slice(r + 1, r + 9), slice(r - 1, r + 7)
             sea, w_e, count_ns = (self.stat[i, at, :] for i in (0, 2, 5))
             for i in range(FIELDS):
@@ -656,7 +658,8 @@
                 state[i, row : row + 2, :] = ghosts[1]
                 row += UPPER
                 state[i, row : row + 2, :] = strip_ghosts(ghosts, state[i, row : row + 2, :])
-            bands.step()
+            start = 16 if n == STEPS - 2 else 8
+            bands.step([r + UPPER * which for which in (0, 1) for r in range(start, 24, 8)])
         copies = []
         for i, out in enumerate((t_out, s_out, u_out, v_out)):
             row = 8 + UPPER - 2 * HALO

time: 46.4 us -> 46.4 us (level)
  no operation moved by 1% of the time
where the time goes in v6:
time: 46.4 us; the launch traced here: 46 us
  starting transfers between devices  29 us (62%)
  Pallas kernels  10.7 us (23%)
  waiting for transfers between devices  5.67 us (12%)
  between operations  0.72 us (2%)
    ppermute x6, starting transfers between devices, exchange(): return lax.ppermute(x, ('lon', 'lat'), pairs)  29 us
    pallas_call x6, Pallas kernels, call(): pl.pallas_call(kernel, out_shape=[jax.ShapeDtypeStruct(shape, f32) for sh...  7.08 us
    ppermute x6, waiting for transfers between devices, exchange(): return lax.ppermute(x, ('lon', 'lat'), pairs)  5.67 us
    pallas_call x1, Pallas kernels, body(): pl.pallas_call(cap_kernel, out_shape=[jax.ShapeDtypeStruct(t.shape, f32)]...  3.58 us
  transfers between devices with their start and end apart: 6, of which 4 were waited for; matrix products, arithmetic and copies ran while one was open for 0% of the time, Pallas kernels for 7%

profile of v6, /device:TPU:71, one launch (start us, length us, event | category | flops | bytes accessed | tf_op | source)
XLA Modules:
  0.0 46.0 jit_solution(15728205955315531701)
XLA Ops:
  0.6 2.9 %shard_map.93 = (f32[5,96,128]{2,1,0:T(8,128)S(1)}, f32[40,128]{1,0:T(8,128)S(1)}, f32[40,128]{1,0:T(8,128)S(1)}, f32[40,128]{1,0:T(8,128)S(1)}, f32[4,96,128]{2,1,0:T(8,128)S(1)}, /*index=5*/f32[5,64,128]{2,1,0:T(8,128)S(1)}) custom-call(f32[1,96,128]{2,1,0:T(8,128)} %refs_0_.3, f32[1,96,128]{2,1,0:T(8,128)} %refs_1_.3, f32[1,96,128]{2,1,0:T(8,128)} %refs_2_.3, ...), custom_call_target="tpu_custom_call" | custom-call | flops 10000000 | bytes 10000000 | tf_op jit(solution)/shard_map/pallas_call | solution.py:694
  3.6 0.8 %shard_map.94.refs_5_.sb_ref = f32[48,128]{1,0:T(8,128)S(1)} custom-call(f32[1,96,128]{2,1,0:T(8,128)} %refs_0_.3, f32[1,96,128]{2,1,0:T(8,128)} %refs_1_.3, f32[1,96,128]{2,1,0:T(8,128)} %refs_2_.3, f32[1,96,128]{2,1,0:T(8,128)} %refs_3_.3, s32[1,96,128]{2,1,0:T(8,128)} %refs_4_.3, s32[1,128]{1,0:T(1,128)} %bitcast.1, ...), custom_call_target="tpu_custom_call" | custom-call | tf_op jit(solution)/shard_map/pallas_call | solution.py:694
  4.4 0.7 %collective-permute-start.1 = (f32[48,128]{1,0:T(8,128)S(1)}, f32[48,128]{1,0:T(8,128)S(1)}, u32[]{:S(2)}, u32[]{:S(2)}) collective-permute-start(f32[48,128]{1,0:T(8,128)S(1)} %shard_map.94.refs_5_.sb_ref), channel_id=1, source_target_pairs={{1,2},{2,1},{3,4},{4,3},{5,6},{6,5},{7,8},{8,7},{9,10},{10,9},{11,... | collective-permute-start | bytes 73736 | tf_op jit(solution)/shard_map/ppermute | solution.py:721
  5.1 0.1 shard_map.95
  5.2 3.8 %collective-permute-start = (f32[40,128]{1,0:T(8,128)S(1)}, f32[40,128]{1,0:T(8,128)S(1)}, u32[]{:S(2)}, u32[]{:S(2)}) collective-permute-start(f32[40,128]{1,0:T(8,128)S(1)} %get-tuple-element.35), channel_id=1, source_target_pairs={{0,1},{1,0},{2,3},{3,2},{4,5},{5,4},{6,7},{7,6},{8,9},{9,8},{10,11... | collective-permute-start | bytes 61448 | tf_op jit(solution)/shard_map/ppermute | solution.py:721
  9.0 0.8 %collective-permute-done.ra_ref = f32[40,128]{1,0:T(8,128)S(1)} collective-permute-done((f32[40,128]{1,0:T(8,128)S(1)}, f32[40,128]{1,0:T(8,128)S(1)}, u32[]{:S(2)}, u32[]{:S(2)}) %collective-permute-start) | collective-permute-done | bytes 20512 | tf_op jit(solution)/shard_map/ppermute | solution.py:721
  9.9 0.0 collective-permute-done.1.rb_ref
  9.9 0.1 shard_map.96
  9.9 14.0 %collective-permute-start.2 = (f32[136,128]{1,0:T(8,128)S(1)}, f32[136,128]{1,0:T(8,128)S(1)}, u32[]{:S(2)}, u32[]{:S(2)}) collective-permute-start(f32[136,128]{1,0:T(8,128)S(1)} %get-tuple-element.38), channel_id=1, source_target_pairs={{0,496},{1,497},{2,498},{3,499},{4,500},{5,501},{6,502},{7,503},{8... | collective-permute-start | bytes 208904 | tf_op jit(solution)/shard_map/ppermute | solution.py:721
  24.0 1.9 %collective-permute-start.3 = (f32[136,128]{1,0:T(8,128)S(1)}, f32[136,128]{1,0:T(8,128)S(1)}, u32[]{:S(2)}, u32[]{:S(2)}) collective-permute-start(f32[136,128]{1,0:T(8,128)S(1)} %get-tuple-element.39), channel_id=1, source_target_pairs={{0,16},{1,17},{2,18},{3,19},{4,20},{5,21},{6,22},{7,23},{8,24},{9,... | collective-permute-start | bytes 208904 | tf_op jit(solution)/shard_map/ppermute | solution.py:721
  25.9 0.3 collective-permute-done.2.first_in
  26.2 3.3 %collective-permute-done.3.second_in = f32[136,128]{1,0:T(8,128)S(1)} collective-permute-done((f32[136,128]{1,0:T(8,128)S(1)}, f32[136,128]{1,0:T(8,128)S(1)}, u32[]{:S(2)}, u32[]{:S(2)}) %collective-permute-start.3) | collective-permute-done | bytes 69664 | tf_op jit(solution)/shard_map/ppermute | solution.py:721
  29.5 1.9 %collective-permute-start.4 = (f32[128,128]{1,0:T(8,128)S(1)}, f32[128,128]{1,0:T(8,128)S(1)}, u32[]{:S(2)}, u32[]{:S(2)}) collective-permute-start(f32[128,128]{1,0:T(8,128)S(1)} %get-tuple-element.46), channel_id=1, source_target_pairs={{15,63},{31,495},{47,95},{63,15},{79,127},{95,47},{111,159},{127,7... | collective-permute-start | bytes 196616 | tf_op jit(solution)/shard_map/ppermute | solution.py:721
  31.4 6.6 %collective-permute-start.5 = (f32[128,128]{1,0:T(8,128)S(1)}, f32[128,128]{1,0:T(8,128)S(1)}, u32[]{:S(2)}, u32[]{:S(2)}) collective-permute-start(f32[128,128]{1,0:T(8,128)S(1)} %get-tuple-element.47), channel_id=1, source_target_pairs={{15,479},{31,79},{47,511},{63,111},{79,31},{95,143},{111,63},{127,... | collective-permute-start | bytes 196616 | tf_op jit(solution)/shard_map/ppermute | solution.py:721
  38.0 3.1 %shard_map.97 = (f32[1,96,128]{2,1,0:T(8,128)}, f32[1,96,128]{2,1,0:T(8,128)}, f32[1,96,128]{2,1,0:T(8,128)}, f32[1,96,128]{2,1,0:T(8,128)}, f32[4,2,24,128]{3,2...) custom-call(f32[5,96,128]{2,1,0:T(8,128)S(1)} %get-tuple-element.32.fields, f32[5,64,128]{2,1,0:T(8,128)S(1)} %get-tuple-element.33.strip, ...), custom_call_target="tpu_custom_call" | custom-call | flops 10000000 | bytes 10000000 | tf_op jit(solution)/shard_map/pallas_call | solution.py:694
  41.2 0.0 collective-permute-done.4.first_far
  41.2 1.3 %collective-permute-done.5.second_far = f32[128,128]{1,0:T(8,128)S(1)} collective-permute-done((f32[128,128]{1,0:T(8,128)S(1)}, f32[128,128]{1,0:T(8,128)S(1)}, u32[]{:S(2)}, u32[]{:S(2)}) %collective-permute-start.5) | collective-permute-done | bytes 65568 | tf_op jit(solution)/shard_map/ppermute | solution.py:721
  42.5 3.6 %shard_map.99 = (f32[1,96,128]{2,1,0:T(8,128)}, f32[1,96,128]{2,1,0:T(8,128)}, f32[1,96,128]{2,1,0:T(8,128)}, f32[1,96,128]{2,1,0:T(8,128)}) custom-call(f32[1,96,128]{2,1,0:T(8,128)} %get-tuple-element.40.t_in, f32[1,96,128]{2,1,0:T(8,128)} %get-tuple-element.41.s_in, ...), custom_call_target="tpu_custom_call", output_to_operand_aliasing={{0}: (0, {}), {1}: (1, {}), {2}: (2, {}), {3}: (3, {})} | custom-call | tf_op jit(solution)/shard_map/pallas_call | solution.py:765
  (1 shorter events, 0.0 us)
Async XLA Ops:
  4.4 5.5 %collective-permute-start.1 = (f32[48,128]{1,0:T(8,128)S(1)}, f32[48,128]{1,0:T(8,128)S(1)}, u32[]{:S(2)}, u32[]{:S(2)}) collective-permute-start(f32[48,128]{1,0:T(8,128)S(1)} %shard_map.94.refs_5_.sb_ref), channel_id=1, source_target_pairs={{1,2},{2,1},{3,4},{4,3},{5,6},{6,5},{7,8},{8,7},{9,10},{10,9},{11,... | collective-permute-start | bytes 73736 | tf_op jit(solution)/shard_map/ppermute | solution.py:721
  5.2 4.7 %collective-permute-start = (f32[40,128]{1,0:T(8,128)S(1)}, f32[40,128]{1,0:T(8,128)S(1)}, u32[]{:S(2)}, u32[]{:S(2)}) collective-permute-start(f32[40,128]{1,0:T(8,128)S(1)} %get-tuple-element.35), channel_id=1, source_target_pairs={{0,1},{1,0},{2,3},{3,2},{4,5},{5,4},{6,7},{7,6},{8,9},{9,8},{10,11... | collective-permute-start | bytes 61448 | tf_op jit(solution)/shard_map/ppermute | solution.py:721
  9.9 16.2 %collective-permute-start.2 = (f32[136,128]{1,0:T(8,128)S(1)}, f32[136,128]{1,0:T(8,128)S(1)}, u32[]{:S(2)}, u32[]{:S(2)}) collective-permute-start(f32[136,128]{1,0:T(8,128)S(1)} %get-tuple-element.38), channel_id=1, source_target_pairs={{0,496},{1,497},{2,498},{3,499},{4,500},{5,501},{6,502},{7,503},{8... | collective-permute-start | bytes 208904 | tf_op jit(solution)/shard_map/ppermute | solution.py:721
  24.0 5.5 %collective-permute-start.3 = (f32[136,128]{1,0:T(8,128)S(1)}, f32[136,128]{1,0:T(8,128)S(1)}, u32[]{:S(2)}, u32[]{:S(2)}) collective-permute-start(f32[136,128]{1,0:T(8,128)S(1)} %get-tuple-element.39), channel_id=1, source_target_pairs={{0,16},{1,17},{2,18},{3,19},{4,20},{5,21},{6,22},{7,23},{8,24},{9,... | collective-permute-start | bytes 208904 | tf_op jit(solution)/shard_map/ppermute | solution.py:721
  29.5 11.7 %collective-permute-start.4 = (f32[128,128]{1,0:T(8,128)S(1)}, f32[128,128]{1,0:T(8,128)S(1)}, u32[]{:S(2)}, u32[]{:S(2)}) collective-permute-start(f32[128,128]{1,0:T(8,128)S(1)} %get-tuple-element.46), channel_id=1, source_target_pairs={{15,63},{31,495},{47,95},{63,15},{79,127},{95,47},{111,159},{127,7... | collective-permute-start | bytes 196616 | tf_op jit(solution)/shard_map/ppermute | solution.py:721
  31.4 11.0 %collective-permute-start.5 = (f32[128,128]{1,0:T(8,128)S(1)}, f32[128,128]{1,0:T(8,128)S(1)}, u32[]{:S(2)}, u32[]{:S(2)}) collective-permute-start(f32[128,128]{1,0:T(8,128)S(1)} %get-tuple-element.47), channel_id=1, source_target_pairs={{15,479},{31,79},{47,511},{63,111},{79,31},{95,143},{111,63},{127,... | collective-permute-start | bytes 196616 | tf_op jit(solution)/shard_map/ppermute | solution.py:721

commit v7 on v6

--- a/solution.py
+++ b/solution.py
@@ -471,16 +471,24 @@
             out[0, 8 * g : 8 * g + 8, :] = join_columns(centre, state[i, row : row + 8, :], late)
 
 
-def arc_east(blocks):
-    lane, last = lane_index(), len(blocks) - 1
-    e = [roll(x, -1) for x in blocks]
-    return [jnp.where(lane == LANES - 1, e[min(k + 1, last)], e[k]) for k in range(last + 1)]
-
-
-def arc_west(blocks):
+class Each:
+    def __init__(self, make):
+        self.make, self.made = make, {}
+
+    def __call__(self, k):
+        if k not in self.made:
+            self.made[k] = self.make(k)
+        return self.made[k]
+
+
+def beside(block, first, last):
     lane = lane_index()
-    w = [roll(x, 1) for x in blocks]
-    return [jnp.where(lane == 0, w[max(k - 1, 0)], w[k]) for k in range(len(blocks))]
+    e = Each(lambda k: roll(block(k), -1))
+    w = Each(lambda k: roll(block(k), 1))
+    return (
+        Each(lambda k: jnp.where(lane == LANES - 1, e(min(k + 1, last)), e(k))),
+        Each(lambda k: jnp.where(lane == 0, w(max(k - 1, first)), w(k))),
+    )
 
 
 def cap_kernel(
@@ -526,7 +534,7 @@
     cap_turn = turning_of(float(total_rows - HALO + 1) + row_in_tile(), total_rows)
 
     def fill_ghosts(ref, parities, low, high, sides):
-        for side in range(sides):
+        for side in sides:
             ghosts = {}
             for k in range(low, high):
                 index = cap_opp[side, k]
@@ -558,28 +566,32 @@
     def cap_weigh():
         for side in (0, 1):
             for start in (0, 1):
-                seas = [cap_stat[side, 0, k, start : start + 8, :] for k in range(ARC)]
-                east, west = arc_east(seas), arc_west(seas)
+                seas = Each(lambda k: cap_stat[side, 0, k, start : start + 8, :])
+                east, west = beside(seas, 0, ARC - 1)
                 for k in range(ARC):
                     north = cap_stat[side, 0, k, start + 1 : start + 9, :]
                     if start:
                         south = cap_stat[side, 0, k, start - 1 : start + 7, :]
-                        cap_stat[side, 1, k, 1:9, :] = (east[k] + west[k]) + (north + south)
+                        cap_stat[side, 1, k, 1:9, :] = (east(k) + west(k)) + (north + south)
                         cap_stat[side, 4, k, 1:9, :] = north + south
-                    cap_stat[side, 2, k, start : start + 8, :] = seas[k] * east[k]
-                    cap_stat[side, 3, k, start : start + 8, :] = seas[k] * north
+                    cap_stat[side, 2, k, start : start + 8, :] = seas(k) * east(k)
+                    cap_stat[side, 3, k, start : start + 8, :] = seas(k) * north
 
     def cap_first(side, low, high):
-        span = range(low - 1, high + 1)
-        fields = [[cap[side, i, k, 1:9, :] for k in span] for i in range(FIELDS)]
-        east, west = [arc_east(f) for f in fields], [arc_west(f) for f in fields]
-        for n, k in enumerate(span):
+        west_end, east_end = low - 1, high
+
+        def field(i):
+            centre = Each(lambda k: cap[side, i, k, 1:9, :])
+            return centre, *beside(centre, west_end, east_end)
+
+        fields = [field(i) for i in range(FIELDS)]
+        for k in range(west_end, east_end + 1):
             lap, partial, fluxes = first_pass(
-                [f[n] for f in fields],
+                [centre(k) for centre, _, _ in fields],
                 [cap[side, i, k, 2:10, :] for i in range(FIELDS)],
                 [cap[side, i, k, 0:8, :] for i in range(FIELDS)],
-                [f[n] for f in east],
-                [f[n] for f in west],
+                [east(k) for _, east, _ in fields],
+                [west(k) for _, _, west in fields],
                 [cap_stat[side, i, k, 1:9, :] for i in range(4)] + [cap_turn],
                 cap_stat[side, 3, k, 0:8, :],
             )
@@ -591,32 +603,34 @@
                     cap_part[side, i, k, 0:8, :] = partial[i]
 
     def cap_second(side, low, high):
-        span = range(low - 1, high + 1)
-        for i in range(FIELDS):
-            blocks = [cap_lap[side, i, k, 1:9, :] for k in span]
-            terms = [
-                face_terms(
+        def field(i):
+            lap = Each(lambda k: cap_lap[side, i, k, 1:9, :])
+            east, _ = beside(lap, low - 1, high)
+            terms = Each(
+                lambda k: face_terms(
                     i,
-                    blocks[n],
-                    east,
-                    cap_stat[side, 2, span[n], 1:9, :],
-                    cap_flux[side, i, span[n], 0:8, :] if i < 3 else None,
+                    lap(k),
+                    east(k),
+                    cap_stat[side, 2, k, 1:9, :],
+                    cap_flux[side, i, k, 0:8, :] if i < 3 else None,
                 )
-                for n, east in enumerate(arc_east(blocks))
-            ]
-            gains = arc_west([gain for _, gain in terms])
-            for n, k in enumerate(span):
-                if low <= k < high:
-                    cap[side, i, k, 1:9, :] = second_pass(
-                        cap_part[side, i, k, 0:8, :],
-                        terms[n][0],
-                        gains[n],
-                        blocks[n],
-                        cap_lap[side, i, k, 2:10, :],
-                        cap_lap[side, i, k, 0:8, :],
-                        cap_stat[side, 0, k, 1:9, :],
-                        cap_stat[side, 4, k, 1:9, :],
-                    )
+            )
+            _, gain = beside(lambda k: terms(k)[1], low - 1, high)
+            return lap, terms, gain
+
+        fields = [field(i) for i in range(FIELDS)]
+        for k in range(low, high):
+            for i, (lap, terms, gain) in enumerate(fields):
+                cap[side, i, k, 1:9, :] = second_pass(
+                    cap_part[side, i, k, 0:8, :],
+                    terms(k)[0],
+                    gain(k),
+                    lap(k),
+                    cap_lap[side, i, k, 2:10, :],
+                    cap_lap[side, i, k, 0:8, :],
+                    cap_stat[side, 0, k, 1:9, :],
+                    cap_stat[side, 4, k, 1:9, :],
+                )
 
     @pl.when(is_top())
     def _():
@@ -638,8 +652,8 @@
                 state[i, row : row + UPPER, :] = upper_state[i, which]
             for i in range(STATS):
                 stat[i, row : row + UPPER, :] = upper_stat[i, which]
-        fill_ghosts(cap_stat, (1.0,), 0, ARC, 2)
-        fill_ghosts(cap, PARITY, 0, ARC, 2)
+        fill_ghosts(cap_stat, (1.0,), 0, ARC, (0, 1))
+        fill_ghosts(cap, PARITY, 0, ARC, (0, 1))
         cap_weigh()
         for n in range(STEPS - 1):
             low, high = n + 1, ARC - 1 - n
@@ -651,7 +665,11 @@
                 return carry
 
             lax.fori_loop(first_side, 2, one, 0)
-            fill_ghosts(cap, PARITY, low, high, 2 - first_side)
+            if n == STEPS - 3:
+                fill_ghosts(cap, PARITY, REACH - 1, REACH + 2, (0,))
+                fill_ghosts(cap, PARITY, low, high, (1,))
+            else:
+                fill_ghosts(cap, PARITY, low, high, range(2 - first_side))
             for i in range(FIELDS):
                 ghosts = [cap[0, i, k, 8:10, :] for k in (REACH - 1, REACH, REACH + 1)]
                 row = 8 + UPPER - HALO
@@ -671,8 +689,7 @@
                     rows_out.at[i], out.at[0, pl.ds(height - HALO, HALO), :], sems.at[i]
                 )
             )
-        for copy in copies:
-            copy.start()
+            copies[-1].start()
         for copy in copies:
             copy.wait()
 

time: 46.4 us -> 46.3 us (level)
  no operation moved by 1% of the time
where the time goes in v7:
time: 46.3 us; the launch traced here: 46 us
  starting transfers between devices  29 us (63%)
  Pallas kernels  10.6 us (23%)
  waiting for transfers between devices  5.67 us (12%)
  between operations  0.72 us (2%)
    ppermute x6, starting transfers between devices, exchange(): return lax.ppermute(x, ('lon', 'lat'), pairs)  29 us
    pallas_call x6, Pallas kernels, call(): pl.pallas_call(kernel, out_shape=[jax.ShapeDtypeStruct(shape, f32) for sh...  7.08 us
    ppermute x6, waiting for transfers between devices, exchange(): return lax.ppermute(x, ('lon', 'lat'), pairs)  5.67 us
    pallas_call x1, Pallas kernels, body(): pl.pallas_call(cap_kernel, out_shape=[jax.ShapeDtypeStruct(t.shape, f32)]...  3.5 us
  transfers between devices with their start and end apart: 6, of which 4 were waited for; matrix products, arithmetic and copies ran while one was open for 0% of the time, Pallas kernels for 7%

profile of v7, /device:TPU:71, one launch (start us, length us, event | category | flops | bytes accessed | tf_op | source)
XLA Modules:
  0.0 46.0 jit_solution(7607338468691571002)
XLA Ops:
  0.6 2.9 %shard_map.93 = (f32[5,96,128]{2,1,0:T(8,128)S(1)}, f32[40,128]{1,0:T(8,128)S(1)}, f32[40,128]{1,0:T(8,128)S(1)}, f32[40,128]{1,0:T(8,128)S(1)}, f32[4,96,128]{2,1,0:T(8,128)S(1)}, /*index=5*/f32[5,64,128]{2,1,0:T(8,128)S(1)}) custom-call(f32[1,96,128]{2,1,0:T(8,128)} %refs_0_.3, f32[1,96,128]{2,1,0:T(8,128)} %refs_1_.3, f32[1,96,128]{2,1,0:T(8,128)} %refs_2_.3, ...), custom_call_target="tpu_custom_call" | custom-call | flops 10000000 | bytes 10000000 | tf_op jit(solution)/shard_map/pallas_call | solution.py:711
  3.6 0.8 %shard_map.94.refs_5_.sb_ref = f32[48,128]{1,0:T(8,128)S(1)} custom-call(f32[1,96,128]{2,1,0:T(8,128)} %refs_0_.3, f32[1,96,128]{2,1,0:T(8,128)} %refs_1_.3, f32[1,96,128]{2,1,0:T(8,128)} %refs_2_.3, f32[1,96,128]{2,1,0:T(8,128)} %refs_3_.3, s32[1,96,128]{2,1,0:T(8,128)} %refs_4_.3, s32[1,128]{1,0:T(1,128)} %bitcast.1, ...), custom_call_target="tpu_custom_call" | custom-call | tf_op jit(solution)/shard_map/pallas_call | solution.py:711
  4.4 0.7 %collective-permute-start.1 = (f32[48,128]{1,0:T(8,128)S(1)}, f32[48,128]{1,0:T(8,128)S(1)}, u32[]{:S(2)}, u32[]{:S(2)}) collective-permute-start(f32[48,128]{1,0:T(8,128)S(1)} %shard_map.94.refs_5_.sb_ref), channel_id=1, source_target_pairs={{1,2},{2,1},{3,4},{4,3},{5,6},{6,5},{7,8},{8,7},{9,10},{10,9},{11,... | collective-permute-start | bytes 73736 | tf_op jit(solution)/shard_map/ppermute | solution.py:738
  5.1 0.1 shard_map.95
  5.2 3.8 %collective-permute-start = (f32[40,128]{1,0:T(8,128)S(1)}, f32[40,128]{1,0:T(8,128)S(1)}, u32[]{:S(2)}, u32[]{:S(2)}) collective-permute-start(f32[40,128]{1,0:T(8,128)S(1)} %get-tuple-element.35), channel_id=1, source_target_pairs={{0,1},{1,0},{2,3},{3,2},{4,5},{5,4},{6,7},{7,6},{8,9},{9,8},{10,11... | collective-permute-start | bytes 61448 | tf_op jit(solution)/shard_map/ppermute | solution.py:738
  9.0 0.8 %collective-permute-done.ra_ref = f32[40,128]{1,0:T(8,128)S(1)} collective-permute-done((f32[40,128]{1,0:T(8,128)S(1)}, f32[40,128]{1,0:T(8,128)S(1)}, u32[]{:S(2)}, u32[]{:S(2)}) %collective-permute-start) | collective-permute-done | bytes 20512 | tf_op jit(solution)/shard_map/ppermute | solution.py:738
  9.9 0.0 collective-permute-done.1.rb_ref
  9.9 0.1 shard_map.96
  9.9 14.0 %collective-permute-start.2 = (f32[136,128]{1,0:T(8,128)S(1)}, f32[136,128]{1,0:T(8,128)S(1)}, u32[]{:S(2)}, u32[]{:S(2)}) collective-permute-start(f32[136,128]{1,0:T(8,128)S(1)} %get-tuple-element.38), channel_id=1, source_target_pairs={{0,496},{1,497},{2,498},{3,499},{4,500},{5,501},{6,502},{7,503},{8... | collective-permute-start | bytes 208904 | tf_op jit(solution)/shard_map/ppermute | solution.py:738
  24.0 1.9 %collective-permute-start.3 = (f32[136,128]{1,0:T(8,128)S(1)}, f32[136,128]{1,0:T(8,128)S(1)}, u32[]{:S(2)}, u32[]{:S(2)}) collective-permute-start(f32[136,128]{1,0:T(8,128)S(1)} %get-tuple-element.39), channel_id=1, source_target_pairs={{0,16},{1,17},{2,18},{3,19},{4,20},{5,21},{6,22},{7,23},{8,24},{9,... | collective-permute-start | bytes 208904 | tf_op jit(solution)/shard_map/ppermute | solution.py:738
  25.9 0.3 collective-permute-done.2.first_in
  26.2 3.3 %collective-permute-done.3.second_in = f32[136,128]{1,0:T(8,128)S(1)} collective-permute-done((f32[136,128]{1,0:T(8,128)S(1)}, f32[136,128]{1,0:T(8,128)S(1)}, u32[]{:S(2)}, u32[]{:S(2)}) %collective-permute-start.3) | collective-permute-done | bytes 69664 | tf_op jit(solution)/shard_map/ppermute | solution.py:738
  29.5 1.9 %collective-permute-start.4 = (f32[128,128]{1,0:T(8,128)S(1)}, f32[128,128]{1,0:T(8,128)S(1)}, u32[]{:S(2)}, u32[]{:S(2)}) collective-permute-start(f32[128,128]{1,0:T(8,128)S(1)} %get-tuple-element.46), channel_id=1, source_target_pairs={{15,63},{31,495},{47,95},{63,15},{79,127},{95,47},{111,159},{127,7... | collective-permute-start | bytes 196616 | tf_op jit(solution)/shard_map/ppermute | solution.py:738
  31.4 6.6 %collective-permute-start.5 = (f32[128,128]{1,0:T(8,128)S(1)}, f32[128,128]{1,0:T(8,128)S(1)}, u32[]{:S(2)}, u32[]{:S(2)}) collective-permute-start(f32[128,128]{1,0:T(8,128)S(1)} %get-tuple-element.47), channel_id=1, source_target_pairs={{15,479},{31,79},{47,511},{63,111},{79,31},{95,143},{111,63},{127,... | collective-permute-start | bytes 196616 | tf_op jit(solution)/shard_map/ppermute | solution.py:738
  38.0 3.1 %shard_map.97 = (f32[1,96,128]{2,1,0:T(8,128)}, f32[1,96,128]{2,1,0:T(8,128)}, f32[1,96,128]{2,1,0:T(8,128)}, f32[1,96,128]{2,1,0:T(8,128)}, f32[4,2,24,128]{3,2...) custom-call(f32[5,96,128]{2,1,0:T(8,128)S(1)} %get-tuple-element.32.fields, f32[5,64,128]{2,1,0:T(8,128)S(1)} %get-tuple-element.33.strip, ...), custom_call_target="tpu_custom_call" | custom-call | flops 10000000 | bytes 10000000 | tf_op jit(solution)/shard_map/pallas_call | solution.py:711
  41.2 0.0 collective-permute-done.4.first_far
  41.2 1.3 %collective-permute-done.5.second_far = f32[128,128]{1,0:T(8,128)S(1)} collective-permute-done((f32[128,128]{1,0:T(8,128)S(1)}, f32[128,128]{1,0:T(8,128)S(1)}, u32[]{:S(2)}, u32[]{:S(2)}) %collective-permute-start.5) | collective-permute-done | bytes 65568 | tf_op jit(solution)/shard_map/ppermute | solution.py:738
  42.5 3.5 %shard_map.99 = (f32[1,96,128]{2,1,0:T(8,128)}, f32[1,96,128]{2,1,0:T(8,128)}, f32[1,96,128]{2,1,0:T(8,128)}, f32[1,96,128]{2,1,0:T(8,128)}) custom-call(f32[1,96,128]{2,1,0:T(8,128)} %get-tuple-element.40.t_in, f32[1,96,128]{2,1,0:T(8,128)} %get-tuple-element.41.s_in, ...), custom_call_target="tpu_custom_call", output_to_operand_aliasing={{0}: (0, {}), {1}: (1, {}), {2}: (2, {}), {3}: (3, {})} | custom-call | tf_op jit(solution)/shard_map/pallas_call | solution.py:782
  (1 shorter events, 0.0 us)
Async XLA Ops:
  4.4 5.5 %collective-permute-start.1 = (f32[48,128]{1,0:T(8,128)S(1)}, f32[48,128]{1,0:T(8,128)S(1)}, u32[]{:S(2)}, u32[]{:S(2)}) collective-permute-start(f32[48,128]{1,0:T(8,128)S(1)} %shard_map.94.refs_5_.sb_ref), channel_id=1, source_target_pairs={{1,2},{2,1},{3,4},{4,3},{5,6},{6,5},{7,8},{8,7},{9,10},{10,9},{11,... | collective-permute-start | bytes 73736 | tf_op jit(solution)/shard_map/ppermute | solution.py:738
  5.2 4.7 %collective-permute-start = (f32[40,128]{1,0:T(8,128)S(1)}, f32[40,128]{1,0:T(8,128)S(1)}, u32[]{:S(2)}, u32[]{:S(2)}) collective-permute-start(f32[40,128]{1,0:T(8,128)S(1)} %get-tuple-element.35), channel_id=1, source_target_pairs={{0,1},{1,0},{2,3},{3,2},{4,5},{5,4},{6,7},{7,6},{8,9},{9,8},{10,11... | collective-permute-start | bytes 61448 | tf_op jit(solution)/shard_map/ppermute | solution.py:738
  9.9 16.2 %collective-permute-start.2 = (f32[136,128]{1,0:T(8,128)S(1)}, f32[136,128]{1,0:T(8,128)S(1)}, u32[]{:S(2)}, u32[]{:S(2)}) collective-permute-start(f32[136,128]{1,0:T(8,128)S(1)} %get-tuple-element.38), channel_id=1, source_target_pairs={{0,496},{1,497},{2,498},{3,499},{4,500},{5,501},{6,502},{7,503},{8... | collective-permute-start | bytes 208904 | tf_op jit(solution)/shard_map/ppermute | solution.py:738
  24.0 5.5 %collective-permute-start.3 = (f32[136,128]{1,0:T(8,128)S(1)}, f32[136,128]{1,0:T(8,128)S(1)}, u32[]{:S(2)}, u32[]{:S(2)}) collective-permute-start(f32[136,128]{1,0:T(8,128)S(1)} %get-tuple-element.39), channel_id=1, source_target_pairs={{0,16},{1,17},{2,18},{3,19},{4,20},{5,21},{6,22},{7,23},{8,24},{9,... | collective-permute-start | bytes 208904 | tf_op jit(solution)/shard_map/ppermute | solution.py:738
  29.5 11.7 %collective-permute-start.4 = (f32[128,128]{1,0:T(8,128)S(1)}, f32[128,128]{1,0:T(8,128)S(1)}, u32[]{:S(2)}, u32[]{:S(2)}) collective-permute-start(f32[128,128]{1,0:T(8,128)S(1)} %get-tuple-element.46), channel_id=1, source_target_pairs={{15,63},{31,495},{47,95},{63,15},{79,127},{95,47},{111,159},{127,7... | collective-permute-start | bytes 196616 | tf_op jit(solution)/shard_map/ppermute | solution.py:738
  31.4 11.0 %collective-permute-start.5 = (f32[128,128]{1,0:T(8,128)S(1)}, f32[128,128]{1,0:T(8,128)S(1)}, u32[]{:S(2)}, u32[]{:S(2)}) collective-permute-start(f32[128,128]{1,0:T(8,128)S(1)} %get-tuple-element.47), channel_id=1, source_target_pairs={{15,479},{31,79},{47,511},{63,111},{79,31},{95,143},{111,63},{127,... | collective-permute-start | bytes 196616 | tf_op jit(solution)/shard_map/ppermute | solution.py:738
